TPU v7x, 32 devices: a whole 2x2x4 slice. The times are simulated.
32 devices in a mesh: ctx: 8 (over z, x), ch: 4 (over y, core).
Axes of the slice: x: 2, y: 2, z: 4, core: 2. Of those that a mesh axis runs over, the one named last changes fastest.
Arguments:
- signal: bfloat16 [2048, 4096], P('ctx', 'ch'), may hold values from -6 to 6
- upstream: bfloat16 [2048, 8192], P('ctx', 'ch'), may hold values from -6 to 6
- out_weight: bfloat16 [4096, 8192], P(None, 'ch'), may hold values from -0.0625 to 0.0625
- residues: float32 [4096, 16], P('ch'), may hold values from -6 to 6
- decays: float32 [4096, 16], P('ch'), may hold values from 0.5 to 300
- skip_gain: float32 [4096], P('ch'), may hold values from 0.2 to 1
Outputs:
- grad_signal: bfloat16 [2048, 4096], P('ctx', 'ch')
- grad_residues: float32 [4096, 16], P('ch')
- grad_decays: float32 [4096, 16], P('ch')
- grad_skip: float32 [4096], P('ch')
All inputs are finite; a program needn't handle non-finite values.
Results may differ from a plain program's by a relative error of at most 0.019.
Values may be sent and summed in bfloat16 or wider, within the bound.
No kernel may reach another device: no remote copies, remote signals or barrier semaphores. Data moves between devices by JAX's collectives and lax.ppermute only.
A program may use at most 128 MiB of HBM per device.

v0:
```python
import math

import jax
import jax.numpy as jnp
from jax import lax
from jax.sharding import PartitionSpec as P

TWO_PI = 2.0 * math.pi
HIGH = lax.Precision.HIGHEST


def regroup(blocks):
    return lax.all_to_all(blocks, "ctx", split_axis=0, concat_axis=0, tiled=True)


def angles(numer, modulus):
    return (numer % modulus).astype(jnp.float32) * (TWO_PI / modulus)


def body(signal, upstream, out_weight, residues, decays, skip_gain):
    tokens, width = signal.shape
    groups = lax.axis_size("ctx")
    inner = tokens // groups
    length = tokens * groups
    padded = 2 * length
    modes = residues.shape[1]
    myself = lax.axis_index("ctx")
    summed = lax.psum_scatter(
        lax.dot_general(
            out_weight, upstream, (((1,), (1,)), ((), ())), preferred_element_type=jnp.float32
        ).astype(jnp.bfloat16),
        "ch",
        scatter_dimension=0,
        tiled=True,
    ).astype(jnp.float32)
    grad_conv = summed.T.astype(jnp.bfloat16).astype(jnp.float32)
    sig = signal.astype(jnp.float32)
    source = jnp.arange(groups, dtype=jnp.int32)
    pair = jnp.arange(2, dtype=jnp.int32)
    row_index = jnp.arange(inner, dtype=jnp.int32)
    spectral_index = jnp.arange(tokens, dtype=jnp.int32)
    first_freq = 2 * source[:, None] + pair[None, :]
    outer_angle = angles(first_freq[:, :, None] * source[None, None, :], 2 * groups)
    outer_cos = jnp.cos(outer_angle)
    outer_sin = jnp.sin(outer_angle)
    full_pos = source[:, None] * inner + row_index[None, :]
    inner_angle = angles(full_pos[:, :, None] * spectral_index[None, None, :], tokens)
    inner_cos = jnp.cos(inner_angle)
    inner_sin = jnp.sin(inner_angle)
    stacked = jnp.stack(
        [sig.reshape(groups, inner, width), grad_conv.reshape(groups, inner, width)], axis=1
    )
    columns = regroup(stacked)
    along_cos = jnp.einsum("jip,pzrc->jizrc", outer_cos, columns, precision=HIGH)
    along_sin = jnp.einsum("jip,pzrc->jizrc", outer_sin, columns, precision=HIGH)
    local_pos = myself * inner + row_index
    twist = angles(first_freq[:, :, None] * local_pos[None, None, :], padded)
    twist_cos = jnp.cos(twist)[:, :, None, :, None]
    twist_sin = jnp.sin(twist)[:, :, None, :, None]
    part_real = along_cos * twist_cos - along_sin * twist_sin
    part_imag = -along_sin * twist_cos - along_cos * twist_sin
    mixed = regroup(jnp.stack([part_real, part_imag], axis=3))
    mixed_real = mixed[:, :, :, 0]
    mixed_imag = mixed[:, :, :, 1]
    freq_real = jnp.einsum("gizrc,grq->izqc", mixed_real, inner_cos, precision=HIGH) + jnp.einsum(
        "gizrc,grq->izqc", mixed_imag, inner_sin, precision=HIGH
    )
    freq_imag = jnp.einsum("gizrc,grq->izqc", mixed_imag, inner_cos, precision=HIGH) - jnp.einsum(
        "gizrc,grq->izqc", mixed_real, inner_sin, precision=HIGH
    )
    sig_real = freq_real[:, 0]
    sig_imag = freq_imag[:, 0]
    conv_real = freq_real[:, 1]
    conv_imag = freq_imag[:, 1]
    cross_real = sig_real * conv_real + sig_imag * conv_imag
    cross_imag = sig_real * conv_imag - sig_imag * conv_real
    frequency = (2 * myself + pair)[:, None] + 2 * groups * spectral_index[None, :]
    theta = angles(frequency, padded)
    wave_cos = jnp.cos(theta)[:, :, None]
    wave_sin = jnp.sin(theta)[:, :, None]
    half_sq = 2.0 * jnp.square(jnp.sin(0.5 * theta))[:, :, None]
    parity = (1 - 2 * pair).astype(jnp.float32)[:, None, None]
    pole_all = jnp.exp(-decays / length)
    gap_all = -jnp.expm1(-decays / length)
    end_all = jnp.exp(-decays)
    spread = jnp.zeros((2, tokens, width), jnp.float32)
    start_sums = jnp.zeros((width, modes), jnp.float32)

    def mode_step(index, carry):
        filt_real, filt_imag, res_sums, dec_sums = carry
        pole = lax.dynamic_index_in_dim(pole_all, index, 1, keepdims=False)
        gap = lax.dynamic_index_in_dim(gap_all, index, 1, keepdims=False)
        pole_end = lax.dynamic_index_in_dim(end_all, index, 1, keepdims=False)
        weight = lax.dynamic_index_in_dim(residues, index, 1, keepdims=False)
        pole_real = pole * wave_cos
        pole_imag = -pole * wave_sin
        base_real = gap + pole * half_sq
        base_imag = -pole_imag
        numer = 1.0 - pole_end * parity
        denom = base_real * base_real + base_imag * base_imag
        gamma_real = numer * base_real / denom
        gamma_imag = -numer * base_imag / denom
        filt_real = filt_real + weight * gamma_real
        filt_imag = filt_imag + weight * gamma_imag
        top_real = pole_real * numer / length - pole_end * parity * base_real
        top_imag = pole_imag * numer / length - pole_end * parity * base_imag
        square_real = base_real * base_real - base_imag * base_imag
        square_imag = 2.0 * base_real * base_imag
        quartic = denom * denom
        deriv_real = (top_real * square_real + top_imag * square_imag) / quartic
        deriv_imag = (top_imag * square_real - top_real * square_imag) / quartic
        res_col = jnp.sum(cross_real * gamma_real + cross_imag * gamma_imag, axis=(0, 1))
        dec_col = jnp.sum(cross_real * deriv_real + cross_imag * deriv_imag, axis=(0, 1))
        res_sums = lax.dynamic_update_index_in_dim(res_sums, res_col, index, 1)
        dec_sums = lax.dynamic_update_index_in_dim(dec_sums, dec_col, index, 1)
        return (filt_real, filt_imag, res_sums, dec_sums)

    filt_real, filt_imag, res_sums, dec_sums = lax.fori_loop(
        0, modes, mode_step, (spread, spread, start_sums, start_sums)
    )
    scale = 1.0 / math.sqrt(length)
    filt_real = filt_real * scale
    filt_imag = filt_imag * scale
    back_real = filt_real * conv_real + filt_imag * conv_imag
    back_imag = filt_real * conv_imag - filt_imag * conv_real
    spec_real = back_real[:, None]
    spec_imag = back_imag[:, None]
    wide_real = jnp.einsum("izqc,grq->gizrc", spec_real, inner_cos, precision=HIGH) - jnp.einsum(
        "izqc,grq->gizrc", spec_imag, inner_sin, precision=HIGH
    )
    wide_imag = jnp.einsum("izqc,grq->gizrc", spec_imag, inner_cos, precision=HIGH) + jnp.einsum(
        "izqc,grq->gizrc", spec_real, inner_sin, precision=HIGH
    )
    back_angle = angles(full_pos[:, None, :] * (2 * myself + pair)[None, :, None], padded)
    back_cos = jnp.cos(back_angle)[:, :, None, :, None]
    back_sin = jnp.sin(back_angle)[:, :, None, :, None]
    rot_real = wide_real * back_cos - wide_imag * back_sin
    rot_imag = wide_real * back_sin + wide_imag * back_cos
    moved = regroup(jnp.stack([rot_real, rot_imag], axis=3))
    rebuilt = (
        jnp.einsum("jizrc,jip->pzrc", moved[:, :, :, 0], outer_cos, precision=HIGH)
        - jnp.einsum("jizrc,jip->pzrc", moved[:, :, :, 1], outer_sin, precision=HIGH)
    ) / padded
    placed = regroup(rebuilt)
    conv_back = placed[:, 0].reshape(tokens, width)
    grad_signal = (conv_back + skip_gain[None, :] * grad_conv).astype(jnp.bfloat16)
    res_part = res_sums / (length * padded)
    dec_part = -residues * dec_sums / (length * padded)
    skip_part = jnp.sum(grad_conv * sig, axis=0) * scale
    totals = lax.psum((res_part, dec_part, skip_part), "ctx")
    return (grad_signal, totals[0], totals[1], totals[2])


def solution(mesh):
    placed = (P("ctx", "ch"), P("ctx", "ch"), P(None, "ch"), P("ch", None), P("ch", None), P("ch"))
    return jax.shard_map(
        body,
        mesh=mesh,
        in_specs=placed,
        out_specs=(P("ctx", "ch"), P("ch", None), P("ch", None), P("ch")),
        check_vma=False,
    )
```

profile of v0, /device:TPU:0, one launch (start us, length us, event | category | flops | bytes accessed | tf_op | source)
XLA Modules:
  0.0 686.5 jit_solution(7103781879562371775)
XLA Ops:
  8.4 9.7 %convolution_convert_fusion = bf16[4096,256]{1,0:T(8,128)(2,1)} fusion(bf16[4096,2048]{1,0:T(8,128)(2,1)} %param.10, bf16[256,2048]{1,0:T(8,128)(2,1)S(1)} %copy-done), kind=kOutput, calls=%fused_computation.49 | convolution fusion | flops 4296015872 | bytes 19922944 | tf_op jit(solution)/shard_map/dot_general | solution.py:29
  19.6 32.8 %reduce-scatter.2.cloned.1.call-done = bf16[1024,256]{1,0:T(8,128)(2,1)} async-done(((bf16[4096,256]{1,0:T(8,128)(2,1)}), bf16[1024,256]{1,0:T(8,128)(2,1)}) %reduce-scatter.2.cloned.1.call-update) | async-done | bytes 524304 | tf_op jit(solution)/shard_map/reduce_scatter | solution.py:28
  57.8 5.8 all-to-all-start
  63.9 47.6 %all-to-all-done = f32[8,2,32,1024]{3,2,1,0:T(8,128)S(1)} async-done(((f32[8,2,32,1024]{3,2,1,0:T(8,128)}), f32[8,2,32,1024]{3,2,1,0:T(8,128)S(1)}, u32[]{:S(2)}, u32[]{:S(2)}) %all-to-all-start) | async-done | bytes 2097184 | tf_op jit(solution)/shard_map/all_to_all | solution.py:13
  111.5 4.3 fusion.54
  115.8 5.3 subtract_bitcast_fusion.1
  121.2 1.7 pad_maximum_fusion
  122.8 8.6 %copy.84 = f32[8,2,2,2,32,1024]{5,4,2,1,3,0:T(8,128)} copy(f32[8,2,2,2,32,1024]{5,0,4,2,1,3:T(8,128)S(1)} %pad_maximum_fusion) | data formatting | bytes 16777216 | tf_op jit(solution)/shard_map/stack | solution.py:62
  131.4 5.1 all-to-all-start.1
  136.9 181.8 %all-to-all-done.1 = f32[8,2,2,2,32,1024]{5,4,2,1,3,0:T(8,128)} async-done(((f32[8,2,2,2,32,1024]{5,4,2,1,3,0:T(8,128)}), f32[8,2,2,2,32,1024]{5,4,2,1,3,0:T(8,128)}, u32[]{:S(2)}, u32[]{:S(2)}) %all-to-all-start.1) | async-done | bytes 8388640 | tf_op jit(solution)/shard_map/all_to_all | solution.py:13
  318.8 9.3 %slice_bitcast_fusion.4 = (f32[8,2,2,32,1024]{4,3,2,1,0:T(8,128)}, f32[8,2,2,32,1024]{4,3,2,1,0:T(8,128)}, f32[8,2,2,1,32,1024]{5,4,2,1,3,0:T(8,128)S(1)}, f32[8,2,2,1,32,1024]{5,4,2,1,3,0:T(8,128)}) fusion(f32[8,2,2,2,32,1024]{5,4,2,1,3,0:T(8,128)} %all-to-all-done.1), kind=kLoop, calls=%fused_computation.225 | loop fusion | bytes 25165824 | tf_op jit(solution)/shard_map/squeeze | solution.py:64
  328.1 7.8 %fusion.30 = f32[256,2,2,1024,1]{3,0,4,1,2:T(8,128)S(1)} fusion(f32[8,2,2,32,1024]{4,3,2,1,0:T(8,128)} %get-tuple-element.454, s32[8,32]{1,0:T(8,128)S(1)} %iota_add_fusion), kind=kOutput, calls=%fused_computation.51 | convolution fusion | flops 3222142976 | bytes 8389632 | tf_op jit(solution)/shard_map/gizrc,grq->izqc/dot_general | solution.py:68
  335.9 5.1 fusion.34
  341.1 5.2 fusion.36
  346.3 5.6 fusion.37
  352.0 2.7 multiply_subtract_fusion.1
  354.7 115.9 %while.22 = (s32[]{:T(128)}, f32[2,256,1024]{2,1,0:T(8,128)}, f32[2,256,1024]{2,1,0:T(8,128)}, f32[1024,16]{0,1:T(8,128)S(1)}, f32[1024,16]{0,1:T(8,128)S(1)}, /...) while((s32[]{:T(128)}, f32[2,256,1024]{2,1,0:T(8,128)}, ...), condition=%wide.region_4.5_spmd.clone.clone.clone, body=%wide.region_1.4_spmd.clone.clone.clone.sunk | while | flops 24131080 | bytes 12731583 | solution.py:118
  355.0 6.1 fusion.181
  361.6 6.8 fusion.181
  368.9 6.8 fusion.181
  376.2 6.8 fusion.181
  383.5 6.8 fusion.181
  390.8 6.8 fusion.181
  398.0 6.8 fusion.181
  405.3 6.8 fusion.181
  412.6 6.8 fusion.181
  419.9 6.8 fusion.181
  427.2 6.8 fusion.181
  434.5 6.8 fusion.181
  441.7 6.8 fusion.181
  449.0 6.8 fusion.181
  456.3 6.8 fusion.181
  463.6 6.8 fusion.181
  470.6 4.5 multiply_add_fusion.1
  475.0 2.9 fusion.48
  478.0 2.9 fusion.46
  480.9 3.0 fusion.60
  483.9 3.6 fusion.43
  488.7 96.7 %all_to_all.20 = f32[8,2,1,2,32,1024]{5,4,1,3,2,0:T(8,128)S(1)} all-to-all(f32[8,2,1,2,32,1024]{5,4,1,3,2,0:T(8,128)S(1)} %copy.92), channel_id=1, replica_groups=mesh['ctx'=8,'ch'=4] {'ctx'}, dimensions={0} | all-to-all | bytes 8388608 | tf_op jit(solution)/shard_map/all_to_all | solution.py:13
  586.0 2.3 fusion.66
  588.3 2.3 fusion.70
  590.7 1.6 copy.95
  592.3 3.8 all-to-all-start.3
  596.8 26.5 %all-to-all-done.3 = f32[8,1,32,1024]{3,2,1,0:T(8,128)S(1)} async-done(((f32[8,1,32,1024]{3,2,1,0:T(8,128)}), f32[8,1,32,1024]{3,2,1,0:T(8,128)S(1)}, u32[]{:S(2)}, u32[]{:S(2)}) %all-to-all-start.3) | async-done | bytes 1048608 | tf_op jit(solution)/shard_map/all_to_all | solution.py:13
  624.6 1.7 multiply_reduce_fusion
  627.4 19.8 %psum.23 = f32[1024]{0:T(1024)} all-reduce(f32[1024]{0:T(1024)S(1)} %broadcast_multiply_fusion.2), channel_id=1, replica_groups=mesh['ctx'=8,'ch'=4] {'ctx'}, use_global_device_ids=true, to_apply=%region_8.9 | all-reduce | flops 1024 | bytes 8192 | tf_op jit(solution)/shard_map/psum | solution.py:150
  647.1 29.4 %all-reduce.3.cloned.1.call-done = (f32[1024,16]{0,1:T(8,128)}, f32[1024,16]{0,1:T(8,128)}) async-done(((f32[1024,16]{0,1:T(8,128)}, f32[1024,16]{0,1:T(8,128)}), (f32[1024,16]{0,1:T(8,128)}, f32[1024,16]{0,1:T(8,128)})) %all-reduce.3.cloned.1.call-update) | async-done | bytes 131088 | tf_op jit(solution)/shard_map/psum | solution.py:150
  676.5 1.5 copy.180
  (190 shorter events, 22.2 us)
Async XLA Ops:
  7.2 1.2 copy-start
  7.2 45.2 %reduce-scatter.2.cloned.1.call-start = ((), (), s32[]{:S(2)}) async-start(), calls=%async_computation.5 | async-start | bytes 2621440 | tf_op jit(solution)/shard_map/reduce_scatter | solution.py:28
  18.1 1.0 copy-start.9
  19.3 35.5 %copy-start.4 = (bf16[256,1024]{0,1:T(8,128)(2,1)}, bf16[256,1024]{0,1:T(8,128)(2,1)S(1)}, u32[]{:S(2)}) copy-start(bf16[256,1024]{0,1:T(8,128)(2,1)S(1)} %copy.74) | copy-start | bytes 1572868
  57.8 53.8 %all-to-all-start = ((f32[8,2,32,1024]{3,2,1,0:T(8,128)}), f32[8,2,32,1024]{3,2,1,0:T(8,128)S(1)}, u32[]{:S(2)}, u32[]{:S(2)}) async-start(f32[8,2,32,1024]{3,2,1,0:T(8,128)} %copy.77), calls=%async_computation.1 | async-start | bytes 4194304 | tf_op jit(solution)/shard_map/all_to_all | solution.py:13
  131.4 5.4 copy-start.11
  131.4 187.3 %all-to-all-start.1 = ((f32[8,2,2,2,32,1024]{5,4,2,1,3,0:T(8,128)}), f32[8,2,2,2,32,1024]{5,4,2,1,3,0:T(8,128)}, u32[]{:S(2)}, u32[]{:S(2)}) async-start(f32[8,2,2,2,32,1024]{5,4,2,1,3,0:T(8,128)} %copy.84), calls=%async_computation.2 | async-start | bytes 16777216 | tf_op jit(solution)/shard_map/all_to_all | solution.py:13
  328.1 7.8 %copy-start.7 = (f32[8,2,2,1,32,1024]{5,4,2,1,3,0:T(8,128)S(1)}, f32[8,2,2,1,32,1024]{5,4,2,1,3,0:T(8,128)}, u32[]{:S(2)}) copy-start(f32[8,2,2,1,32,1024]{5,4,2,1,3,0:T(8,128)} %get-tuple-element.456) | copy-start | bytes 12582916
  335.9 5.1 copy-start.6
  346.3 5.7 copy-start.2
  351.9 2.7 copy-start.3
  351.9 2.7 copy-start.10
  592.3 32.3 %copy-start.5 = (bf16[256,1024]{0,1:T(8,128)(2,1)S(1)}, bf16[256,1024]{0,1:T(8,128)(2,1)}, u32[]{:S(2)}) copy-start(bf16[256,1024]{0,1:T(8,128)(2,1)} %copy-done.4) | copy-start | bytes 1572868
  592.3 32.3 %copy-start.8 = (bf16[1024,256]{1,0:T(8,128)(2,1)S(1)}, bf16[1024,256]{1,0:T(8,128)(2,1)}, u32[]{:S(2)}) copy-start(bf16[1024,256]{1,0:T(8,128)(2,1)} %reduce-scatter.2.cloned.1.call-done) | copy-start | bytes 1572868
  592.3 32.3 %copy-start.12 = (f32[1024]{0:T(1024)S(1)}, f32[1024]{0:T(1024)}, u32[]{:S(2)}) copy-start(f32[1024]{0:T(1024)} %param.13) | copy-start | bytes 12292
  592.3 31.0 %all-to-all-start.3 = ((f32[8,1,32,1024]{3,2,1,0:T(8,128)}), f32[8,1,32,1024]{3,2,1,0:T(8,128)S(1)}, u32[]{:S(2)}, u32[]{:S(2)}) async-start(f32[8,1,32,1024]{3,2,1,0:T(8,128)} %copy.95), calls=%async_computation.4 | async-start | bytes 2097152 | tf_op jit(solution)/shard_map/all_to_all | solution.py:13
  596.1 80.5 %all-reduce.3.cloned.1.call-start = ((), (), s32[]{:S(2)}) async-start(), calls=%async_computation.6 | async-start | bytes 262144 | tf_op jit(solution)/shard_map/psum | solution.py:150
  623.3 56.2 %copy-start.1 = (bf16[256,2048]{1,0:T(8,128)(2,1)S(1)}, bf16[256,2048]{1,0:T(8,128)(2,1)}, u32[]{:S(2)}) copy-start(bf16[256,2048]{1,0:T(8,128)(2,1)} %param.9) | copy-start | bytes 3145732
Sparse Core Ops, SparseCore 0:
  18.2 34.1 reduce-scatter.1
  601.3 75.1 all-reduce.2
where the time goes:
time: 691 us; the launch traced here: 687 us
  waiting for transfers between devices  318 us (46%)
  other arithmetic  126 us (18%)
  blocking collectives  116 us (17%)
  matrix products  60.2 us (9%)
  local copies, waits for them, and re-layouts  35.1 us (5%)
  starting transfers between devices  14.7 us (2%)
  between operations  14.6 us (2%)
    all_to_all x3, waiting for transfers between devices, regroup(): lax.all_to_all(blocks, 'ctx', split_axis=0, concat_axis=0, tiled=True)  256 us
    reduce_sum x16, other arithmetic, mode_step(): jnp.sum(cross_real * deriv_real + cross_imag * deriv_imag, axis=(0, 1))  108 us
    all_to_all x1, blocking collectives, regroup(): lax.all_to_all(blocks, 'ctx', split_axis=0, concat_axis=0, tiled=True)  96.7 us
    reduce_scatter x1, waiting for transfers between devices, body(): lax.psum_scatter(lax.dot_general(out_weight, upstream, (((1,), (1,)), (()...  32.8 us
    psum x1, waiting for transfers between devices, body(): totals = lax.psum((res_part, dec_part, skip_part), 'ctx')  29.4 us
    psum x1, blocking collectives, body(): totals = lax.psum((res_part, dec_part, skip_part), 'ctx')  19.8 us
    all_to_all x3, starting transfers between devices, regroup(): lax.all_to_all(blocks, 'ctx', split_axis=0, concat_axis=0, tiled=True)  14.7 us
  transfers between devices with their start and end apart: 5, of which 5 were waited for; matrix products, arithmetic and copies ran while one was open for 1% of the time, Pallas kernels for 0%

commit v1 on v0

v1 whole, which is shorter than its diff:
```python
import functools
import math

import jax
import jax.numpy as jnp
from jax import lax
from jax.experimental import pallas as pl
from jax.experimental.pallas import tpu as pltpu
from jax.sharding import PartitionSpec as P

F32 = jnp.float32
BF16 = jnp.bfloat16
SUB = 8
LANES = 128
VMEM_LIMIT = 48 * 1024 * 1024


def interleave(tokens, transpose=False):
    steps = tokens // SUB
    row = lax.broadcasted_iota(jnp.int32, (tokens, tokens), 1 if transpose else 0)
    col = lax.broadcasted_iota(jnp.int32, (tokens, tokens), 0 if transpose else 1)
    return jnp.where(col == (row % SUB) * steps + row // SUB, 1.0, 0.0).astype(BF16)


def params():
    return pltpu.CompilerParams(vmem_limit_bytes=VMEM_LIMIT)


def whole(ref):
    return pl.BlockSpec(memory_space=pltpu.VMEM)


def order_kernel(up_ref, o_ref):
    o_ref[...] = jnp.dot(
        interleave(up_ref.shape[0]), up_ref[...], preferred_element_type=F32
    ).astype(BF16)


def reorder(x):
    return pl.pallas_call(
        order_kernel,
        out_shape=jax.ShapeDtypeStruct(x.shape, BF16),
        in_specs=[whole(x)],
        out_specs=whole(x),
        compiler_params=params(),
        name="reorder",
    )(x)


def project_kernel(added, blk_ref, up_ref, w_ref, *refs):
    o_ref = refs[-1]
    part = lax.dot_general(
        up_ref[...], w_ref[...], (((1,), (1,)), ((), ())), preferred_element_type=F32
    )
    if added:
        part = part + refs[0][...].astype(F32)
    o_ref[...] = part.astype(o_ref.dtype)


def project(up, weight, block, width, extra, dtype):
    tokens, feats = up.shape
    rows = min(256, width)
    per = width // rows
    in_specs = [
        pl.BlockSpec((tokens, feats), lambda s, b: (0, 0)),
        pl.BlockSpec((rows, feats), lambda s, b: (b[0] * per + s, 0)),
    ]
    args = [up, weight]
    if extra is not None:
        in_specs.append(pl.BlockSpec((tokens, rows), lambda s, b: (0, s)))
        args.append(extra)
    return pl.pallas_call(
        functools.partial(project_kernel, extra is not None),
        out_shape=jax.ShapeDtypeStruct((tokens, width), dtype),
        grid_spec=pltpu.PrefetchScalarGridSpec(
            num_scalar_prefetch=1,
            grid=(per,),
            in_specs=in_specs,
            out_specs=pl.BlockSpec((tokens, rows), lambda s, b: (0, s)),
        ),
        compiler_params=params(),
        cost_estimate=pl.CostEstimate(
            flops=2 * tokens * feats * width,
            bytes_accessed=2 * feats * (width + tokens),
            transcendentals=0,
        ),
        name="project",
    )(jnp.reshape(block, (1,)).astype(jnp.int32), *args)


def bcast(row):
    return jnp.broadcast_to(row, (SUB, row.shape[-1]))


def signal_kernel(length, sig_ref, dec_ref, sigp_ref, y_ref, y1_ref, end_ref, sp, ebuf, e1buf):
    tokens, width = sig_ref.shape
    modes = dec_ref.shape[0]
    steps = tokens // SUB
    ordered = jnp.dot(interleave(tokens), sig_ref[...], preferred_element_type=F32)
    sigp_ref[...] = ordered.astype(BF16)
    sp[...] = ordered
    half = modes // 2

    @pl.loop(0, width // LANES)
    def _(block):
        lanes = pl.ds(pl.multiple_of(block * LANES, LANES), LANES)
        rate = dec_ref[:, lanes] * (1.0 / length)
        pole = jnp.exp(-rate)
        pole_sub = jnp.exp(-rate * steps)
        for first in (0, half):
            poles = [bcast(pole[n : n + 1]) for n in range(first, first + half)]

            def step(i, state):
                ends, firsts = state
                value = sp[pl.ds(pl.multiple_of(i * SUB, SUB), SUB), lanes]
                ends = [p * (e + value) for p, e in zip(poles, ends)]
                firsts = [p * f + e for p, f, e in zip(poles, firsts, ends)]
                return ends, firsts

            zeros = [jnp.zeros((SUB, LANES), F32)] * half
            ends, firsts = lax.fori_loop(0, steps, step, (zeros, zeros), unroll=4)
            for n in range(half):
                ebuf[pl.ds((first + n) * SUB, SUB), :] = ends[n]
                e1buf[pl.ds((first + n) * SUB, SUB), :] = firsts[n]
        carry = jnp.zeros((modes, LANES), F32)
        carry1 = jnp.zeros((modes, LANES), F32)
        for j in range(SUB):
            y_ref[j, :, lanes] = carry
            y1_ref[j, :, lanes] = carry1
            carry1 = pole_sub * (carry1 + steps * carry) + e1buf[pl.ds(j, modes, stride=SUB), :]
            carry = pole_sub * carry + ebuf[pl.ds(j, modes, stride=SUB), :]
        end_ref[0:modes, lanes] = carry
        end_ref[modes : 2 * modes, lanes] = carry1


def signal_states(signal, decays, length):
    tokens, width = signal.shape
    modes = decays.shape[0]
    return pl.pallas_call(
        functools.partial(signal_kernel, length),
        out_shape=(
            jax.ShapeDtypeStruct((tokens, width), BF16),
            jax.ShapeDtypeStruct((SUB, modes, width), F32),
            jax.ShapeDtypeStruct((SUB, modes, width), F32),
            jax.ShapeDtypeStruct((2 * modes, width), F32),
        ),
        in_specs=[whole(None)] * 2,
        out_specs=(whole(None),) * 4,
        scratch_shapes=[
            pltpu.VMEM((tokens, width), F32),
            pltpu.VMEM((modes * SUB, LANES), F32),
            pltpu.VMEM((modes * SUB, LANES), F32),
        ],
        compiler_params=params(),
        cost_estimate=pl.CostEstimate(
            flops=4 * modes * tokens * width, bytes_accessed=8 * tokens * width, transcendentals=0
        ),
        name="signal_states",
    )(signal, decays)


def gradient_kernel(
    length, own_ref, got_ref, sigp_ref, dec_ref, res_ref, y_ref, y1_ref, ydev_ref,
    loc_ref, grad_ref, carry_ref, pay_ref, gs, ss, zero, sbuf, s1buf, abuf, a1buf,
):
    tokens, width = sigp_ref.shape
    modes = dec_ref.shape[0]
    steps = tokens // SUB
    half = modes // 2
    zero[...] = jnp.zeros_like(zero)

    @pl.loop(0, width // LANES)
    def _(block):
        lanes = pl.ds(pl.multiple_of(block * LANES, LANES), LANES)
        total = own_ref[:, lanes]
        for q in range(got_ref.shape[0]):
            total = total + got_ref[q, :, lanes].astype(F32)
        total = total.astype(BF16)
        grad_ref[:, lanes] = total
        gs[...] = total.astype(F32)
        ss[...] = sigp_ref[:, lanes].astype(F32)
        pay_ref[3 * modes : 3 * modes + SUB, lanes] = bcast(
            jnp.sum(gs[...] * ss[...], axis=0, keepdims=True)
        )
        rate = dec_ref[:, lanes] * (1.0 / length)
        pole = jnp.exp(-rate)
        pole_sub = jnp.exp(-rate * steps)
        weight = res_ref[:, lanes]
        for first in (0, half):
            poles = [bcast(pole[n : n + 1]) for n in range(first, first + half)]
            weights = [bcast(weight[n : n + 1]) for n in range(first, first + half)]

            def step(t, state):
                hs, ks, res, dec = state
                rows = pl.ds(pl.multiple_of((steps - 1 - t) * SUB, SUB), SUB)
                value = gs[rows, :]
                seen = ss[rows, :]
                ks = [p * (k + h) for p, k, h in zip(poles, ks, hs)]
                hs = [p * h + value for p, h in zip(poles, hs)]
                res = [a + seen * h for a, h in zip(res, hs)]
                dec = [a + seen * k for a, k in zip(dec, ks)]
                terms = [r * h for r, h in zip(weights, hs)]
                while len(terms) > 1:
                    terms = [a + b for a, b in zip(terms[::2], terms[1::2])]
                if first == 0:
                    loc_ref[rows, lanes] = terms[0]
                else:
                    loc_ref[rows, lanes] = loc_ref[rows, lanes] + terms[0]
                return hs, ks, res, dec

            zeros = [zero[...]] * half
            hs, ks, res, dec = lax.fori_loop(0, steps, step, (zeros,) * 4, unroll=2)
            for n in range(half):
                rows = pl.ds((first + n) * SUB, SUB)
                sbuf[rows, :] = hs[n]
                s1buf[rows, :] = ks[n]
                abuf[rows, :] = res[n]
                a1buf[rows, :] = dec[n]
        carry = jnp.zeros((modes, LANES), F32)
        carry1 = jnp.zeros((modes, LANES), F32)
        res_sum = jnp.zeros((modes, LANES), F32)
        dec_sum = jnp.zeros((modes, LANES), F32)
        for j in reversed(range(SUB)):
            pick = pl.ds(j, modes, stride=SUB)
            start = sbuf[pick, :]
            start1 = s1buf[pick, :]
            before = y_ref[j, :, lanes]
            before1 = y1_ref[j, :, lanes]
            res_sum = res_sum + abuf[pick, :] + start * before
            dec_sum = dec_sum + a1buf[pick, :] + start1 * before + start * before1
            carry_ref[j, :, lanes] = carry
            carry1 = start1 + pole_sub * (carry1 + steps * carry)
            carry = start + pole_sub * carry
        before = ydev_ref[0:modes, lanes]
        before1 = ydev_ref[modes : 2 * modes, lanes]
        pay_ref[0:modes, lanes] = carry
        pay_ref[modes : 2 * modes, lanes] = res_sum + carry * before
        pay_ref[2 * modes : 3 * modes, lanes] = dec_sum + carry1 * before + carry * before1


def gradient_states(own, got, sigp, decays, residues, y, y1, ydev, length):
    tokens, width = sigp.shape
    modes = decays.shape[0]
    return pl.pallas_call(
        functools.partial(gradient_kernel, length),
        out_shape=(
            jax.ShapeDtypeStruct((tokens, width), F32),
            jax.ShapeDtypeStruct((tokens, width), BF16),
            jax.ShapeDtypeStruct((SUB, modes, width), F32),
            jax.ShapeDtypeStruct((3 * modes + SUB, width), F32),
        ),
        in_specs=[whole(None)] * 8,
        out_specs=(whole(None),) * 4,
        scratch_shapes=[
            pltpu.VMEM((tokens, LANES), F32),
            pltpu.VMEM((tokens, LANES), F32),
            pltpu.VMEM((SUB, LANES), F32),
            pltpu.VMEM((modes * SUB, LANES), F32),
            pltpu.VMEM((modes * SUB, LANES), F32),
            pltpu.VMEM((modes * SUB, LANES), F32),
            pltpu.VMEM((modes * SUB, LANES), F32),
        ],
        compiler_params=params(),
        cost_estimate=pl.CostEstimate(
            flops=10 * modes * tokens * width, bytes_accessed=16 * tokens * width, transcendentals=0
        ),
        name="gradient_states",
    )(own, got, sigp, decays, residues, y, y1, ydev)


def finish_kernel(
    length, loc_ref, grad_ref, carry_ref, later_ref, dec_ref, res_ref, gain_ref, sums_ref,
    o_ref, ores_ref, odec_ref, oskip_ref, vals, cbuf,
):
    tokens, width = loc_ref.shape
    modes = dec_ref.shape[0]
    steps = tokens // SUB
    scale = 1.0 / math.sqrt(length)

    @pl.loop(0, width // LANES)
    def _(block):
        lanes = pl.ds(pl.multiple_of(block * LANES, LANES), LANES)
        rate = dec_ref[:, lanes] * (1.0 / length)
        pole = jnp.exp(-rate)
        pole_sub = jnp.exp(-rate * steps)
        weight = res_ref[:, lanes]
        later = later_ref[:, lanes]
        for j in reversed(range(SUB)):
            cbuf[pl.ds(j, modes, stride=SUB), :] = weight * (carry_ref[j, :, lanes] + later)
            later = later * pole_sub
        poles = [bcast(pole[n : n + 1]) for n in range(modes)]
        start = [cbuf[pl.ds(n * SUB, SUB), :] for n in range(modes)]
        gain = bcast(gain_ref[:, lanes])

        def step(t, state):
            first = steps - 2 - 2 * t
            both = pl.ds(pl.multiple_of(first * SUB, 2 * SUB), 2 * SUB)
            outs = []
            for _ in range(2):
                state = [p * e for p, e in zip(poles, state)]
                terms = state
                while len(terms) > 1:
                    terms = [a + b for a, b in zip(terms[::2], terms[1::2])]
                outs.append(terms[0])
            more = jnp.concatenate(outs[::-1], axis=0)
            grad = grad_ref[both, lanes].astype(F32)
            skip = jnp.concatenate([gain, gain], axis=0) * grad
            vals[both, lanes] = ((loc_ref[both, lanes] + more) * scale + skip).astype(BF16)
            return state

        lax.fori_loop(0, steps // 2, step, start, unroll=2)

    o_ref[...] = jnp.dot(
        interleave(tokens, transpose=True), vals[...], preferred_element_type=F32
    ).astype(BF16)
    ores_ref[...] = (sums_ref[modes : 2 * modes, :] * (1.0 / length)).T
    odec_ref[...] = (
        sums_ref[2 * modes : 3 * modes, :] * (-1.0 / (length * length)) * res_ref[...]
    ).T
    oskip_ref[...] = sums_ref[3 * modes : 3 * modes + 1, :] * scale


def finish(loc, grad, carry, later, decays, residues, gain, sums, length):
    tokens, width = loc.shape
    modes = decays.shape[0]
    return pl.pallas_call(
        functools.partial(finish_kernel, length),
        out_shape=(
            jax.ShapeDtypeStruct((tokens, width), BF16),
            jax.ShapeDtypeStruct((width, modes), F32),
            jax.ShapeDtypeStruct((width, modes), F32),
            jax.ShapeDtypeStruct((1, width), F32),
        ),
        in_specs=[whole(None)] * 8,
        out_specs=(whole(None),) * 4,
        scratch_shapes=[
            pltpu.VMEM((tokens, width), BF16),
            pltpu.VMEM((modes * SUB, LANES), F32),
        ],
        compiler_params=params(),
        cost_estimate=pl.CostEstimate(
            flops=2 * modes * tokens * width, bytes_accessed=10 * tokens * width, transcendentals=0
        ),
        name="finish",
    )(loc, grad, carry, later, decays, residues, gain, sums)


def send(x, axis, size, hop):
    return lax.ppermute(x, axis, [(i, i ^ hop) for i in range(size)])


def prefix_over_ctx(ends, rate, length, tokens, groups, modes):
    me = lax.axis_index("ctx")
    state, first = ends[:modes], ends[modes:]
    before = jnp.zeros_like(state)
    before1 = jnp.zeros_like(state)
    hop = 1
    while hop < groups:
        there = send(jnp.concatenate([state, first]).astype(BF16), "ctx", groups, hop).astype(F32)
        other, other1 = there[:modes], there[modes:]
        inside = (me & (hop - 1)).astype(F32)
        upper = (me & hop) != 0
        reach = jnp.exp(-rate * (inside * tokens))
        before = before + jnp.where(upper, reach * other, 0.0)
        before1 = before1 + jnp.where(upper, reach * (other1 + (inside * tokens) * other), 0.0)
        span = jnp.exp(-rate * (hop * tokens))
        late = jnp.where(upper, state, other)
        late1 = jnp.where(upper, first, other1)
        early = jnp.where(upper, other, state)
        early1 = jnp.where(upper, other1, first)
        first = late1 + span * (early1 + (hop * tokens) * early)
        state = late + span * early
        hop *= 2
    return jnp.concatenate([before, before1])


def suffix_over_ctx(pay, rate, tokens, groups, modes):
    me = lax.axis_index("ctx")
    state, sums = pay[:modes], pay[modes:]
    later = jnp.zeros_like(state)
    hop = 1
    while hop < groups:
        there = send(jnp.concatenate([state, sums]).astype(BF16), "ctx", groups, hop).astype(F32)
        other, other_sums = there[:modes], there[modes:]
        inside = (me & (hop - 1)).astype(F32)
        lower = (me & hop) == 0
        reach = jnp.exp(-rate * ((hop - 1 - inside) * tokens))
        later = later + jnp.where(lower, reach * other, 0.0)
        span = jnp.exp(-rate * (hop * tokens))
        early = jnp.where(lower, state, other)
        late = jnp.where(lower, other, state)
        state = early + span * late
        sums = sums + other_sums
        hop *= 2
    return later, sums


def body(signal, upstream, out_weight, residues, decays, skip_gain):
    tokens, width = signal.shape
    groups = lax.axis_size("ctx")
    blocks = lax.axis_size("ch")
    length = tokens * groups
    modes = residues.shape[1]
    me = lax.axis_index("ch")
    dec = decays.T
    res = residues.T
    rate = dec * (1.0 / length)

    up = reorder(upstream)
    arrived = []
    for hop in range(2, blocks, 2):
        lent = project(up, out_weight, me ^ hop ^ 1, width, None, BF16)
        lent = send(lent, "ch", blocks, 1)
        pair = project(up, out_weight, me ^ hop, width, lent, BF16)
        arrived.append(send(pair, "ch", blocks, hop))
    lent = project(up, out_weight, me ^ 1, width, None, BF16)
    lent = send(lent, "ch", blocks, 1)
    own = project(up, out_weight, me, width, lent, F32)

    sigp, y, y1, ends = signal_states(signal, dec, length)
    ydev = prefix_over_ctx(ends, rate, length, tokens, groups, modes)
    loc, grad, carry, pay = gradient_states(
        own, jnp.stack(arrived), sigp, dec, res, y, y1, ydev, length
    )
    later, sums = suffix_over_ctx(pay, rate, tokens, groups, modes)
    out, ores, odec, oskip = finish(
        loc, grad, carry, later, dec, res, skip_gain[None, :],
        jnp.concatenate([jnp.zeros_like(later), sums]), length,
    )
    return (out, ores, odec, oskip[0])


def solution(mesh):
    placed = (P("ctx", "ch"), P("ctx", "ch"), P(None, "ch"), P("ch", None), P("ch", None), P("ch"))
    return jax.shard_map(
        body,
        mesh=mesh,
        in_specs=placed,
        out_specs=(P("ctx", "ch"), P("ch", None), P("ch", None), P("ch")),
        check_vma=False,
    )
```

time: 691 us -> 78.3 us (0.11)
  waiting for transfers between devices: 318 us -> 17.6 us
  other arithmetic: 126 us -> 2.85 us
  blocking collectives: 116 us -> 0 us
  matrix products: 60.2 us -> 0 us
  Pallas kernels: 0 us -> 33.9 us
  local copies, waits for them, and re-layouts: 35.1 us -> 8.43 us
  between operations: 14.6 us -> 0.9 us
    all_to_all x3 -> x0, waiting for transfers between devices: 256 us -> none  [regroup(): lax.all_to_all(blocks, 'ctx', split_axis=0, concat_axis=0, tiled=True)]
    reduce_sum x17 -> x0, other arithmetic: 109 us -> none  [the longest x16 108 us: mode_step(): jnp.sum(cross_real * deriv_real + cross_imag * deriv_imag, axis=(0, 1))]
    all_to_all x1 -> x0, blocking collectives: 96.7 us -> none  [regroup(): lax.all_to_all(blocks, 'ctx', split_axis=0, concat_axis=0, tiled=True)]
    dot_general x13 -> x0, matrix products: 60.2 us -> none  [the longest x1 9.69 us: body(): lax.dot_general(out_weight, upstream, (((1,), (1,)), ((), ())), preferred...]
    pallas_call x0 -> x8, Pallas kernels: none -> 33.9 us  [the longest x4 16.9 us: project(): pl.pallas_call(functools.partial(project_kernel, extra is not None), out_...]
    reduce_scatter x1 -> x0, waiting for transfers between devices: 32.8 us -> none  [body(): lax.psum_scatter(lax.dot_general(out_weight, upstream, (((1,), (1,)), (()...]
    psum x1 -> x0, waiting for transfers between devices: 29.4 us -> none  [body(): totals = lax.psum((res_part, dec_part, skip_part), 'ctx')]
    psum x1 -> x0, blocking collectives: 19.8 us -> none  [body(): totals = lax.psum((res_part, dec_part, skip_part), 'ctx')]
  transfers between devices with their start and end apart: 5 -> 9, of which waited for: 5 -> 5; matrix products, arithmetic and copies ran while one was open for 1% -> 3% of each run, Pallas kernels for 0% -> 22%
where the time goes in v1:
time: 78.3 us; the launch traced here: 77.6 us
  Pallas kernels  33.9 us (43%)
  waiting for transfers between devices  17.6 us (22%)
  starting transfers between devices  14 us (18%)
  local copies, waits for them, and re-layouts  8.43 us (11%)
  other arithmetic  2.85 us (4%)
  between operations  0.9 us (1%)
    ppermute x9, waiting for transfers between devices, send(): return lax.ppermute(x, axis, [(i, i ^ hop) for i in range(size)])  17.6 us
    pallas_call x4, Pallas kernels, project(): pl.pallas_call(functools.partial(project_kernel, extra is not None), out_...  16.9 us
    ppermute x9, starting transfers between devices, send(): return lax.ppermute(x, axis, [(i, i ^ hop) for i in range(size)])  14 us
    pallas_call x1, Pallas kernels, gradient_states(): pl.pallas_call(functools.partial(gradient_kernel, length), out_shape=(jax...  10.1 us
    unnamed x22, local copies, waits for them, and re-layouts  8.41 us
    pallas_call x1, Pallas kernels, signal_states(): pl.pallas_call(functools.partial(signal_kernel, length), out_shape=(jax.S...  3.37 us
    pallas_call x1, Pallas kernels, finish(): pl.pallas_call(functools.partial(finish_kernel, length), out_shape=(jax.S...  2.99 us
    another operation x6, other arithmetic  1.69 us
  transfers between devices with their start and end apart: 9, of which 5 were waited for; matrix products, arithmetic and copies ran while one was open for 3% of the time, Pallas kernels for 22%

profile of v1, /device:TPU:0, one launch (start us, length us, event | category | flops | bytes accessed | tf_op | source)
XLA Modules:
  0.0 77.6 jit_solution(12541764925349037398)
XLA Ops:
  0.6 0.0 copy-start
  0.6 0.8 %copy-done = f32[1024,16]{0,1:T(8,128)S(1)} copy-done((f32[1024,16]{0,1:T(8,128)S(1)}, f32[1024,16]{0,1:T(8,128)}, u32[]{:S(2)}) %copy-start) | copy-done | bytes 65560
  1.5 1.0 %copy-done.3 = bf16[256,1024]{1,0:T(8,128)(2,1)S(1)} copy-done((bf16[256,1024]{1,0:T(8,128)(2,1)S(1)}, bf16[256,1024]{1,0:T(8,128)(2,1)}, u32[]{:S(2)}) %copy-start.3) | copy-done | bytes 524312
  2.5 0.0 copy-start.1
  2.5 3.4 %signal_states.1 = (bf16[256,1024]{1,0:T(8,128)(2,1)S(1)}, f32[8,16,1024]{2,1,0:T(8,128)S(1)}, f32[8,16,1024]{2,1,0:T(8,128)S(1)}, f32[32,1024]{1,0:T(8,128)S(1)}) custom-call(bf16[256,1024]{1,0:T(8,128)(2,1)S(1)} %copy-done.3, f32[16,1024]{1,0:T(8,128)S(1)} %bitcast.24), custom_call_target="tpu_custom_call" | custom-call | flops 16777216 | bytes 2097152 | tf_op jit(solution)/shard_map/signal_states/pallas_call | solution.py:139
  5.9 0.0 copy-start.4
  5.9 0.8 %copy-done.4 = f32[8,16,1024]{2,1,0:T(8,128)} copy-done((f32[8,16,1024]{2,1,0:T(8,128)}, f32[8,16,1024]{2,1,0:T(8,128)S(1)}, u32[]{:S(2)}) %copy-start.4) | copy-done | bytes 524312
  6.7 0.8 %copy-done.6 = f32[8,16,1024]{2,1,0:T(8,128)} copy-done((f32[8,16,1024]{2,1,0:T(8,128)}, f32[8,16,1024]{2,1,0:T(8,128)S(1)}, u32[]{:S(2)}) %copy-start.6) | copy-done | bytes 524312
  7.5 3.0 %collective-permute-start.3 = (bf16[32,1024]{1,0:T(8,128)(2,1)S(1)}, bf16[32,1024]{1,0:T(8,128)(2,1)S(1)}, u32[]{:S(2)}, u32[]{:S(2)}) collective-permute-start(bf16[32,1024]{1,0:T(8,128)(2,1)S(1)} %convert_element_type.36), channel_id=1, source_target_pairs={{0,4},{4,0},{8,12},{12,8},{16,20},{20,16},{24,28},{28,24},{1,5},{5... | collective-permute-start | bytes 196616 | tf_op jit(solution)/shard_map/ppermute | solution.py:349
  10.5 1.2 %copy-done.2 = bf16[256,2048]{1,0:T(8,128)(2,1)S(1)} copy-done((bf16[256,2048]{1,0:T(8,128)(2,1)S(1)}, bf16[256,2048]{1,0:T(8,128)(2,1)}, u32[]{:S(2)}) %copy-start.2) | copy-done | bytes 1048600
  11.8 0.4 reorder.1.up_ref
  12.2 4.0 %project.6 = bf16[256,1024]{1,0:T(8,128)(2,1)S(1)} custom-call(s32[1]{0:T(128)} %bitcast.3.blk_ref, bf16[256,2048]{1,0:T(8,128)(2,1)S(1)} %reorder.1.up_ref, bf16[4096,2048]{1,0:T(8,128)(2,1)} %w_ref.7), custom_call_target="tpu_custom_call" | custom-call | flops 1073741824 | bytes 5242880 | tf_op jit(solution)/shard_map/project/pallas_call | solution.py:72
  16.2 0.1 collective-permute-start.1
  16.3 0.0 collective-permute-done.3
  16.3 0.0 copy-done.1
  16.4 0.7 fusion.8
  17.0 1.6 %collective-permute-start.4 = (bf16[32,1024]{1,0:T(8,128)(2,1)S(1)}, bf16[32,1024]{1,0:T(8,128)(2,1)}, u32[]{:S(2)}, u32[]{:S(2)}) collective-permute-start(bf16[32,1024]{1,0:T(8,128)(2,1)S(1)} %pad_maximum_fusion.3), channel_id=1, source_target_pairs={{0,8},{4,12},{8,0},{12,4},{16,24},{20,28},{24,16},{28,20},{1,9},{5... | collective-permute-start | bytes 196616 | tf_op jit(solution)/shard_map/ppermute | solution.py:349
  18.6 4.8 %project.4 = bf16[256,1024]{1,0:T(8,128)(2,1)} custom-call(s32[1]{0:T(128)} %bitcast.1.blk_ref, bf16[256,2048]{1,0:T(8,128)(2,1)S(1)} %reorder.1.up_ref, bf16[4096,2048]{1,0:T(8,128)(2,1)} %w_ref.7), custom_call_target="tpu_custom_call" | custom-call | flops 1073741824 | bytes 5242880 | tf_op jit(solution)/shard_map/project/pallas_call | solution.py:72
  23.4 0.2 collective-permute-start
  23.6 0.0 collective-permute-done.4
  23.6 0.8 %convert_element_type.39 = f32[32,1024]{1,0:T(8,128)S(1)} convert(bf16[32,1024]{1,0:T(8,128)(2,1)} %collective-permute-done.4) | non-fusion elementwise | flops 32768 | bytes 196608 | tf_op jit(solution)/shard_map/convert_element_type | solution.py:359
  24.4 0.9 %add_convert_fusion.2 = (bf16[16,1024]{1,0:T(8,128)(2,1)S(1)}, bf16[16,1024]{1,0:T(8,128)(2,1)S(1)}) fusion(f32[16,1024]{1,0:T(8,128)S(1)} %get-tuple-element.33, f32[32,1024]{1,0:T(8,128)S(1)} %convert_element_type.39, pred[]{:T(512)S(6)} %ne.10, f32[1024,16]{0,1:T(8,128)S(1)} %copy-done.1, f32[16,1024]{1,0:T(8,128)} %get-tuple-element.39), kind=kLoop, calls=%fused_computation.19 | loop fusion | flops 245760 | bytes 393217 | tf_op jit(solution)/shard_map/convert.4
  25.3 0.0 collective-permute-done.1.refs_0_
  25.3 0.0 copy-start.8
  25.4 4.1 %project.7 = bf16[256,1024]{1,0:T(8,128)(2,1)S(1)} custom-call(s32[1]{0:T(128)} %bitcast.2.blk_ref, bf16[256,2048]{1,0:T(8,128)(2,1)S(1)} %reorder.1.up_ref, bf16[4096,2048]{1,0:T(8,128)(2,1)} %w_ref.7, bf16[256,1024]{1,0:T(8,128)(2,1)S(1)} %collective-permute-done.1.refs_0_), custom_call_target="tpu_custom_call" | custom-call | flops 1073741824 | bytes 5242880 | tf_op jit(solution)/shard_map/project/pallas_call | solution.py:72
  29.5 0.0 copy-start.9
  29.5 1.6 %collective-permute-start.2 = (bf16[256,1024]{1,0:T(8,128)(2,1)S(1)}, bf16[256,1024]{1,0:T(8,128)(2,1)}, u32[]{:S(2)}, u32[]{:S(2)}) collective-permute-start(bf16[256,1024]{1,0:T(8,128)(2,1)S(1)} %project.7), channel_id=1, source_target_pairs={{0,2},{1,3},{2,0},{3,1},{4,6},{5,7},{6,4},{7,5},{8,10},{9,11},{10,... | collective-permute-start | bytes 1572872 | tf_op jit(solution)/shard_map/ppermute | solution.py:349
  31.1 2.6 %collective-permute-start.5 = (bf16[32,1024]{1,0:T(8,128)(2,1)S(1)}, bf16[32,1024]{1,0:T(8,128)(2,1)S(1)}, u32[]{:S(2)}, u32[]{:S(2)}) collective-permute-start(bf16[32,1024]{1,0:T(8,128)(2,1)S(1)} %pad_maximum_fusion.4), channel_id=1, source_target_pairs={{0,16},{4,20},{8,24},{12,28},{16,0},{20,4},{24,8},{28,12},{1,17},{... | collective-permute-start | bytes 196616 | tf_op jit(solution)/shard_map/ppermute | solution.py:349
  33.6 3.6 %collective-permute-done.5 = bf16[32,1024]{1,0:T(8,128)(2,1)S(1)} collective-permute-done((bf16[32,1024]{1,0:T(8,128)(2,1)S(1)}, bf16[32,1024]{1,0:T(8,128)(2,1)S(1)}, u32[]{:S(2)}, u32[]{:S(2)}) %collective-permute-start.5) | collective-permute-done | bytes 65568 | tf_op jit(solution)/shard_map/ppermute | solution.py:349
  37.3 0.1 select_add_fusion
  37.4 0.0 collective-permute-done.refs_0_
  37.4 4.1 %project.5.own_ref = f32[256,1024]{1,0:T(8,128)S(1)} custom-call(s32[1]{0:T(128)} %bitcast.blk_ref, bf16[256,2048]{1,0:T(8,128)(2,1)S(1)} %reorder.1.up_ref, bf16[4096,2048]{1,0:T(8,128)(2,1)} %w_ref.7, bf16[256,1024]{1,0:T(8,128)(2,1)S(1)} %collective-permute-done.refs_0_), custom_call_target="tpu_custom_call" | custom-call | flops 1073741824 | bytes 5242880 | tf_op jit(solution)/shard_map/project/pallas_call | solution.py:72
  41.5 2.3 %collective-permute-done.2 = bf16[256,1024]{1,0:T(8,128)(2,1)} collective-permute-done((bf16[256,1024]{1,0:T(8,128)(2,1)S(1)}, bf16[256,1024]{1,0:T(8,128)(2,1)}, u32[]{:S(2)}, u32[]{:S(2)}) %collective-permute-start.2) | collective-permute-done | bytes 524320 | tf_op jit(solution)/shard_map/ppermute | solution.py:349
  43.8 0.0 copy-done.8
  43.8 1.0 %copy-done.5 = f32[8,16,1024]{2,1,0:T(8,128)S(1)} copy-done((f32[8,16,1024]{2,1,0:T(8,128)S(1)}, f32[8,16,1024]{2,1,0:T(8,128)}, u32[]{:S(2)}) %copy-start.5) | copy-done | bytes 524312
  44.8 1.0 %copy-done.7 = f32[8,16,1024]{2,1,0:T(8,128)S(1)} copy-done((f32[8,16,1024]{2,1,0:T(8,128)S(1)}, f32[8,16,1024]{2,1,0:T(8,128)}, u32[]{:S(2)}) %copy-start.7) | copy-done | bytes 524312
  45.9 10.1 %gradient_states.1 = (f32[256,1024]{1,0:T(8,128)S(1)}, bf16[256,1024]{1,0:T(8,128)(2,1)S(1)}, f32[8,16,1024]{2,1,0:T(8,128)S(1)}, f32[56,1024]{1,0:T(8,128)S(1)}) custom-call(f32[256,1024]{1,0:T(8,128)S(1)} %project.5.own_ref, bf16[1,256,1024]{2,1,0:T(8,128)(2,1)} %bitcast.4.got_ref, bf16[256,1024]{1,0:T(8,128)(2,1)S(1)} %get-tuple-element.16.sigp_ref, ...), custom_call_target="tpu_custom_call" | custom-call | flops 41943040 | bytes 4194304 | tf_op jit(solution)/shard_map/gradient_states/pallas_call | solution.py:244
  56.0 0.6 collective-permute-start.6
  56.6 4.3 %collective-permute-done.6 = bf16[56,1024]{1,0:T(8,128)(2,1)S(1)} collective-permute-done((bf16[56,1024]{1,0:T(8,128)(2,1)S(1)}, bf16[56,1024]{1,0:T(8,128)(2,1)S(1)}, u32[]{:S(2)}, u32[]{:S(2)}) %collective-permute-start.6) | collective-permute-done | bytes 114720 | tf_op jit(solution)/shard_map/ppermute | solution.py:349
  61.0 0.5 collective-permute-start.7
  61.5 4.3 %collective-permute-done.7 = bf16[56,1024]{1,0:T(8,128)(2,1)S(1)} collective-permute-done((bf16[56,1024]{1,0:T(8,128)(2,1)S(1)}, bf16[56,1024]{1,0:T(8,128)(2,1)S(1)}, u32[]{:S(2)}, u32[]{:S(2)}) %collective-permute-start.7) | collective-permute-done | bytes 114720 | tf_op jit(solution)/shard_map/ppermute | solution.py:349
  66.0 3.9 %collective-permute-start.8 = (bf16[56,1024]{1,0:T(8,128)(2,1)S(1)}, bf16[56,1024]{1,0:T(8,128)(2,1)S(1)}, u32[]{:S(2)}, u32[]{:S(2)}) collective-permute-start(bf16[56,1024]{1,0:T(8,128)(2,1)S(1)} %pad_maximum_fusion.2), channel_id=1, source_target_pairs={{0,16},{4,20},{8,24},{12,28},{16,0},{20,4},{24,8},{28,12},{1,17},{... | collective-permute-start | bytes 344072 | tf_op jit(solution)/shard_map/ppermute | solution.py:349
  69.8 3.0 %collective-permute-done.8 = bf16[56,1024]{1,0:T(8,128)(2,1)S(1)} collective-permute-done((bf16[56,1024]{1,0:T(8,128)(2,1)S(1)}, bf16[56,1024]{1,0:T(8,128)(2,1)S(1)}, u32[]{:S(2)}, u32[]{:S(2)}) %collective-permute-start.8) | collective-permute-done | bytes 114720 | tf_op jit(solution)/shard_map/ppermute | solution.py:349
  72.9 0.1 fusion.1.later_ref
  73.0 0.0 copy-done.9
  73.0 3.0 %finish.1 = (bf16[256,1024]{1,0:T(8,128)(2,1)}, f32[1024,16]{1,0:T(8,128)S(1)}, f32[1024,16]{1,0:T(8,128)S(1)}, f32[1,1024]{1,0:T(1,128)}) custom-call(f32[256,1024]{1,0:T(8,128)S(1)} %get-tuple-element.20.loc_ref, bf16[256,1024]{1,0:T(8,128)(2,1)S(1)} %get-tuple-element.21.grad_ref, f32[8,16,1024]{2,1,0:T(8,128)S(1)} %get-tuple-element.22.carry_ref, ...), custom_call_target="tpu_custom_call" | custom-call | flops 8388608 | bytes 2621440 | tf_op jit(solution)/shard_map/finish/pallas_call | solution.py:326
  76.0 0.8 %copy.10 = f32[1024,16]{0,1:T(8,128)} copy(f32[1024,16]{1,0:T(8,128)S(1)} %get-tuple-element.29) | data formatting | bytes 131072
  76.8 0.8 %copy.11 = f32[1024,16]{0,1:T(8,128)} copy(f32[1024,16]{1,0:T(8,128)S(1)} %get-tuple-element.30) | data formatting | bytes 131072
  (23 shorter events, 0.3 us)
Async XLA Ops:
  0.6 0.8 %copy-start = (f32[1024,16]{0,1:T(8,128)S(1)}, f32[1024,16]{0,1:T(8,128)}, u32[]{:S(2)}) copy-start(f32[1024,16]{0,1:T(8,128)} %param.10) | copy-start | bytes 196612
  1.5 1.0 %copy-start.3 = (bf16[256,1024]{1,0:T(8,128)(2,1)S(1)}, bf16[256,1024]{1,0:T(8,128)(2,1)}, u32[]{:S(2)}) copy-start(bf16[256,1024]{1,0:T(8,128)(2,1)} %sig_ref.1) | copy-start | bytes 1572868
  2.5 13.8 %copy-start.1 = (f32[1024,16]{0,1:T(8,128)S(1)}, f32[1024,16]{0,1:T(8,128)}, u32[]{:S(2)}) copy-start(f32[1024,16]{0,1:T(8,128)} %param.10) | copy-start | bytes 196612
  5.9 0.8 %copy-start.4 = (f32[8,16,1024]{2,1,0:T(8,128)}, f32[8,16,1024]{2,1,0:T(8,128)S(1)}, u32[]{:S(2)}) copy-start(f32[8,16,1024]{2,1,0:T(8,128)S(1)} %get-tuple-element.17.y_ref) | copy-start | bytes 1572868
  6.7 0.8 %copy-start.6 = (f32[8,16,1024]{2,1,0:T(8,128)}, f32[8,16,1024]{2,1,0:T(8,128)S(1)}, u32[]{:S(2)}) copy-start(f32[8,16,1024]{2,1,0:T(8,128)S(1)} %get-tuple-element.18.y1_ref) | copy-start | bytes 1572868
  7.5 8.8 %collective-permute-start.3 = (bf16[32,1024]{1,0:T(8,128)(2,1)S(1)}, bf16[32,1024]{1,0:T(8,128)(2,1)S(1)}, u32[]{:S(2)}, u32[]{:S(2)}) collective-permute-start(bf16[32,1024]{1,0:T(8,128)(2,1)S(1)} %convert_element_type.36), channel_id=1, source_target_pairs={{0,4},{4,0},{8,12},{12,8},{16,20},{20,16},{24,28},{28,24},{1,5},{5... | collective-permute-start | bytes 196616 | tf_op jit(solution)/shard_map/ppermute | solution.py:349
  10.5 1.2 %copy-start.2 = (bf16[256,2048]{1,0:T(8,128)(2,1)S(1)}, bf16[256,2048]{1,0:T(8,128)(2,1)}, u32[]{:S(2)}) copy-start(bf16[256,2048]{1,0:T(8,128)(2,1)} %up_ref.1) | copy-start | bytes 3145732
  16.2 9.1 %collective-permute-start.1 = (bf16[256,1024]{1,0:T(8,128)(2,1)S(1)}, bf16[256,1024]{1,0:T(8,128)(2,1)S(1)}, u32[]{:S(2)}, u32[]{:S(2)}) collective-permute-start(bf16[256,1024]{1,0:T(8,128)(2,1)S(1)} %project.6), channel_id=1, source_target_pairs={{0,1},{1,0},{2,3},{3,2},{4,5},{5,4},{6,7},{7,6},{8,9},{9,8},{10,11... | collective-permute-start | bytes 1572872 | tf_op jit(solution)/shard_map/ppermute | solution.py:349
  17.0 6.6 %collective-permute-start.4 = (bf16[32,1024]{1,0:T(8,128)(2,1)S(1)}, bf16[32,1024]{1,0:T(8,128)(2,1)}, u32[]{:S(2)}, u32[]{:S(2)}) collective-permute-start(bf16[32,1024]{1,0:T(8,128)(2,1)S(1)} %pad_maximum_fusion.3), channel_id=1, source_target_pairs={{0,8},{4,12},{8,0},{12,4},{16,24},{20,28},{24,16},{28,20},{1,9},{5... | collective-permute-start | bytes 196616 | tf_op jit(solution)/shard_map/ppermute | solution.py:349
  23.4 14.0 %collective-permute-start = (bf16[256,1024]{1,0:T(8,128)(2,1)}, bf16[256,1024]{1,0:T(8,128)(2,1)S(1)}, u32[]{:S(2)}, u32[]{:S(2)}) collective-permute-start(bf16[256,1024]{1,0:T(8,128)(2,1)} %project.4), channel_id=1, source_target_pairs={{0,1},{1,0},{2,3},{3,2},{4,5},{5,4},{6,7},{7,6},{8,9},{9,8},{10,11... | collective-permute-start | bytes 1572872 | tf_op jit(solution)/shard_map/ppermute | solution.py:349
  25.3 18.4 %copy-start.8 = (f32[1024,16]{0,1:T(8,128)S(1)}, f32[1024,16]{0,1:T(8,128)}, u32[]{:S(2)}) copy-start(f32[1024,16]{0,1:T(8,128)} %param.9) | copy-start | bytes 196612
  29.5 43.5 %copy-start.9 = (f32[1024]{0:T(1024)S(1)}, f32[1024]{0:T(1024)}, u32[]{:S(2)}) copy-start(f32[1024]{0:T(1024)} %param.11) | copy-start | bytes 12292
  29.5 14.3 %collective-permute-start.2 = (bf16[256,1024]{1,0:T(8,128)(2,1)S(1)}, bf16[256,1024]{1,0:T(8,128)(2,1)}, u32[]{:S(2)}, u32[]{:S(2)}) collective-permute-start(bf16[256,1024]{1,0:T(8,128)(2,1)S(1)} %project.7), channel_id=1, source_target_pairs={{0,2},{1,3},{2,0},{3,1},{4,6},{5,7},{6,4},{7,5},{8,10},{9,11},{10,... | collective-permute-start | bytes 1572872 | tf_op jit(solution)/shard_map/ppermute | solution.py:349
  31.1 6.2 %collective-permute-start.5 = (bf16[32,1024]{1,0:T(8,128)(2,1)S(1)}, bf16[32,1024]{1,0:T(8,128)(2,1)S(1)}, u32[]{:S(2)}, u32[]{:S(2)}) collective-permute-start(bf16[32,1024]{1,0:T(8,128)(2,1)S(1)} %pad_maximum_fusion.4), channel_id=1, source_target_pairs={{0,16},{4,20},{8,24},{12,28},{16,0},{20,4},{24,8},{28,12},{1,17},{... | collective-permute-start | bytes 196616 | tf_op jit(solution)/shard_map/ppermute | solution.py:349
  43.8 1.0 %copy-start.5 = (f32[8,16,1024]{2,1,0:T(8,128)S(1)}, f32[8,16,1024]{2,1,0:T(8,128)}, u32[]{:S(2)}) copy-start(f32[8,16,1024]{2,1,0:T(8,128)} %copy-done.4) | copy-start | bytes 1572868
  44.8 1.0 %copy-start.7 = (f32[8,16,1024]{2,1,0:T(8,128)S(1)}, f32[8,16,1024]{2,1,0:T(8,128)}, u32[]{:S(2)}) copy-start(f32[8,16,1024]{2,1,0:T(8,128)} %copy-done.6) | copy-start | bytes 1572868
  56.0 4.9 %collective-permute-start.6 = (bf16[56,1024]{1,0:T(8,128)(2,1)S(1)}, bf16[56,1024]{1,0:T(8,128)(2,1)S(1)}, u32[]{:S(2)}, u32[]{:S(2)}) collective-permute-start(bf16[56,1024]{1,0:T(8,128)(2,1)S(1)} %convert_element_type.42), channel_id=1, source_target_pairs={{0,4},{4,0},{8,12},{12,8},{16,20},{20,16},{24,28},{28,24},{1,5},{5... | collective-permute-start | bytes 344072 | tf_op jit(solution)/shard_map/ppermute | solution.py:349
  61.0 4.9 %collective-permute-start.7 = (bf16[56,1024]{1,0:T(8,128)(2,1)S(1)}, bf16[56,1024]{1,0:T(8,128)(2,1)S(1)}, u32[]{:S(2)}, u32[]{:S(2)}) collective-permute-start(bf16[56,1024]{1,0:T(8,128)(2,1)S(1)} %pad_maximum_fusion.1), channel_id=1, source_target_pairs={{0,8},{4,12},{8,0},{12,4},{16,24},{20,28},{24,16},{28,20},{1,9},{5... | collective-permute-start | bytes 344072 | tf_op jit(solution)/shard_map/ppermute | solution.py:349
  66.0 6.9 %collective-permute-start.8 = (bf16[56,1024]{1,0:T(8,128)(2,1)S(1)}, bf16[56,1024]{1,0:T(8,128)(2,1)S(1)}, u32[]{:S(2)}, u32[]{:S(2)}) collective-permute-start(bf16[56,1024]{1,0:T(8,128)(2,1)S(1)} %pad_maximum_fusion.2), channel_id=1, source_target_pairs={{0,16},{4,20},{8,24},{12,28},{16,0},{20,4},{24,8},{28,12},{1,17},{... | collective-permute-start | bytes 344072 | tf_op jit(solution)/shard_map/ppermute | solution.py:349

commit v2 on v0

v2 whole, which is shorter than its diff:
```python
import functools
import math

import jax
import jax.numpy as jnp
from jax import lax
from jax.experimental import pallas as pl
from jax.experimental.pallas import tpu as pltpu
from jax.sharding import PartitionSpec as P

F32 = jnp.float32
BF16 = jnp.bfloat16
SUB = 16
HALF = 8
LANES = 128
VMEM_LIMIT = 12 * 1024 * 1024
PROJECT_LIMIT = 50 * 1024 * 1024
VM = pl.BlockSpec(memory_space=pltpu.VMEM)
SM = pl.BlockSpec(memory_space=pltpu.SMEM)


def interleave(tokens, transpose=False):
    steps = tokens // SUB
    row = lax.broadcasted_iota(jnp.int32, (tokens, tokens), 1 if transpose else 0)
    col = lax.broadcasted_iota(jnp.int32, (tokens, tokens), 0 if transpose else 1)
    return jnp.where(col == (row % SUB) * steps + row // SUB, 1.0, 0.0).astype(BF16)


def group_sums(groups, size):
    col = lax.broadcasted_iota(jnp.int32, (groups, groups * size), 1)
    row = lax.broadcasted_iota(jnp.int32, (groups, groups * size), 0)
    return jnp.where(col // size == row, 1.0, 0.0).astype(F32)


def params(limit=VMEM_LIMIT):
    return pltpu.CompilerParams(vmem_limit_bytes=limit)


SMALL = pl.CostEstimate(flops=1, bytes_accessed=1, transcendentals=0)


def spread(row):
    return jnp.broadcast_to(row, (HALF, row.shape[-1]))


def pairwise(terms):
    while len(terms) > 1:
        rest = terms[len(terms) // 2 * 2 :]
        terms = [a + b for a, b in zip(terms[::2], terms[1::2])] + rest
    return terms[0]


def lane_block(block):
    return pl.ds(pl.multiple_of(block * LANES, LANES), LANES)


def rows_of(i, half):
    return pl.ds(SUB * i + HALF * half, HALF)


def recur(poles, values):
    last = values[-1]
    sums = [last] * len(poles)
    firsts = None
    for value in values[-2::-1]:
        if firsts is None:
            moved = [p * s for p, s in zip(poles, sums)]
            firsts = moved
        else:
            firsts = [p * (f + s) for p, f, s in zip(poles, firsts, sums)]
            moved = [p * s for p, s in zip(poles, sums)]
        sums = [m + value for m in moved]
    return sums, firsts


def signal_chunk(length, low, high, sig_ref, dec_ref, end_ref, sigp_ref, y_ref, y1_ref, ebuf, e1buf):
    tokens, width = sig_ref.shape[0], high - low
    modes = dec_ref.shape[0]
    steps = tokens // SUB
    sigp_ref[...] = jnp.dot(
        interleave(tokens), sig_ref[:, low:high], preferred_element_type=F32
    ).astype(BF16)

    @pl.loop(0, width // LANES)
    def _(block):
        lanes = lane_block(block)
        there = lane_block(block + low // LANES)
        rate = dec_ref[:, there] * (1.0 / length)
        pole_all = jnp.exp(-rate)
        pole_sub = jnp.exp(-rate * steps)
        both = [sigp_ref[pl.ds(SUB * i, SUB), lanes].astype(F32) for i in range(steps)]
        for half in range(2):
            values = [both[i][HALF * half : HALF * (half + 1)] for i in reversed(range(steps))]
            for first in range(0, modes, 8):
                poles = [spread(pole_all[n : n + 1]) for n in range(first, first + 8)]
                sums, firsts = recur(poles, values)
                for n in range(8):
                    rows = rows_of(first + n, half)
                    end = poles[n] * sums[n]
                    ebuf[rows, :] = end
                    e1buf[rows, :] = poles[n] * firsts[n] + end
        carry = jnp.zeros((modes, LANES), F32)
        carry1 = jnp.zeros((modes, LANES), F32)
        for j in range(SUB):
            pick = pl.ds(j, modes, stride=SUB)
            end, end1 = ebuf[pick, :], e1buf[pick, :]
            ebuf[pick, :] = carry
            e1buf[pick, :] = carry1
            carry1 = pole_sub * (carry1 + steps * carry) + end1
            carry = pole_sub * carry + end
        y_ref[:, lanes] = ebuf[...].astype(BF16)
        y1_ref[:, lanes] = e1buf[...].astype(BF16)
        end_ref[0:modes, there] = carry
        end_ref[modes : 2 * modes, there] = carry1


def gradient_kernel(length, base, lent, parts, *refs):
    own_ref, *got_refs = refs[: 1 + parts]
    (sigp_ref, dec_ref, y_ref, y1_ref,
     grad_ref, z_ref, pay_ref, sbuf, s1buf, rbuf, dbuf, gf) = refs[1 + parts :]
    tokens, width = grad_ref.shape
    modes = dec_ref.shape[0]
    steps = tokens // SUB
    mine = slice(base, base + width)
    place = lax.broadcasted_iota(jnp.int32, (HALF, LANES), 0).astype(F32) * steps
    lent_ref, *got_refs = got_refs
    total = own_ref[:, mine].astype(F32)
    total = total + lent_ref[:, own_ref.shape[1] * lent + base : own_ref.shape[1] * lent + base + width].astype(F32)
    for got in got_refs:
        total = total + got[...].astype(F32)
    grad_ref[...] = jnp.dot(
        interleave(tokens), total.astype(BF16), preferred_element_type=F32
    )

    @pl.loop(0, width // LANES)
    def _(block):
        here = lane_block(block)
        rate = dec_ref[:, lane_block(block + base // LANES)] * (-1.0 / length)
        pole_all = jnp.exp(rate)
        both = [sigp_ref[pl.ds(SUB * i, SUB), here].astype(F32) for i in range(steps)]
        for half in range(2):
            values = [grad_ref[rows_of(i, half), here] for i in range(steps)]
            for first in range(0, modes, 8):
                poles = [spread(pole_all[n : n + 1]) for n in range(first, first + 8)]
                sums, firsts = recur(poles, values)
                for n in range(8):
                    rows = rows_of(first + n, half)
                    out = pl.ds(HALF * (first + n), HALF)
                    before, before1 = y_ref[rows, here].astype(F32), y1_ref[rows, here].astype(F32)
                    reach = jnp.exp(spread(rate[first + n : first + n + 1]) * (place + half * HALF * steps))
                    moved = reach * sums[n]
                    z_ref[block, rows, :] = moved
                    terms = (
                        (sbuf, moved),
                        (s1buf, reach * firsts[n] + (place + half * HALF * steps) * moved),
                        (rbuf, sums[n] * before),
                        (dbuf, sums[n] * before1 + firsts[n] * before),
                    )
                    for ref, term in terms:
                        ref[out, here] = term if half == 0 else ref[out, here] + term
            seen = [v[HALF * half : HALF * (half + 1)] for v in both]
            for lag in range(steps):
                term = pairwise([values[i + lag] * seen[i] for i in range(steps - lag)])
                out = pl.ds(HALF * lag, HALF)
                gf[out, here] = term if half == 0 else gf[out, here] + term

    adder = group_sums(modes, HALF)
    add = lambda m, ref: jnp.dot(m, ref[...], preferred_element_type=F32)
    lags = add(group_sums(steps, HALF), gf)
    res, dec = add(adder, rbuf), add(adder, dbuf)
    state, first = add(adder, sbuf), add(adder, s1buf)
    pole = jnp.exp(dec_ref[:, mine] * (-1.0 / length))
    res = res + lags[0:1]
    weight = pole
    for lag in range(1, steps):
        term = weight * lags[lag : lag + 1]
        res = res + term
        dec = dec + lag * term
        weight = weight * pole
    for k, rows in enumerate((state, res, dec, first)):
        pay_ref[k * modes : (k + 1) * modes, :] = rows
    pay_ref[4 * modes :, :] = jnp.broadcast_to(lags[0:1], (8, width))


def gradient_states(pieces, lent, width, base, sigp, decays, y, y1, length):
    tokens = sigp.shape[0]
    modes = decays.shape[0]
    buf = pltpu.VMEM((modes * HALF, width), F32)
    return pl.pallas_call(
        functools.partial(gradient_kernel, length, base, lent, len(pieces) - 1),
        out_shape=(
            jax.ShapeDtypeStruct((tokens, width), F32),
            jax.ShapeDtypeStruct((width // LANES, modes * SUB, LANES), F32),
            jax.ShapeDtypeStruct((4 * modes + 8, width), F32),
        ),
        in_specs=[VM] * (len(pieces) + 4),
        out_specs=(VM,) * 3,
        scratch_shapes=[buf] * 4 + [pltpu.VMEM((tokens // SUB * HALF, width), F32)],
        compiler_params=params(),
        cost_estimate=SMALL,
        name="gradient_states",
    )(*pieces, sigp, decays, y, y1)


def carry_out(outs, poles, starts):
    outs = list(outs)
    for i in reversed(range(len(outs))):
        outs[i] = outs[i] + pairwise(starts)
        if i:
            starts = [p * s for p, s in zip(poles, starts)]
    return outs


def local_kernel(length, base, grad_ref, z_ref, dec_ref, res_ref, gain_ref, loc_ref, cbuf):
    tokens, width = grad_ref.shape
    modes = dec_ref.shape[0]
    steps = tokens // SUB

    @pl.loop(0, width // LANES)
    def _(block):
        here = lane_block(block)
        lanes = lane_block(block + base // LANES)
        rate = dec_ref[:, lanes] * (1.0 / length)
        pole_all = jnp.exp(-rate)
        weight = res_ref[:, lanes] * (1.0 / math.sqrt(length))
        gain = spread(gain_ref[:, lanes])
        sums = jnp.zeros((modes, LANES), F32)
        for j in reversed(range(SUB)):
            pick = pl.ds(j, modes, stride=SUB)
            back = jnp.exp(rate * (steps * (j + 1) - 1))
            cbuf[pick, :] = weight * (back * sums)
            sums = sums + z_ref[block, pick, :]
        filt = []
        for _ in range(steps):
            filt.append(spread(jnp.sum(weight, axis=0, keepdims=True)))
            weight = weight * pole_all
        for half in range(2):
            values = [grad_ref[rows_of(i, half), here] for i in range(steps)]
            outs = [
                pairwise([filt[lag] * values[i + lag] for lag in range(steps - i)]) for i in range(steps)
            ]
            for first in range(0, modes, 8):
                picked = range(first, first + 8)
                poles = [spread(pole_all[n : n + 1]) for n in picked]
                outs = carry_out(outs, poles, [cbuf[rows_of(n, half), :] for n in picked])
            for i in range(steps):
                loc_ref[rows_of(i, half), here] = outs[i] + gain * values[i]


def local_part(grad, z, decays, residues, gain, length, base):
    tokens, width = grad.shape
    modes = decays.shape[0]
    return pl.pallas_call(
        functools.partial(local_kernel, length, base),
        out_shape=jax.ShapeDtypeStruct((tokens, width), F32),
        in_specs=[VM] * 5,
        out_specs=VM,
        scratch_shapes=[pltpu.VMEM((modes * SUB, LANES), F32)],
        compiler_params=params(),
        cost_estimate=SMALL,
        name="local_part",
    )(grad, z, decays, residues, gain)


def finish_kernel(length, hop, chunks, me_ref, there_ref, state_ref, later_ref, dec_ref, res_ref, *refs):
    locs = refs[: len(chunks)]
    o_ref, ores_ref, odec_ref, oskip_ref, vals = refs[len(chunks) :]
    tokens = o_ref.shape[0]
    modes = dec_ref.shape[0]
    steps = tokens // SUB
    scale = 1.0 / math.sqrt(length)
    ahead = (SUB - 1 - lax.broadcasted_iota(jnp.int32, (HALF, LANES), 0)).astype(F32) * steps
    vals[...] = later_step(me_ref, there_ref, later_ref, dec_ref, length, tokens, hop)

    for loc_ref, (low, high) in zip(locs, chunks):
        @pl.loop(0, (high - low) // LANES)
        def _(block):
            here = lane_block(block)
            lanes = lane_block(block + low // LANES)
            rate = dec_ref[:, lanes] * (-1.0 / length)
            pole_all = jnp.exp(rate)
            lead = scale * res_ref[:, lanes] * pole_all * vals[:, lanes]
            for half in range(2):
                outs = [loc_ref[rows_of(i, half), here] for i in range(steps)]
                for first in range(0, modes, 8):
                    picked = range(first, first + 8)
                    poles = [spread(pole_all[n : n + 1]) for n in picked]
                    starts = [
                        spread(lead[n : n + 1]) * jnp.exp(spread(rate[n : n + 1]) * (ahead - half * HALF * steps))
                        for n in picked
                    ]
                    outs = carry_out(outs, poles, starts)
                for i in range(steps):
                    loc_ref[rows_of(i, half), here] = outs[i]

    turn = interleave(tokens, transpose=True)
    for loc_ref, (low, high) in zip(locs, chunks):
        o_ref[:, low:high] = jnp.dot(
            turn, loc_ref[...].astype(BF16), preferred_element_type=F32
        ).astype(BF16)
    sums = state_ref[modes:, :] + there_ref[modes:, :].astype(F32)
    ores_ref[...] = sums[0:modes] * (1.0 / length)
    odec_ref[...] = sums[modes : 2 * modes] * (-1.0 / (length * length)) * res_ref[...]
    oskip_ref[...] = sums[2 * modes : 2 * modes + 1] * scale


def finish(me, there, state, later, decays, residues, locs, chunks, tokens, length, hop):
    modes, width = decays.shape
    return pl.pallas_call(
        functools.partial(finish_kernel, length, hop, chunks),
        out_shape=(
            jax.ShapeDtypeStruct((tokens, width), BF16),
            jax.ShapeDtypeStruct((modes, width), F32),
            jax.ShapeDtypeStruct((modes, width), F32),
            jax.ShapeDtypeStruct((1, width), F32),
        ),
        in_specs=[SM] + [VM] * (5 + len(locs)),
        out_specs=(VM,) * 4,
        scratch_shapes=[pltpu.VMEM((modes, width), F32)],
        compiler_params=params(),
        cost_estimate=SMALL,
        name="finish",
    )(me, there, state, later, decays, residues, *locs)


def place_bits(me_ref, hop):
    me = me_ref[0]
    return (me & (hop - 1)).astype(F32), (me & hop) != 0


def prefix_kernel(length, tokens, hop, me_ref, there_ref, state_ref, *refs):
    *before_ref, dec_ref, sent_ref, next_ref, after_ref = refs
    modes = dec_ref.shape[0]
    rate = dec_ref[...] * (1.0 / length)
    there = there_ref[...].astype(F32)
    other, other1 = there[:modes], there[modes:]
    state, first = state_ref[0:modes, :], state_ref[modes : 2 * modes, :]
    inside, upper = place_bits(me_ref, hop)
    reach = jnp.exp(-rate * (inside * tokens))
    after = jnp.where(upper, reach * other, 0.0)
    after1 = jnp.where(upper, reach * (other1 + (inside * tokens) * other), 0.0)
    if before_ref:
        after = after + before_ref[0][0:modes, :]
        after1 = after1 + before_ref[0][modes : 2 * modes, :]
    after_ref[0:modes, :] = after
    after_ref[modes : 2 * modes, :] = after1
    span = jnp.exp(-rate * (hop * tokens))
    late, early = jnp.where(upper, state, other), jnp.where(upper, other, state)
    late1, early1 = jnp.where(upper, first, other1), jnp.where(upper, other1, first)
    first = late1 + span * (early1 + (hop * tokens) * early)
    state = late + span * early
    for rows, value in ((slice(0, modes), state), (slice(modes, 2 * modes), first)):
        next_ref[rows, :] = value
        sent_ref[rows, :] = value.astype(BF16)


def later_step(me_ref, there_ref, later_ref, dec_ref, length, tokens, hop):
    modes = dec_ref.shape[0]
    inside, upper = place_bits(me_ref, hop)
    reach = jnp.exp(dec_ref[...] * (-1.0 / length) * ((hop - 1 - inside) * tokens))
    return later_ref[...] + jnp.where(upper, 0.0, reach * there_ref[0:modes, :].astype(F32))


def suffix_kernel(length, tokens, hop, me_ref, there_ref, state_ref, later_ref, dec_ref, sent_ref, next_ref, after_ref):
    modes = dec_ref.shape[0]
    after_ref[...] = later_step(me_ref, there_ref, later_ref, dec_ref, length, tokens, hop)
    _, upper = place_bits(me_ref, hop)
    span = jnp.exp(dec_ref[...] * (-1.0 / length) * (hop * tokens))
    there = there_ref[...].astype(F32)
    state, other = state_ref[0:modes, :], there[:modes]
    state = jnp.where(upper, other, state) + span * jnp.where(upper, state, other)
    sums = state_ref[modes:, :] + there[modes:]
    next_ref[0:modes, :] = state
    next_ref[modes:, :] = sums
    sent_ref[0:modes, :] = state.astype(BF16)
    sent_ref[modes:, :] = sums.astype(BF16)


def step_call(kernel, me, there, state, carried, decays):
    rows = state.shape[0] if kernel.func is prefix_kernel else decays.shape[0]
    args = [there, state, *carried, decays]
    return pl.pallas_call(
        kernel,
        out_shape=(
            jax.ShapeDtypeStruct(state.shape, BF16),
            jax.ShapeDtypeStruct(state.shape, F32),
            jax.ShapeDtypeStruct((rows, decays.shape[1]), F32),
        ),
        in_specs=[SM] + [VM] * len(args),
        out_specs=(VM,) * 3,
        compiler_params=params(),
        cost_estimate=SMALL,
        name="exchange_step",
    )(me, *args)


def gather_kernel(chunks, modes, before_ref, *refs):
    pays, (sent_ref, state_ref, later_ref) = refs[: len(chunks)], refs[len(chunks) :]
    later_ref[...] = jnp.zeros_like(later_ref)
    for pay_ref, (low, high) in zip(pays, chunks):
        state, res, dec, first = [pay_ref[k * modes : (k + 1) * modes, :] for k in range(4)]
        before = before_ref[0:modes, low:high]
        before1 = before_ref[modes : 2 * modes, low:high]
        res = res + state * before
        dec = dec + first * before + state * before1
        for k, value in enumerate((state, res, dec, pay_ref[4 * modes :, :])):
            rows = slice(k * modes, k * modes + value.shape[0])
            state_ref[rows, low:high] = value
            sent_ref[rows, low:high] = value.astype(BF16)


def gather_sums(pays, before, chunks):
    modes, width = before.shape[0] // 2, before.shape[1]
    rows = pays[0].shape[0] - modes
    return pl.pallas_call(
        functools.partial(gather_kernel, chunks, modes),
        out_shape=(
            jax.ShapeDtypeStruct((rows, width), BF16),
            jax.ShapeDtypeStruct((rows, width), F32),
            jax.ShapeDtypeStruct((modes, width), F32),
        ),
        in_specs=[VM] * (1 + len(pays)),
        out_specs=(VM,) * 3,
        compiler_params=params(),
        cost_estimate=SMALL,
        name="gather_sums",
    )(before, *pays)


def start_weights(blocks_ref, w_ref, w_buf, sems):
    width = w_buf.shape[1]
    copies = []
    for q in range(w_buf.shape[0]):
        start = pl.multiple_of(blocks_ref[q] * width, width)
        copies.append(pltpu.make_async_copy(w_ref.at[pl.ds(start, width)], w_buf.at[q], sems.at[q]))
        copies[-1].start()
    return copies


def finish_weights(copies, up_ref, w_buf, outs):
    width = w_buf.shape[1]
    for copy in copies:
        copy.wait()
    rows = min(width, 256)
    for q, out in enumerate(outs):
        for start in range(0, width, rows):
            out[:, start : start + rows] = lax.dot_general(
                up_ref[...], w_buf[q, start : start + rows, :], (((1,), (1,)), ((), ())),
                preferred_element_type=F32,
            ).astype(out.dtype)


def project_kernel(pieces, blocks_ref, up_ref, w_ref, *refs):
    outs, (w_buf, sems) = refs[:pieces], refs[pieces:]
    finish_weights(start_weights(blocks_ref, w_ref, w_buf, sems), up_ref, w_buf, outs)


def first_kernel(pieces, chunks, length, blocks_ref, up_ref, w_ref, sig_ref, dec_ref, *refs):
    lents = pieces // 2 + 1
    lent_ref, *pairs = refs[:lents]
    end_ref, sent_ref, *tables = refs[lents:-4]
    w_buf, sems, ebuf, e1buf = refs[-4:]
    width = w_buf.shape[1]
    outs = [lent_ref.at[:, k * width : (k + 1) * width] for k in range(lents)] + pairs
    copies = start_weights(blocks_ref, w_ref, w_buf, sems)
    for k, (low, high) in enumerate(chunks):
        signal_chunk(length, low, high, sig_ref, dec_ref, end_ref, *tables[3 * k : 3 * k + 3], ebuf, e1buf)
    sent_ref[...] = end_ref[...].astype(BF16)
    finish_weights(copies, up_ref, w_buf, outs)


def weight_scratch(pieces, width, feats):
    return [pltpu.VMEM((pieces, width, feats), BF16), pltpu.SemaphoreType.DMA((pieces,))]


def project(up, weight, width, blocks):
    tokens, feats = up.shape
    pieces = len(blocks)
    return pl.pallas_call(
        functools.partial(project_kernel, pieces),
        out_shape=[jax.ShapeDtypeStruct((tokens, width), BF16)] * pieces,
        in_specs=[pl.BlockSpec(memory_space=pltpu.SMEM), VM, pl.BlockSpec(memory_space=pl.ANY)],
        out_specs=[VM] * pieces,
        scratch_shapes=weight_scratch(pieces, width, feats),
        compiler_params=params(PROJECT_LIMIT),
        cost_estimate=SMALL,
        name="project",
    )(jnp.stack(blocks).astype(jnp.int32), up, weight)


def project_and_scan(up, weight, width, blocks, signal, decays, chunks, length):
    tokens, feats = up.shape
    modes = decays.shape[0]
    pieces = len(blocks)
    lents = pieces // 2 + 1
    shapes = [jax.ShapeDtypeStruct((tokens, lents * width), BF16)]
    shapes += [jax.ShapeDtypeStruct((tokens, width), BF16)] * (pieces - lents)
    shapes += [jax.ShapeDtypeStruct((2 * modes, width), dtype) for dtype in (F32, BF16)]
    for low, high in chunks:
        states = jax.ShapeDtypeStruct((modes * SUB, high - low), BF16)
        shapes += [jax.ShapeDtypeStruct((tokens, high - low), BF16), states, states]
    out = pl.pallas_call(
        functools.partial(first_kernel, pieces, chunks, length),
        out_shape=shapes,
        in_specs=[pl.BlockSpec(memory_space=pltpu.SMEM), VM, pl.BlockSpec(memory_space=pl.ANY), VM, VM],
        out_specs=[VM] * len(shapes),
        scratch_shapes=weight_scratch(pieces, width, feats) + [pltpu.VMEM((modes * SUB, LANES), F32)] * 2,
        compiler_params=params(PROJECT_LIMIT),
        cost_estimate=SMALL,
        name="project_and_scan",
    )(jnp.stack(blocks).astype(jnp.int32), up, weight, signal, decays)
    start = 1 + pieces - lents
    tables = out[start + 2 :]
    return out[0], out[1:start], out[start : start + 2], [
        tables[3 * k : 3 * k + 3] for k in range(len(chunks))
    ]


def pair_kernel(chunks, lent, mine_ref, lent_ref, *outs):
    base = mine_ref.shape[1] * lent
    for (low, high), out in zip(chunks, outs):
        total = mine_ref[:, low:high].astype(F32) + lent_ref[:, base + low : base + high].astype(F32)
        out[...] = total.astype(BF16)


def pair_sums(mine, lent, index, chunks):
    tokens = mine.shape[0]
    return pl.pallas_call(
        functools.partial(pair_kernel, chunks, index),
        out_shape=[jax.ShapeDtypeStruct((tokens, high - low), BF16) for low, high in chunks],
        in_specs=[VM] * 2,
        out_specs=[VM] * len(chunks),
        compiler_params=params(),
        cost_estimate=SMALL,
        name="pair_sums",
    )(mine, lent)


def send(x, axis, size, hop):
    return lax.ppermute(x, axis, [(i, i ^ hop) for i in range(size)])


def cuts(width):
    lane_blocks = width // LANES
    first = lane_blocks // 2 * LANES
    return [(0, first), (first, width)]


def body(signal, upstream, out_weight, residues, decays, skip_gain):
    tokens, width = signal.shape
    groups = lax.axis_size("ctx")
    blocks = lax.axis_size("ch")
    length = tokens * groups
    modes = residues.shape[1]
    me = lax.axis_index("ch")
    place = jnp.reshape(lax.axis_index("ctx").astype(jnp.int32), (1,))
    dec = decays.T
    res = residues.T
    gain = skip_gain[None, :]
    chunks = cuts(width)
    hops = range(2, blocks, 2)
    levels = [1 << k for k in range(groups.bit_length() - 1)]

    wanted = [me ^ hop ^ 1 for hop in hops] + [me ^ 1] + [me ^ hop for hop in hops]
    lent, parts, (state, sent), tables = project_and_scan(
        upstream, out_weight, width, wanted, signal, dec, chunks, length
    )
    lent = send(lent, "ch", blocks, 1)
    pairs = [pair_sums(part, lent, index, chunks) for index, part in enumerate(parts)]
    upstream, pairs = lax.optimization_barrier((upstream, pairs))
    arrived = [[send(pair[k], "ch", blocks, hop) for pair, hop in zip(pairs, hops)] for k in range(len(chunks))]
    (own,) = project(upstream, out_weight, width, [me])

    before = []
    for hop in levels:
        if hop == levels[-1]:
            sent, arrived = lax.optimization_barrier((sent, arrived))
        there = send(sent, "ctx", groups, hop)
        sent, state, *before = step_call(
            functools.partial(prefix_kernel, length, tokens, hop), place, there, state, before, dec
        )
    pays, locs = [], []
    for chunk, (low, high), (sigp, y, y1) in zip(arrived, chunks, tables):
        grad, z, pay = gradient_states(
            [own, lent, *chunk], len(hops), high - low, low, sigp, dec, y, y1, length
        )
        pays.append(pay)
        locs.append((grad, z, low))
    sent, state, later = gather_sums(pays, before[0], chunks)
    locs = [local_part(grad, z, dec, res, gain, length, low) for grad, z, low in locs]
    for hop in levels[:-1]:
        there = send(sent, "ctx", groups, hop)
        sent, state, later = step_call(
            functools.partial(suffix_kernel, length, tokens, hop), place, there, state, [later], dec
        )
    there = send(sent, "ctx", groups, levels[-1])
    out, ores, odec, oskip = finish(
        place, there, state, later, dec, res, locs, chunks, tokens, length, levels[-1]
    )
    return (out, ores.T, odec.T, oskip[0])


def solution(mesh):
    placed = (P("ctx", "ch"), P("ctx", "ch"), P(None, "ch"), P("ch", None), P("ch", None), P("ch"))
    return jax.shard_map(
        body,
        mesh=mesh,
        in_specs=placed,
        out_specs=(P("ctx", "ch"), P("ch", None), P("ch", None), P("ch")),
        check_vma=False,
    )
```

time: 691 us -> 63.5 us (0.09)
  waiting for transfers between devices: 318 us -> 18.5 us
  other arithmetic: 126 us -> 0.08 us
  blocking collectives: 116 us -> 0 us
  matrix products: 60.2 us -> 0 us
  local copies, waits for them, and re-layouts: 35.1 us -> 2.82 us
  Pallas kernels: 0 us -> 27.3 us
  between operations: 14.6 us -> 0.77 us
    all_to_all x3 -> x0, waiting for transfers between devices: 256 us -> none  [regroup(): lax.all_to_all(blocks, 'ctx', split_axis=0, concat_axis=0, tiled=True)]
    reduce_sum x17 -> x0, other arithmetic: 109 us -> none  [the longest x16 108 us: mode_step(): jnp.sum(cross_real * deriv_real + cross_imag * deriv_imag, axis=(0, 1))]
    all_to_all x1 -> x0, blocking collectives: 96.7 us -> none  [regroup(): lax.all_to_all(blocks, 'ctx', split_axis=0, concat_axis=0, tiled=True)]
    dot_general x13 -> x0, matrix products: 60.2 us -> none  [the longest x1 9.69 us: body(): lax.dot_general(out_weight, upstream, (((1,), (1,)), ((), ())), preferred...]
    reduce_scatter x1 -> x0, waiting for transfers between devices: 32.8 us -> none  [body(): lax.psum_scatter(lax.dot_general(out_weight, upstream, (((1,), (1,)), (()...]
    psum x1 -> x0, waiting for transfers between devices: 29.4 us -> none  [body(): totals = lax.psum((res_part, dec_part, skip_part), 'ctx')]
    pallas_call x0 -> x14, Pallas kernels: none -> 27.3 us  [the longest x1 9.46 us: project_and_scan(): pl.pallas_call(functools.partial(first_kernel, pieces, chunks, length), o...]
    psum x1 -> x0, blocking collectives: 19.8 us -> none  [body(): totals = lax.psum((res_part, dec_part, skip_part), 'ctx')]
  transfers between devices with their start and end apart: 5 -> 9, of which waited for: 5 -> 7; matrix products, arithmetic and copies ran while one was open for 1% -> 0% of each run, Pallas kernels for 0% -> 21%
where the time goes in v2:
time: 63.5 us; the launch traced here: 63.1 us
  Pallas kernels  27.3 us (43%)
  waiting for transfers between devices  18.5 us (29%)
  starting transfers between devices  13.7 us (22%)
  local copies, waits for them, and re-layouts  2.82 us (4%)
  between operations  0.77 us (1%)
    ppermute x9, waiting for transfers between devices, send(): return lax.ppermute(x, axis, [(i, i ^ hop) for i in range(size)])  18.5 us
    ppermute x9, starting transfers between devices, send(): return lax.ppermute(x, axis, [(i, i ^ hop) for i in range(size)])  13.7 us
    pallas_call x1, Pallas kernels, project_and_scan(): pl.pallas_call(functools.partial(first_kernel, pieces, chunks, length), o...  9.46 us
    pallas_call x2, Pallas kernels, gradient_states(): pl.pallas_call(functools.partial(gradient_kernel, length, base, lent, len...  6.33 us
    pallas_call x1, Pallas kernels, project(): pl.pallas_call(functools.partial(project_kernel, pieces), out_shape=[jax....  3.48 us
    pallas_call x1, Pallas kernels, finish(): pl.pallas_call(functools.partial(finish_kernel, length, hop, chunks), out...  2.85 us
    unnamed x20, local copies, waits for them, and re-layouts  2.82 us
    pallas_call x2, Pallas kernels, local_part(): pl.pallas_call(functools.partial(local_kernel, length, base), out_shape=j...  2.48 us
  transfers between devices with their start and end apart: 9, of which 7 were waited for; matrix products, arithmetic and copies ran while one was open for 0% of the time, Pallas kernels for 21%

profile of v2, /device:TPU:0, one launch (start us, length us, event | category | flops | bytes accessed | tf_op | source)
XLA Modules:
  0.0 63.1 jit_solution(8018078541178441106)
XLA Ops:
  0.6 0.1 pad_add_fusion.blocks_ref
  0.7 0.0 copy-start
  0.7 0.8 %copy-done = f32[1024,16]{0,1:T(8,128)S(1)} copy-done((f32[1024,16]{0,1:T(8,128)S(1)}, f32[1024,16]{0,1:T(8,128)}, u32[]{:S(2)}) %copy-start) | copy-done | bytes 65560
  1.6 0.0 copy-start.4
  1.6 1.0 %copy-done.4 = bf16[256,1024]{1,0:T(8,128)(2,1)S(1)} copy-done((bf16[256,1024]{1,0:T(8,128)(2,1)S(1)}, bf16[256,1024]{1,0:T(8,128)(2,1)}, u32[]{:S(2)}) %copy-start.4) | copy-done | bytes 524312
  2.6 9.5 %project_and_scan.1 = (bf16[256,2048]{1,0:T(8,128)(2,1)S(1)}, bf16[256,1024]{1,0:T(8,128)(2,1)S(1)}, f32[32,1024]{1,0:T(8,128)S(1)}, bf16[32,1024]{1,0:T(8,128)(...) custom-call(s32[3]{0:T(128)S(1)} %pad_add_fusion.blocks_ref, ...), custom_call_target="tpu_custom_call" | custom-call | flops 1 | bytes 1 | tf_op jit(solution)/shard_map/project_and_scan/pallas_call | solution.py:502
  12.1 0.0 copy-start.5
  12.1 0.0 copy-start.7
  12.1 0.0 copy-start.3
  12.1 0.0 copy-start.9
  12.1 0.5 collective-permute-start.2
  12.6 2.3 %collective-permute-done.2.lent_ref.refs_1_ = bf16[256,2048]{1,0:T(8,128)(2,1)S(1)} collective-permute-done((bf16[256,2048]{1,0:T(8,128)(2,1)S(1)}, bf16[256,2048]{1,0:T(8,128)(2,1)S(1)}, u32[]{:S(2)}, u32[]{:S(2)}) %collective-permute-start.2) | collective-permute-done | bytes 1048608 | tf_op jit(solution)/shard_map/ppermute | solution.py:540
  14.9 0.9 %pair_sums.1 = (bf16[256,512]{1,0:T(8,128)(2,1)}, bf16[256,512]{1,0:T(8,128)(2,1)}) custom-call(bf16[256,1024]{1,0:T(8,128)(2,1)S(1)} %get-tuple-element.54.mine_ref, bf16[256,2048]{1,0:T(8,128)(2,1)S(1)} %collective-permute-done.2.lent_ref.refs_1_), custom_call_target="tpu_custom_call" | custom-call | flops 1 | bytes 1 | tf_op jit(solution)/shard_map/pair_sums/pallas_call | solution.py:528
  15.8 0.0 copy-done.5
  15.8 0.0 copy-done.7
  15.8 2.9 %collective-permute-start.3 = (bf16[256,512]{1,0:T(8,128)(2,1)}, bf16[256,512]{1,0:T(8,128)(2,1)}, u32[]{:S(2)}, u32[]{:S(2)}) collective-permute-start(bf16[256,512]{1,0:T(8,128)(2,1)} %get-tuple-element.58), channel_id=1, source_target_pairs={{0,2},{1,3},{2,0},{3,1},{4,6},{5,7},{6,4},{7,5},{8,10},{9,11},{10,... | collective-permute-start | bytes 786440 | tf_op jit(solution)/shard_map/ppermute | solution.py:540
  18.7 0.1 collective-permute-start.4
  18.8 1.9 %collective-permute-start = (bf16[32,1024]{1,0:T(8,128)(2,1)}, bf16[32,1024]{1,0:T(8,128)(2,1)}, u32[]{:S(2)}, u32[]{:S(2)}) collective-permute-start(bf16[32,1024]{1,0:T(8,128)(2,1)} %get-tuple-element.48), channel_id=1, source_target_pairs={{0,4},{4,0},{8,12},{12,8},{16,20},{20,16},{24,28},{28,24},{1,5},{5... | collective-permute-start | bytes 196616 | tf_op jit(solution)/shard_map/ppermute | solution.py:540
  20.7 2.7 %collective-permute-done.there_ref = bf16[32,1024]{1,0:T(8,128)(2,1)} collective-permute-done((bf16[32,1024]{1,0:T(8,128)(2,1)}, bf16[32,1024]{1,0:T(8,128)(2,1)}, u32[]{:S(2)}, u32[]{:S(2)}) %collective-permute-start) | collective-permute-done | bytes 65568 | tf_op jit(solution)/shard_map/ppermute | solution.py:540
  23.3 0.0 copy-done.1
  23.3 0.9 %copy-done.8 = f32[32,1024]{1,0:T(8,128)S(1)} copy-done((f32[32,1024]{1,0:T(8,128)S(1)}, f32[32,1024]{1,0:T(8,128)}, u32[]{:S(2)}) %copy-start.8) | copy-done | bytes 131096
  24.2 0.9 %exchange_step.5 = (bf16[32,1024]{1,0:T(8,128)(2,1)S(1)}, f32[32,1024]{1,0:T(8,128)S(1)}, f32[32,1024]{1,0:T(8,128)S(1)}) custom-call(s32[1]{0:T(128)} %bitcast.me_ref, bf16[32,1024]{1,0:T(8,128)(2,1)} %collective-permute-done.there_ref, f32[32,1024]{1,0:T(8,128)S(1)} %copy-done.8, f32[16,1024]{1,0:T(8,128)S(1)} %bitcast.12), custom_call_target="tpu_custom_call" | custom-call | flops 1 | bytes 1 | tf_op jit(solution)/shard_map/exchange_step/pallas_call | solution.py:382
  25.1 2.1 %collective-permute-start.1 = (bf16[32,1024]{1,0:T(8,128)(2,1)S(1)}, bf16[32,1024]{1,0:T(8,128)(2,1)S(1)}, u32[]{:S(2)}, u32[]{:S(2)}) collective-permute-start(bf16[32,1024]{1,0:T(8,128)(2,1)S(1)} %get-tuple-element.50), channel_id=1, source_target_pairs={{0,8},{4,12},{8,0},{12,4},{16,24},{20,28},{24,16},{28,20},{1,9},{5... | collective-permute-start | bytes 196616 | tf_op jit(solution)/shard_map/ppermute | solution.py:540
  27.2 2.3 %collective-permute-done.1.there_ref = bf16[32,1024]{1,0:T(8,128)(2,1)S(1)} collective-permute-done((bf16[32,1024]{1,0:T(8,128)(2,1)S(1)}, bf16[32,1024]{1,0:T(8,128)(2,1)S(1)}, u32[]{:S(2)}, u32[]{:S(2)}) %collective-permute-start.1) | collective-permute-done | bytes 65568 | tf_op jit(solution)/shard_map/ppermute | solution.py:540
  29.5 0.1 exchange_step.6
  29.5 0.0 collective-permute-done.3.refs_2_
  29.6 1.7 %collective-permute-done.4.refs_2_ = bf16[256,512]{1,0:T(8,128)(2,1)} collective-permute-done((bf16[256,512]{1,0:T(8,128)(2,1)}, bf16[256,512]{1,0:T(8,128)(2,1)}, u32[]{:S(2)}, u32[]{:S(2)}) %collective-permute-start.4) | collective-permute-done | bytes 262176 | tf_op jit(solution)/shard_map/ppermute | solution.py:540
  31.2 2.8 %collective-permute-start.5 = (bf16[32,1024]{1,0:T(8,128)(2,1)S(1)}, bf16[32,1024]{1,0:T(8,128)(2,1)S(1)}, u32[]{:S(2)}, u32[]{:S(2)}) collective-permute-start(bf16[32,1024]{1,0:T(8,128)(2,1)S(1)} %get-tuple-element.60), channel_id=1, source_target_pairs={{0,16},{4,20},{8,24},{12,28},{16,0},{20,4},{24,8},{28,12},{1,17},{... | collective-permute-start | bytes 196616 | tf_op jit(solution)/shard_map/ppermute | solution.py:540
  34.0 0.0 copy-done.2
  34.0 3.5 %project.1.refs_0_ = bf16[256,1024]{1,0:T(8,128)(2,1)S(1)} custom-call(s32[1]{0:T(128)} %bitcast.5.blocks_ref, bf16[256,2048]{1,0:T(8,128)(2,1)S(1)} %copy-done.2, bf16[4096,2048]{1,0:T(8,128)(2,1)} %w_ref.3), custom_call_target="tpu_custom_call" | custom-call | flops 1 | bytes 1 | tf_op jit(solution)/shard_map/project/pallas_call | solution.py:479
  37.5 0.0 copy-done.6
  37.5 3.2 %gradient_states.3 = (f32[256,512]{1,0:T(8,128)S(1)}, f32[4,256,128]{2,1,0:T(8,128)S(1)}, f32[72,512]{1,0:T(8,128)S(1)}) custom-call(bf16[256,1024]{1,0:T(8,128)(2,1)S(1)} %project.1.refs_0_, bf16[256,2048]{1,0:T(8,128)(2,1)S(1)} %collective-permute-done.2.lent_ref.refs_1_, bf16[256,512]{1,0:T(8,128)(2,1)} %collective-permute-done.4.refs_2_, ...), custom_call_target="tpu_custom_call" | custom-call | flops 1 | bytes 1 | tf_op jit(solution)/shard_map/gradient_states/pallas_call | solution.py:189
  40.7 3.2 %gradient_states.2 = (f32[256,512]{1,0:T(8,128)S(1)}, f32[4,256,128]{2,1,0:T(8,128)S(1)}, f32[72,512]{1,0:T(8,128)S(1)}) custom-call(bf16[256,1024]{1,0:T(8,128)(2,1)S(1)} %project.1.refs_0_, bf16[256,2048]{1,0:T(8,128)(2,1)S(1)} %collective-permute-done.2.lent_ref.refs_1_, bf16[256,512]{1,0:T(8,128)(2,1)} %collective-permute-done.3.refs_2_, ...), custom_call_target="tpu_custom_call" | custom-call | flops 1 | bytes 1 | tf_op jit(solution)/shard_map/gradient_states/pallas_call | solution.py:189
  43.9 0.0 collective-permute-done.5.there_ref
  43.9 0.7 %exchange_step.7 = (bf16[32,1024]{1,0:T(8,128)(2,1)}, f32[32,1024]{1,0:T(8,128)}, f32[32,1024]{1,0:T(8,128)S(1)}) custom-call(s32[1]{0:T(128)} %bitcast.me_ref, bf16[32,1024]{1,0:T(8,128)(2,1)S(1)} %collective-permute-done.5.there_ref, f32[32,1024]{1,0:T(8,128)S(1)} %get-tuple-element.61.state_ref, f32[32,1024]{1,0:T(8,128)S(1)} %get-tuple-element.62.refs_0_, ...), custom_call_target="tpu_custom_call" | custom-call | flops 1 | bytes 1 | tf_op jit(solution)/shard_map/exchange_step/pallas_call | solution.py:382
  44.6 1.6 %collective-permute-start.6 = (bf16[56,1024]{1,0:T(8,128)(2,1)S(1)}, bf16[56,1024]{1,0:T(8,128)(2,1)S(1)}, u32[]{:S(2)}, u32[]{:S(2)}) collective-permute-start(bf16[56,1024]{1,0:T(8,128)(2,1)S(1)} %get-tuple-element.75), channel_id=1, source_target_pairs={{0,4},{4,0},{8,12},{12,8},{16,20},{20,16},{24,28},{28,24},{1,5},{5... | collective-permute-start | bytes 344072 | tf_op jit(solution)/shard_map/ppermute | solution.py:540
  46.2 3.3 %collective-permute-done.6.there_ref = bf16[56,1024]{1,0:T(8,128)(2,1)S(1)} collective-permute-done((bf16[56,1024]{1,0:T(8,128)(2,1)S(1)}, bf16[56,1024]{1,0:T(8,128)(2,1)S(1)}, u32[]{:S(2)}, u32[]{:S(2)}) %collective-permute-start.6) | collective-permute-done | bytes 114720 | tf_op jit(solution)/shard_map/ppermute | solution.py:540
  49.5 0.1 exchange_step.8
  49.6 1.6 %collective-permute-start.7 = (bf16[56,1024]{1,0:T(8,128)(2,1)S(1)}, bf16[56,1024]{1,0:T(8,128)(2,1)S(1)}, u32[]{:S(2)}, u32[]{:S(2)}) collective-permute-start(bf16[56,1024]{1,0:T(8,128)(2,1)S(1)} %get-tuple-element.78), channel_id=1, source_target_pairs={{0,8},{4,12},{8,0},{12,4},{16,24},{20,28},{24,16},{28,20},{1,9},{5... | collective-permute-start | bytes 344072 | tf_op jit(solution)/shard_map/ppermute | solution.py:540
  51.2 3.2 %collective-permute-done.7.there_ref = bf16[56,1024]{1,0:T(8,128)(2,1)S(1)} collective-permute-done((bf16[56,1024]{1,0:T(8,128)(2,1)S(1)}, bf16[56,1024]{1,0:T(8,128)(2,1)S(1)}, u32[]{:S(2)}, u32[]{:S(2)}) %collective-permute-start.7) | collective-permute-done | bytes 114720 | tf_op jit(solution)/shard_map/ppermute | solution.py:540
  54.4 0.1 exchange_step.9
  54.5 0.2 collective-permute-start.8
  54.7 0.0 copy-done.3
  54.7 0.0 copy-done.9
  54.7 1.2 %local_part.3.refs_1_ = f32[256,512]{1,0:T(8,128)S(1)} custom-call(f32[256,512]{1,0:T(8,128)S(1)} %get-tuple-element.86.grad_ref, f32[4,256,128]{2,1,0:T(8,128)S(1)} %get-tuple-element.87.z_ref, f32[16,1024]{1,0:T(8,128)S(1)} %bitcast.19, f32[16,1024]{1,0:T(8,128)S(1)} %bitcast.22, f32[1,1024]{1,0:T(1,128)S(1)} %bitcast.25), custom_call_target="tpu_custom_call" | custom-call | flops 1 | bytes 1 | tf_op jit(solution)/shard_map/local_part/pallas_call | solution.py:253
  55.9 1.2 %local_part.2.refs_0_ = f32[256,512]{1,0:T(8,128)S(1)} custom-call(f32[256,512]{1,0:T(8,128)S(1)} %get-tuple-element.84.grad_ref, f32[4,256,128]{2,1,0:T(8,128)S(1)} %get-tuple-element.85.z_ref, f32[16,1024]{1,0:T(8,128)S(1)} %bitcast.20, f32[16,1024]{1,0:T(8,128)S(1)} %bitcast.23, f32[1,1024]{1,0:T(1,128)S(1)} %bitcast.26), custom_call_target="tpu_custom_call" | custom-call | flops 1 | bytes 1 | tf_op jit(solution)/shard_map/local_part/pallas_call | solution.py:253
  57.2 3.1 %collective-permute-done.8.there_ref = bf16[56,1024]{1,0:T(8,128)(2,1)S(1)} collective-permute-done((bf16[56,1024]{1,0:T(8,128)(2,1)S(1)}, bf16[56,1024]{1,0:T(8,128)(2,1)S(1)}, u32[]{:S(2)}, u32[]{:S(2)}) %collective-permute-start.8) | collective-permute-done | bytes 114720 | tf_op jit(solution)/shard_map/ppermute | solution.py:540
  60.2 2.9 %finish.1 = (bf16[256,1024]{1,0:T(8,128)(2,1)}, f32[16,1024]{1,0:T(8,128)}, f32[16,1024]{1,0:T(8,128)}, f32[1,1024]{1,0:T(1,128)}) custom-call(s32[1]{0:T(128)} %bitcast.me_ref, bf16[56,1024]{1,0:T(8,128)(2,1)S(1)} %collective-permute-done.8.there_ref, f32[56,1024]{1,0:T(8,128)S(1)} %get-tuple-element.82.state_ref, ...), custom_call_target="tpu_custom_call" | custom-call | flops 1 | bytes 1 | tf_op jit(solution)/shard_map/finish/pallas_call | solution.py:309
  (5 shorter events, 0.0 us)
Async XLA Ops:
  0.7 0.8 %copy-start = (f32[1024,16]{0,1:T(8,128)S(1)}, f32[1024,16]{0,1:T(8,128)}, u32[]{:S(2)}) copy-start(f32[1024,16]{0,1:T(8,128)} %param.10) | copy-start | bytes 196612
  1.6 1.0 %copy-start.4 = (bf16[256,1024]{1,0:T(8,128)(2,1)S(1)}, bf16[256,1024]{1,0:T(8,128)(2,1)}, u32[]{:S(2)}) copy-start(bf16[256,1024]{1,0:T(8,128)(2,1)} %sig_ref.1) | copy-start | bytes 1572868
  2.6 20.7 %copy-start.1 = (f32[1024,16]{0,1:T(8,128)S(1)}, f32[1024,16]{0,1:T(8,128)}, u32[]{:S(2)}) copy-start(f32[1024,16]{0,1:T(8,128)} %param.10) | copy-start | bytes 196612
  2.6 31.4 %copy-start.2 = (bf16[256,2048]{1,0:T(8,128)(2,1)S(1)}, bf16[256,2048]{1,0:T(8,128)(2,1)}, u32[]{:S(2)}) copy-start(bf16[256,2048]{1,0:T(8,128)(2,1)} %up_ref.2) | copy-start | bytes 3145732
  12.1 3.7 %copy-start.5 = (bf16[256,512]{1,0:T(8,128)(2,1)}, bf16[256,512]{1,0:T(8,128)(2,1)S(1)}, u32[]{:S(2)}) copy-start(bf16[256,512]{1,0:T(8,128)(2,1)S(1)} %get-tuple-element.73.refs_6_) | copy-start | bytes 786436
  12.1 3.7 %copy-start.7 = (f32[32,1024]{1,0:T(8,128)}, f32[32,1024]{1,0:T(8,128)S(1)}, u32[]{:S(2)}) copy-start(f32[32,1024]{1,0:T(8,128)S(1)} %get-tuple-element.49.state_ref) | copy-start | bytes 393220
  12.1 42.6 %copy-start.3 = (f32[1024,16]{0,1:T(8,128)S(1)}, f32[1024,16]{0,1:T(8,128)}, u32[]{:S(2)}) copy-start(f32[1024,16]{0,1:T(8,128)} %param.9) | copy-start | bytes 196612
  12.1 42.6 %copy-start.9 = (f32[1024]{0:T(1024)S(1)}, f32[1024]{0:T(1024)}, u32[]{:S(2)}) copy-start(f32[1024]{0:T(1024)} %param.11) | copy-start | bytes 12292
  12.1 2.8 %collective-permute-start.2 = (bf16[256,2048]{1,0:T(8,128)(2,1)S(1)}, bf16[256,2048]{1,0:T(8,128)(2,1)S(1)}, u32[]{:S(2)}, u32[]{:S(2)}) collective-permute-start(bf16[256,2048]{1,0:T(8,128)(2,1)S(1)} %get-tuple-element.55), channel_id=1, source_target_pairs={{0,1},{1,0},{2,3},{3,2},{4,5},{5,4},{6,7},{7,6},{8,9},{9,8},{10,11... | collective-permute-start | bytes 3145736 | tf_op jit(solution)/shard_map/ppermute | solution.py:540
  15.8 13.8 %collective-permute-start.3 = (bf16[256,512]{1,0:T(8,128)(2,1)}, bf16[256,512]{1,0:T(8,128)(2,1)}, u32[]{:S(2)}, u32[]{:S(2)}) collective-permute-start(bf16[256,512]{1,0:T(8,128)(2,1)} %get-tuple-element.58), channel_id=1, source_target_pairs={{0,2},{1,3},{2,0},{3,1},{4,6},{5,7},{6,4},{7,5},{8,10},{9,11},{10,... | collective-permute-start | bytes 786440 | tf_op jit(solution)/shard_map/ppermute | solution.py:540
  18.7 12.5 %collective-permute-start.4 = (bf16[256,512]{1,0:T(8,128)(2,1)}, bf16[256,512]{1,0:T(8,128)(2,1)}, u32[]{:S(2)}, u32[]{:S(2)}) collective-permute-start(bf16[256,512]{1,0:T(8,128)(2,1)} %get-tuple-element.59), channel_id=1, source_target_pairs={{0,2},{1,3},{2,0},{3,1},{4,6},{5,7},{6,4},{7,5},{8,10},{9,11},{10,... | collective-permute-start | bytes 786440 | tf_op jit(solution)/shard_map/ppermute | solution.py:540
  18.8 4.6 %collective-permute-start = (bf16[32,1024]{1,0:T(8,128)(2,1)}, bf16[32,1024]{1,0:T(8,128)(2,1)}, u32[]{:S(2)}, u32[]{:S(2)}) collective-permute-start(bf16[32,1024]{1,0:T(8,128)(2,1)} %get-tuple-element.48), channel_id=1, source_target_pairs={{0,4},{4,0},{8,12},{12,8},{16,20},{20,16},{24,28},{28,24},{1,5},{5... | collective-permute-start | bytes 196616 | tf_op jit(solution)/shard_map/ppermute | solution.py:540
  20.7 16.8 %copy-start.6 = (bf16[256,512]{1,0:T(8,128)(2,1)S(1)}, bf16[256,512]{1,0:T(8,128)(2,1)}, u32[]{:S(2)}) copy-start(bf16[256,512]{1,0:T(8,128)(2,1)} %copy-done.5) | copy-start | bytes 786436
  23.3 0.9 %copy-start.8 = (f32[32,1024]{1,0:T(8,128)S(1)}, f32[32,1024]{1,0:T(8,128)}, u32[]{:S(2)}) copy-start(f32[32,1024]{1,0:T(8,128)} %copy-done.7) | copy-start | bytes 393220
  25.1 4.3 %collective-permute-start.1 = (bf16[32,1024]{1,0:T(8,128)(2,1)S(1)}, bf16[32,1024]{1,0:T(8,128)(2,1)S(1)}, u32[]{:S(2)}, u32[]{:S(2)}) collective-permute-start(bf16[32,1024]{1,0:T(8,128)(2,1)S(1)} %get-tuple-element.50), channel_id=1, source_target_pairs={{0,8},{4,12},{8,0},{12,4},{16,24},{20,28},{24,16},{28,20},{1,9},{5... | collective-permute-start | bytes 196616 | tf_op jit(solution)/shard_map/ppermute | solution.py:540
  31.2 12.7 %collective-permute-start.5 = (bf16[32,1024]{1,0:T(8,128)(2,1)S(1)}, bf16[32,1024]{1,0:T(8,128)(2,1)S(1)}, u32[]{:S(2)}, u32[]{:S(2)}) collective-permute-start(bf16[32,1024]{1,0:T(8,128)(2,1)S(1)} %get-tuple-element.60), channel_id=1, source_target_pairs={{0,16},{4,20},{8,24},{12,28},{16,0},{20,4},{24,8},{28,12},{1,17},{... | collective-permute-start | bytes 196616 | tf_op jit(solution)/shard_map/ppermute | solution.py:540
  44.6 4.9 %collective-permute-start.6 = (bf16[56,1024]{1,0:T(8,128)(2,1)S(1)}, bf16[56,1024]{1,0:T(8,128)(2,1)S(1)}, u32[]{:S(2)}, u32[]{:S(2)}) collective-permute-start(bf16[56,1024]{1,0:T(8,128)(2,1)S(1)} %get-tuple-element.75), channel_id=1, source_target_pairs={{0,4},{4,0},{8,12},{12,8},{16,20},{20,16},{24,28},{28,24},{1,5},{5... | collective-permute-start | bytes 344072 | tf_op jit(solution)/shard_map/ppermute | solution.py:540
  49.6 4.9 %collective-permute-start.7 = (bf16[56,1024]{1,0:T(8,128)(2,1)S(1)}, bf16[56,1024]{1,0:T(8,128)(2,1)S(1)}, u32[]{:S(2)}, u32[]{:S(2)}) collective-permute-start(bf16[56,1024]{1,0:T(8,128)(2,1)S(1)} %get-tuple-element.78), channel_id=1, source_target_pairs={{0,8},{4,12},{8,0},{12,4},{16,24},{20,28},{24,16},{28,20},{1,9},{5... | collective-permute-start | bytes 344072 | tf_op jit(solution)/shard_map/ppermute | solution.py:540
  54.5 5.8 %collective-permute-start.8 = (bf16[56,1024]{1,0:T(8,128)(2,1)S(1)}, bf16[56,1024]{1,0:T(8,128)(2,1)S(1)}, u32[]{:S(2)}, u32[]{:S(2)}) collective-permute-start(bf16[56,1024]{1,0:T(8,128)(2,1)S(1)} %get-tuple-element.81), channel_id=1, source_target_pairs={{0,16},{4,20},{8,24},{12,28},{16,0},{20,4},{24,8},{28,12},{1,17},{... | collective-permute-start | bytes 344072 | tf_op jit(solution)/shard_map/ppermute | solution.py:540

commit v3 on v2

--- a/solution.py
+++ b/solution.py
@@ -14,7 +14,7 @@
 HALF = 8
 LANES = 128
 VMEM_LIMIT = 12 * 1024 * 1024
-PROJECT_LIMIT = 50 * 1024 * 1024
+PROJECT_LIMIT = 43 * 1024 * 1024
 VM = pl.BlockSpec(memory_space=pltpu.VMEM)
 SM = pl.BlockSpec(memory_space=pltpu.SMEM)
 
@@ -37,6 +37,10 @@
 
 
 SMALL = pl.CostEstimate(flops=1, bytes_accessed=1, transcendentals=0)
+
+
+def takes(microseconds):
+    return pl.CostEstimate(flops=int(microseconds * 1e9), bytes_accessed=1, transcendentals=0)
 
 
 def spread(row):
@@ -115,22 +119,67 @@
 
 
 def gradient_kernel(length, base, lent, parts, *refs):
-    own_ref, *got_refs = refs[: 1 + parts]
-    (sigp_ref, dec_ref, y_ref, y1_ref,
-     grad_ref, z_ref, pay_ref, sbuf, s1buf, rbuf, dbuf, gf) = refs[1 + parts :]
+    own_ref, lent_ref, *got_refs = refs[: 1 + parts]
+    dec_ref, grad_ref, z_ref, state_ref, sbuf = refs[1 + parts :]
     tokens, width = grad_ref.shape
     modes = dec_ref.shape[0]
     steps = tokens // SUB
-    mine = slice(base, base + width)
+    first_lent = own_ref.shape[1] * lent + base
     place = lax.broadcasted_iota(jnp.int32, (HALF, LANES), 0).astype(F32) * steps
-    lent_ref, *got_refs = got_refs
-    total = own_ref[:, mine].astype(F32)
-    total = total + lent_ref[:, own_ref.shape[1] * lent + base : own_ref.shape[1] * lent + base + width].astype(F32)
+    total = own_ref[:, base : base + width].astype(F32)
+    total = total + lent_ref[:, first_lent : first_lent + width].astype(F32)
     for got in got_refs:
         total = total + got[...].astype(F32)
     grad_ref[...] = jnp.dot(
         interleave(tokens), total.astype(BF16), preferred_element_type=F32
     )
+
+    @pl.loop(0, width // LANES)
+    def _(block):
+        here = lane_block(block)
+        rate = dec_ref[:, lane_block(block + base // LANES)] * (-1.0 / length)
+        pole_all = jnp.exp(rate)
+        for half in range(2):
+            values = [grad_ref[rows_of(i, half), here] for i in range(steps)]
+            for first in range(0, modes, 8):
+                poles = [spread(pole_all[n : n + 1]) for n in range(first, first + 8)]
+                sums = [values[-1]] * 8
+                for value in values[-2::-1]:
+                    sums = [p * v + value for p, v in zip(poles, sums)]
+                for n in range(8):
+                    out = pl.ds(HALF * (first + n), HALF)
+                    reach = jnp.exp(spread(rate[first + n : first + n + 1]) * (place + half * HALF * steps))
+                    moved = reach * sums[n]
+                    z_ref[block, rows_of(first + n, half), :] = moved
+                    sbuf[out, here] = moved if half == 0 else sbuf[out, here] + moved
+
+    state_ref[...] = jnp.dot(group_sums(modes, HALF), sbuf[...], preferred_element_type=F32)
+
+
+def gradient_states(pieces, lent, width, base, decays, length):
+    tokens = pieces[0].shape[0]
+    modes = decays.shape[0]
+    return pl.pallas_call(
+        functools.partial(gradient_kernel, length, base, lent, len(pieces) - 1),
+        out_shape=(
+            jax.ShapeDtypeStruct((tokens, width), F32),
+            jax.ShapeDtypeStruct((width // LANES, modes * SUB, LANES), F32),
+            jax.ShapeDtypeStruct((modes, width), F32),
+        ),
+        in_specs=[VM] * (len(pieces) + 1),
+        out_specs=(VM,) * 3,
+        scratch_shapes=[pltpu.VMEM((modes * HALF, width), F32)],
+        compiler_params=params(),
+        cost_estimate=takes(1),
+        name="gradient_states",
+    )(*pieces, decays)
+
+
+def filter_kernel(length, base, grad_ref, sigp_ref, dec_ref, y_ref, y1_ref, pay_ref, s1buf, rbuf, dbuf, gf):
+    tokens, width = grad_ref.shape
+    modes = dec_ref.shape[0]
+    steps = tokens // SUB
+    place = lax.broadcasted_iota(jnp.int32, (HALF, LANES), 0).astype(F32) * steps
 
     @pl.loop(0, width // LANES)
     def _(block):
@@ -147,12 +196,10 @@
                     rows = rows_of(first + n, half)
                     out = pl.ds(HALF * (first + n), HALF)
                     before, before1 = y_ref[rows, here].astype(F32), y1_ref[rows, here].astype(F32)
-                    reach = jnp.exp(spread(rate[first + n : first + n + 1]) * (place + half * HALF * steps))
-                    moved = reach * sums[n]
-                    z_ref[block, rows, :] = moved
+                    ahead = place + half * HALF * steps
+                    reach = jnp.exp(spread(rate[first + n : first + n + 1]) * ahead)
                     terms = (
-                        (sbuf, moved),
-                        (s1buf, reach * firsts[n] + (place + half * HALF * steps) * moved),
+                        (s1buf, reach * (firsts[n] + ahead * sums[n])),
                         (rbuf, sums[n] * before),
                         (dbuf, sums[n] * before1 + firsts[n] * before),
                     )
@@ -167,9 +214,8 @@
     adder = group_sums(modes, HALF)
     add = lambda m, ref: jnp.dot(m, ref[...], preferred_element_type=F32)
     lags = add(group_sums(steps, HALF), gf)
-    res, dec = add(adder, rbuf), add(adder, dbuf)
-    state, first = add(adder, sbuf), add(adder, s1buf)
-    pole = jnp.exp(dec_ref[:, mine] * (-1.0 / length))
+    res, dec, first = add(adder, rbuf), add(adder, dbuf), add(adder, s1buf)
+    pole = jnp.exp(dec_ref[:, base : base + width] * (-1.0 / length))
     res = res + lags[0:1]
     weight = pole
     for lag in range(1, steps):
@@ -177,29 +223,24 @@
         res = res + term
         dec = dec + lag * term
         weight = weight * pole
-    for k, rows in enumerate((state, res, dec, first)):
+    for k, rows in enumerate((res, dec, first, jnp.broadcast_to(lags[0:1], (modes, width)))):
         pay_ref[k * modes : (k + 1) * modes, :] = rows
-    pay_ref[4 * modes :, :] = jnp.broadcast_to(lags[0:1], (8, width))
-
-
-def gradient_states(pieces, lent, width, base, sigp, decays, y, y1, length):
-    tokens = sigp.shape[0]
+
+
+def filter_sums(grad, sigp, decays, y, y1, length, base):
+    tokens, width = grad.shape
     modes = decays.shape[0]
     buf = pltpu.VMEM((modes * HALF, width), F32)
     return pl.pallas_call(
-        functools.partial(gradient_kernel, length, base, lent, len(pieces) - 1),
-        out_shape=(
-            jax.ShapeDtypeStruct((tokens, width), F32),
-            jax.ShapeDtypeStruct((width // LANES, modes * SUB, LANES), F32),
-            jax.ShapeDtypeStruct((4 * modes + 8, width), F32),
-        ),
-        in_specs=[VM] * (len(pieces) + 4),
-        out_specs=(VM,) * 3,
-        scratch_shapes=[buf] * 4 + [pltpu.VMEM((tokens // SUB * HALF, width), F32)],
-        compiler_params=params(),
-        cost_estimate=SMALL,
-        name="gradient_states",
-    )(*pieces, sigp, decays, y, y1)
+        functools.partial(filter_kernel, length, base),
+        out_shape=jax.ShapeDtypeStruct((4 * modes, width), F32),
+        in_specs=[VM] * 5,
+        out_specs=VM,
+        scratch_shapes=[buf] * 3 + [pltpu.VMEM((tokens // SUB * HALF, width), F32)],
+        compiler_params=params(),
+        cost_estimate=takes(3),
+        name="filter_sums",
+    )(grad, sigp, decays, y, y1)
 
 
 def carry_out(outs, poles, starts):
@@ -257,20 +298,22 @@
         out_specs=VM,
         scratch_shapes=[pltpu.VMEM((modes * SUB, LANES), F32)],
         compiler_params=params(),
-        cost_estimate=SMALL,
+        cost_estimate=takes(1.5),
         name="local_part",
     )(grad, z, decays, residues, gain)
 
 
-def finish_kernel(length, hop, chunks, me_ref, there_ref, state_ref, later_ref, dec_ref, res_ref, *refs):
+def finish_kernel(length, hop, chunks, me_ref, there_ref, later_ref, dec_ref, res_ref, *refs):
     locs = refs[: len(chunks)]
-    o_ref, ores_ref, odec_ref, oskip_ref, vals = refs[len(chunks) :]
+    o_ref, vals = refs[len(chunks) :]
     tokens = o_ref.shape[0]
     modes = dec_ref.shape[0]
     steps = tokens // SUB
     scale = 1.0 / math.sqrt(length)
     ahead = (SUB - 1 - lax.broadcasted_iota(jnp.int32, (HALF, LANES), 0)).astype(F32) * steps
-    vals[...] = later_step(me_ref, there_ref, later_ref, dec_ref, length, tokens, hop)
+    vals[...] = later_step(
+        me_ref, there_ref.at[0:modes, :], later_ref[...], dec_ref, length, tokens, hop
+    )
 
     for loc_ref, (low, high) in zip(locs, chunks):
         @pl.loop(0, (high - low) // LANES)
@@ -298,133 +341,221 @@
         o_ref[:, low:high] = jnp.dot(
             turn, loc_ref[...].astype(BF16), preferred_element_type=F32
         ).astype(BF16)
-    sums = state_ref[modes:, :] + there_ref[modes:, :].astype(F32)
+
+
+def finish(me, there, later, decays, residues, locs, chunks, tokens, length, hop):
+    modes, width = decays.shape
+    return pl.pallas_call(
+        functools.partial(finish_kernel, length, hop, chunks),
+        out_shape=jax.ShapeDtypeStruct((tokens, width), BF16),
+        in_specs=[SM] + [VM] * (4 + len(locs)),
+        out_specs=VM,
+        scratch_shapes=[pltpu.VMEM((modes, width), F32)],
+        compiler_params=params(),
+        cost_estimate=takes(3),
+        name="finish",
+    )(me, there, later, decays, residues, *locs)
+
+
+def place_bits(me_ref, hop):
+    me = me_ref[0]
+    return (me & (hop - 1)).astype(F32), (me & hop) != 0
+
+
+def before_step(me_ref, there_ref, before_refs, dec_ref, length, tokens, hop):
+    modes = dec_ref.shape[0]
+    inside, upper = place_bits(me_ref, hop)
+    reach = jnp.exp(dec_ref[...] * (-1.0 / length) * (inside * tokens))
+    other, other1 = there_ref[0:modes, :].astype(F32), there_ref[modes : 2 * modes, :].astype(F32)
+    before = jnp.where(upper, reach * other, 0.0)
+    before1 = jnp.where(upper, reach * (other1 + (inside * tokens) * other), 0.0)
+    for ref in before_refs:
+        before = before + ref[0:modes, :]
+        before1 = before1 + ref[modes : 2 * modes, :]
+    return before, before1
+
+
+def prefix_kernel(length, tokens, hop, carried, me_ref, there_ref, state_ref, *refs):
+    refs, (sent_ref, after_ref, *next_ref) = refs[: 1 + carried], refs[1 + carried :]
+    *before_refs, dec_ref = refs
+    modes = dec_ref.shape[0]
+    rows, rows1 = slice(0, modes), slice(modes, 2 * modes)
+    after_ref[rows, :], after_ref[rows1, :] = before_step(
+        me_ref, there_ref, before_refs, dec_ref, length, tokens, hop
+    )
+    other, other1 = there_ref[rows, :].astype(F32), there_ref[rows1, :].astype(F32)
+    state, first = state_ref[rows, :], state_ref[rows1, :]
+    _, upper = place_bits(me_ref, hop)
+    span = jnp.exp(dec_ref[...] * (-1.0 / length) * (hop * tokens))
+    late, early = jnp.where(upper, state, other), jnp.where(upper, other, state)
+    late1, early1 = jnp.where(upper, first, other1), jnp.where(upper, other1, first)
+    first = late1 + span * (early1 + (hop * tokens) * early)
+    state = late + span * early
+    for part, value in ((rows, state), (rows1, first)):
+        for ref in next_ref:
+            ref[part, :] = value
+        sent_ref[part, :] = value.astype(BF16)
+
+
+def later_step(me_ref, there_ref, later, dec_ref, length, tokens, hop):
+    inside, upper = place_bits(me_ref, hop)
+    reach = jnp.exp(dec_ref[...] * (-1.0 / length) * ((hop - 1 - inside) * tokens))
+    return later + jnp.where(upper, 0.0, reach * there_ref[...].astype(F32))
+
+
+def suffix_step(me_ref, other, state, dec_ref, length, tokens, hop):
+    _, upper = place_bits(me_ref, hop)
+    span = jnp.exp(dec_ref[...] * (-1.0 / length) * (hop * tokens))
+    return jnp.where(upper, other, state) + span * jnp.where(upper, state, other)
+
+
+def merge_kernel(
+    length, tokens, hop, last, chunks, me_ref, there_ref, state_ref, ends_ref, *refs
+):
+    sent_ref, next_ref, later_ref, sums_ref = refs[-4:]
+    pays, (dec_ref, *before_refs) = refs[: len(chunks)], refs[len(chunks) : -4]
+    modes = dec_ref.shape[0]
+    all_before, all_before1 = before_step(me_ref, ends_ref, before_refs, dec_ref, length, tokens, last)
+    nothing = jnp.zeros_like(later_ref)
+    later_ref[...] = later_step(me_ref, there_ref, nothing, dec_ref, length, tokens, hop)
+    state = suffix_step(
+        me_ref, there_ref[...].astype(F32), state_ref[...], dec_ref, length, tokens, hop
+    )
+    next_ref[...] = state
+    sent_ref[0:modes, :] = state.astype(BF16)
+    for pay_ref, (low, high) in zip(pays, chunks):
+        res, dec, first, skip = [pay_ref[k * modes : (k + 1) * modes, :] for k in range(4)]
+        before, before1 = all_before[:, low:high], all_before1[:, low:high]
+        start = state_ref[:, low:high]
+        res = res + start * before
+        dec = dec + first * before + start * before1
+        for k, value in enumerate((res, dec, skip)):
+            sums_ref[k * modes : (k + 1) * modes, low:high] = value
+            sent_ref[(k + 1) * modes : (k + 2) * modes, low:high] = value.astype(BF16)
+
+
+def merge(me, there, state, ends, pays, decays, before, chunks, tokens, length, hop, last):
+    modes, width = decays.shape
+    args = (there, state, ends, *pays, decays, *before)
+    return pl.pallas_call(
+        functools.partial(merge_kernel, length, tokens, hop, last, chunks),
+        out_shape=tuple(
+            jax.ShapeDtypeStruct((k * modes, width), dtype)
+            for k, dtype in ((4, BF16), (1, F32), (1, F32), (3, F32))
+        ),
+        in_specs=[SM] + [VM] * len(args),
+        out_specs=(VM,) * 4,
+        compiler_params=params(),
+        cost_estimate=SMALL,
+        name="merge",
+    )(me, *args)
+
+
+def tail_kernel(
+    length, tokens, hop, me_ref, there_ref, state_ref, later_ref, sums_ref, dec_ref,
+    sent_ref, after_ref, total_ref, *next_ref,
+):
+    modes = dec_ref.shape[0]
+    there = there_ref.at[0:modes, :]
+    after_ref[...] = later_step(me_ref, there, later_ref[...], dec_ref, length, tokens, hop)
+    state = suffix_step(me_ref, there[...].astype(F32), state_ref[...], dec_ref, length, tokens, hop)
+    if next_ref:
+        next_ref[0][...] = state
+    sent_ref[0:modes, :] = state.astype(BF16)
+    sums = sums_ref[...] + there_ref[modes:, :].astype(F32)
+    total_ref[...] = sums
+    sent_ref[modes:, :] = sums.astype(BF16)
+
+
+def tail_step(me, there, state, later, sums, decays, tokens, length, hop, more):
+    args = (there, state, later, sums, decays)
+    outs = (there, later, sums) + ((state,) if more else ())
+    return pl.pallas_call(
+        functools.partial(tail_kernel, length, tokens, hop),
+        out_shape=tuple(jax.ShapeDtypeStruct(x.shape, x.dtype) for x in outs),
+        in_specs=[SM] + [VM] * 5,
+        out_specs=(VM,) * len(outs),
+        compiler_params=params(),
+        cost_estimate=SMALL,
+        name="tail_step",
+    )(me, *args)
+
+
+def sum_kernel(there_ref, sums_ref, sent_ref, total_ref):
+    sums = sums_ref[...] + there_ref[there_ref.shape[0] - sums_ref.shape[0] :, :].astype(F32)
+    total_ref[...] = sums
+    sent_ref[...] = sums.astype(BF16)
+
+
+def sum_step(there, sums):
+    return pl.pallas_call(
+        sum_kernel,
+        out_shape=(jax.ShapeDtypeStruct(sums.shape, BF16), jax.ShapeDtypeStruct(sums.shape, F32)),
+        in_specs=[VM] * 2,
+        out_specs=(VM,) * 2,
+        compiler_params=params(),
+        cost_estimate=SMALL,
+        name="sum_step",
+    )(there, sums)
+
+
+def result_kernel(length, there_ref, sums_ref, res_ref, ores_ref, odec_ref, oskip_ref):
+    modes = res_ref.shape[0]
+    sums = sums_ref[...] + there_ref[...].astype(F32)
     ores_ref[...] = sums[0:modes] * (1.0 / length)
     odec_ref[...] = sums[modes : 2 * modes] * (-1.0 / (length * length)) * res_ref[...]
-    oskip_ref[...] = sums[2 * modes : 2 * modes + 1] * scale
-
-
-def finish(me, there, state, later, decays, residues, locs, chunks, tokens, length, hop):
-    modes, width = decays.shape
-    return pl.pallas_call(
-        functools.partial(finish_kernel, length, hop, chunks),
+    oskip_ref[...] = sums[2 * modes : 2 * modes + 1] * (1.0 / math.sqrt(length))
+
+
+def results(there, sums, residues, length):
+    modes, width = residues.shape
+    return pl.pallas_call(
+        functools.partial(result_kernel, length),
         out_shape=(
-            jax.ShapeDtypeStruct((tokens, width), BF16),
             jax.ShapeDtypeStruct((modes, width), F32),
             jax.ShapeDtypeStruct((modes, width), F32),
             jax.ShapeDtypeStruct((1, width), F32),
         ),
-        in_specs=[SM] + [VM] * (5 + len(locs)),
-        out_specs=(VM,) * 4,
-        scratch_shapes=[pltpu.VMEM((modes, width), F32)],
+        in_specs=[VM] * 3,
+        out_specs=(VM,) * 3,
         compiler_params=params(),
         cost_estimate=SMALL,
-        name="finish",
-    )(me, there, state, later, decays, residues, *locs)
-
-
-def place_bits(me_ref, hop):
-    me = me_ref[0]
-    return (me & (hop - 1)).astype(F32), (me & hop) != 0
-
-
-def prefix_kernel(length, tokens, hop, me_ref, there_ref, state_ref, *refs):
-    *before_ref, dec_ref, sent_ref, next_ref, after_ref = refs
-    modes = dec_ref.shape[0]
-    rate = dec_ref[...] * (1.0 / length)
-    there = there_ref[...].astype(F32)
-    other, other1 = there[:modes], there[modes:]
-    state, first = state_ref[0:modes, :], state_ref[modes : 2 * modes, :]
-    inside, upper = place_bits(me_ref, hop)
-    reach = jnp.exp(-rate * (inside * tokens))
-    after = jnp.where(upper, reach * other, 0.0)
-    after1 = jnp.where(upper, reach * (other1 + (inside * tokens) * other), 0.0)
-    if before_ref:
-        after = after + before_ref[0][0:modes, :]
-        after1 = after1 + before_ref[0][modes : 2 * modes, :]
-    after_ref[0:modes, :] = after
-    after_ref[modes : 2 * modes, :] = after1
-    span = jnp.exp(-rate * (hop * tokens))
-    late, early = jnp.where(upper, state, other), jnp.where(upper, other, state)
-    late1, early1 = jnp.where(upper, first, other1), jnp.where(upper, other1, first)
-    first = late1 + span * (early1 + (hop * tokens) * early)
-    state = late + span * early
-    for rows, value in ((slice(0, modes), state), (slice(modes, 2 * modes), first)):
-        next_ref[rows, :] = value
-        sent_ref[rows, :] = value.astype(BF16)
-
-
-def later_step(me_ref, there_ref, later_ref, dec_ref, length, tokens, hop):
-    modes = dec_ref.shape[0]
-    inside, upper = place_bits(me_ref, hop)
-    reach = jnp.exp(dec_ref[...] * (-1.0 / length) * ((hop - 1 - inside) * tokens))
-    return later_ref[...] + jnp.where(upper, 0.0, reach * there_ref[0:modes, :].astype(F32))
-
-
-def suffix_kernel(length, tokens, hop, me_ref, there_ref, state_ref, later_ref, dec_ref, sent_ref, next_ref, after_ref):
-    modes = dec_ref.shape[0]
-    after_ref[...] = later_step(me_ref, there_ref, later_ref, dec_ref, length, tokens, hop)
-    _, upper = place_bits(me_ref, hop)
-    span = jnp.exp(dec_ref[...] * (-1.0 / length) * (hop * tokens))
-    there = there_ref[...].astype(F32)
-    state, other = state_ref[0:modes, :], there[:modes]
-    state = jnp.where(upper, other, state) + span * jnp.where(upper, state, other)
-    sums = state_ref[modes:, :] + there[modes:]
-    next_ref[0:modes, :] = state
-    next_ref[modes:, :] = sums
-    sent_ref[0:modes, :] = state.astype(BF16)
-    sent_ref[modes:, :] = sums.astype(BF16)
-
-
-def step_call(kernel, me, there, state, carried, decays):
-    rows = state.shape[0] if kernel.func is prefix_kernel else decays.shape[0]
+        name="results",
+    )(there, sums, residues)
+
+
+def prefix_step(me, there, state, carried, decays, tokens, length, hop, more):
     args = [there, state, *carried, decays]
-    return pl.pallas_call(
-        kernel,
-        out_shape=(
-            jax.ShapeDtypeStruct(state.shape, BF16),
-            jax.ShapeDtypeStruct(state.shape, F32),
-            jax.ShapeDtypeStruct((rows, decays.shape[1]), F32),
-        ),
+    dtypes = (BF16, F32, F32) if more else (BF16, F32)
+    return pl.pallas_call(
+        functools.partial(prefix_kernel, length, tokens, hop, len(carried)),
+        out_shape=tuple(jax.ShapeDtypeStruct(state.shape, dtype) for dtype in dtypes),
         in_specs=[SM] + [VM] * len(args),
-        out_specs=(VM,) * 3,
+        out_specs=(VM,) * len(dtypes),
         compiler_params=params(),
         cost_estimate=SMALL,
-        name="exchange_step",
+        name="prefix_step",
     )(me, *args)
 
 
-def gather_kernel(chunks, modes, before_ref, *refs):
-    pays, (sent_ref, state_ref, later_ref) = refs[: len(chunks)], refs[len(chunks) :]
-    later_ref[...] = jnp.zeros_like(later_ref)
-    for pay_ref, (low, high) in zip(pays, chunks):
-        state, res, dec, first = [pay_ref[k * modes : (k + 1) * modes, :] for k in range(4)]
-        before = before_ref[0:modes, low:high]
-        before1 = before_ref[modes : 2 * modes, low:high]
-        res = res + state * before
-        dec = dec + first * before + state * before1
-        for k, value in enumerate((state, res, dec, pay_ref[4 * modes :, :])):
-            rows = slice(k * modes, k * modes + value.shape[0])
-            state_ref[rows, low:high] = value
-            sent_ref[rows, low:high] = value.astype(BF16)
-
-
-def gather_sums(pays, before, chunks):
-    modes, width = before.shape[0] // 2, before.shape[1]
-    rows = pays[0].shape[0] - modes
-    return pl.pallas_call(
-        functools.partial(gather_kernel, chunks, modes),
-        out_shape=(
-            jax.ShapeDtypeStruct((rows, width), BF16),
-            jax.ShapeDtypeStruct((rows, width), F32),
-            jax.ShapeDtypeStruct((modes, width), F32),
-        ),
-        in_specs=[VM] * (1 + len(pays)),
-        out_specs=(VM,) * 3,
+def join_kernel(chunks, *refs):
+    sent_ref, state_ref = refs[len(chunks) :]
+    for part_ref, (low, high) in zip(refs, chunks):
+        state_ref[:, low:high] = part_ref[...]
+        sent_ref[:, low:high] = part_ref[...].astype(BF16)
+
+
+def join_states(states, chunks):
+    modes, width = states[0].shape[0], chunks[-1][1]
+    return pl.pallas_call(
+        functools.partial(join_kernel, chunks),
+        out_shape=tuple(jax.ShapeDtypeStruct((modes, width), dtype) for dtype in (BF16, F32)),
+        in_specs=[VM] * len(states),
+        out_specs=(VM,) * 2,
         compiler_params=params(),
         cost_estimate=SMALL,
-        name="gather_sums",
-    )(before, *pays)
+        name="join_states",
+    )(*states)
 
 
 def start_weights(blocks_ref, w_ref, w_buf, sems):
@@ -438,24 +569,50 @@
 
 
 def finish_weights(copies, up_ref, w_buf, outs):
-    width = w_buf.shape[1]
+    width = w_buf.shape[-2]
     for copy in copies:
         copy.wait()
     rows = min(width, 256)
     for q, out in enumerate(outs):
+        block = w_buf.at[q] if len(w_buf.shape) == 3 else w_buf
         for start in range(0, width, rows):
             out[:, start : start + rows] = lax.dot_general(
-                up_ref[...], w_buf[q, start : start + rows, :], (((1,), (1,)), ((), ())),
+                up_ref[...], block[start : start + rows, :], (((1,), (1,)), ((), ())),
                 preferred_element_type=F32,
             ).astype(out.dtype)
 
 
-def project_kernel(pieces, blocks_ref, up_ref, w_ref, *refs):
-    outs, (w_buf, sems) = refs[:pieces], refs[pieces:]
-    finish_weights(start_weights(blocks_ref, w_ref, w_buf, sems), up_ref, w_buf, outs)
-
-
-def first_kernel(pieces, chunks, length, blocks_ref, up_ref, w_ref, sig_ref, dec_ref, *refs):
+def fetch_kernel(block_ref, w_ref, o_ref, sem):
+    width = o_ref.shape[0]
+    start = pl.multiple_of(block_ref[0] * width, width)
+    copy = pltpu.make_async_copy(w_ref.at[pl.ds(start, width)], o_ref, sem)
+    copy.start()
+    copy.wait()
+
+
+def fetch(weight, width, block):
+    return pl.pallas_call(
+        fetch_kernel,
+        out_shape=jax.ShapeDtypeStruct((width, weight.shape[1]), BF16),
+        in_specs=[SM, pl.BlockSpec(memory_space=pl.ANY)],
+        out_specs=VM,
+        scratch_shapes=[pltpu.SemaphoreType.DMA],
+        compiler_params=params(PROJECT_LIMIT),
+        cost_estimate=takes(3),
+        name="fetch",
+    )(block, weight)
+
+
+def project_kernel(pieces, blocks_ref, up_hbm, w_ref, *refs):
+    outs, (w_buf, sems, up_ref, up_sem) = refs[:pieces], refs[pieces:]
+    copy = pltpu.make_async_copy(up_hbm, up_ref, up_sem)
+    copy.start()
+    copies = start_weights(blocks_ref, w_ref, w_buf, sems)
+    copy.wait()
+    finish_weights(copies, up_ref, w_buf, outs)
+
+
+def first_kernel(pieces, chunks, length, blocks_ref, held_ref, up_ref, w_ref, sig_ref, dec_ref, *refs):
     lents = pieces // 2 + 1
     lent_ref, *pairs = refs[:lents]
     end_ref, sent_ref, *tables = refs[lents:-4]
@@ -466,7 +623,8 @@
     for k, (low, high) in enumerate(chunks):
         signal_chunk(length, low, high, sig_ref, dec_ref, end_ref, *tables[3 * k : 3 * k + 3], ebuf, e1buf)
     sent_ref[...] = end_ref[...].astype(BF16)
-    finish_weights(copies, up_ref, w_buf, outs)
+    finish_weights([], up_ref, held_ref, outs[:1])
+    finish_weights(copies, up_ref, w_buf, outs[1:])
 
 
 def weight_scratch(pieces, width, feats):
@@ -475,23 +633,24 @@
 
 def project(up, weight, width, blocks):
     tokens, feats = up.shape
-    pieces = len(blocks)
+    pieces = blocks.shape[0]
     return pl.pallas_call(
         functools.partial(project_kernel, pieces),
         out_shape=[jax.ShapeDtypeStruct((tokens, width), BF16)] * pieces,
-        in_specs=[pl.BlockSpec(memory_space=pltpu.SMEM), VM, pl.BlockSpec(memory_space=pl.ANY)],
+        in_specs=[SM] + [pl.BlockSpec(memory_space=pl.ANY)] * 2,
         out_specs=[VM] * pieces,
-        scratch_shapes=weight_scratch(pieces, width, feats),
+        scratch_shapes=weight_scratch(pieces, width, feats)
+        + [pltpu.VMEM(up.shape, up.dtype), pltpu.SemaphoreType.DMA],
         compiler_params=params(PROJECT_LIMIT),
-        cost_estimate=SMALL,
+        cost_estimate=takes(4),
         name="project",
-    )(jnp.stack(blocks).astype(jnp.int32), up, weight)
-
-
-def project_and_scan(up, weight, width, blocks, signal, decays, chunks, length):
+    )(blocks, up, weight)
+
+
+def project_and_scan(up, weight, width, lead, rest, signal, decays, chunks, length):
     tokens, feats = up.shape
     modes = decays.shape[0]
-    pieces = len(blocks)
+    pieces = 1 + rest.shape[0]
     lents = pieces // 2 + 1
     shapes = [jax.ShapeDtypeStruct((tokens, lents * width), BF16)]
     shapes += [jax.ShapeDtypeStruct((tokens, width), BF16)] * (pieces - lents)
@@ -502,13 +661,14 @@
     out = pl.pallas_call(
         functools.partial(first_kernel, pieces, chunks, length),
         out_shape=shapes,
-        in_specs=[pl.BlockSpec(memory_space=pltpu.SMEM), VM, pl.BlockSpec(memory_space=pl.ANY), VM, VM],
+        in_specs=[SM, VM, VM, pl.BlockSpec(memory_space=pl.ANY), VM, VM],
         out_specs=[VM] * len(shapes),
-        scratch_shapes=weight_scratch(pieces, width, feats) + [pltpu.VMEM((modes * SUB, LANES), F32)] * 2,
+        scratch_shapes=weight_scratch(pieces - 1, width, feats)
+        + [pltpu.VMEM((modes * SUB, LANES), F32)] * 2,
         compiler_params=params(PROJECT_LIMIT),
-        cost_estimate=SMALL,
+        cost_estimate=takes(8),
         name="project_and_scan",
-    )(jnp.stack(blocks).astype(jnp.int32), up, weight, signal, decays)
+    )(rest, fetch(weight, width, lead), up, weight, signal, decays)
     start = 1 + pieces - lents
     tables = out[start + 2 :]
     return out[0], out[1:start], out[start : start + 2], [
@@ -562,41 +722,58 @@
     levels = [1 << k for k in range(groups.bit_length() - 1)]
 
     wanted = [me ^ hop ^ 1 for hop in hops] + [me ^ 1] + [me ^ hop for hop in hops]
+    rest = jnp.stack(wanted[1:]).astype(jnp.int32)
+    lead, mine = [jnp.reshape(b, (1,)).astype(jnp.int32) for b in (wanted[0], me)]
+    lead, rest, mine, place = lax.optimization_barrier((lead, rest, mine, place))
     lent, parts, (state, sent), tables = project_and_scan(
-        upstream, out_weight, width, wanted, signal, dec, chunks, length
+        upstream, out_weight, width, lead, rest, signal, dec, chunks, length
     )
     lent = send(lent, "ch", blocks, 1)
     pairs = [pair_sums(part, lent, index, chunks) for index, part in enumerate(parts)]
     upstream, pairs = lax.optimization_barrier((upstream, pairs))
     arrived = [[send(pair[k], "ch", blocks, hop) for pair, hop in zip(pairs, hops)] for k in range(len(chunks))]
-    (own,) = project(upstream, out_weight, width, [me])
-
-    before = []
+    (own,) = project(upstream, out_weight, width, mine)
+
+    before, pays, states, locs = [], [], [], []
+
+    def take(chunk, low, high, sigp, y, y1):
+        grad, z, own_state = gradient_states([own, lent, *chunk], len(hops), high - low, low, dec, length)
+        states.append(own_state)
+        pays.append(filter_sums(grad, sigp, dec, y, y1, length, low))
+        locs.append((grad, z, low))
+
     for hop in levels:
         if hop == levels[-1]:
-            sent, arrived = lax.optimization_barrier((sent, arrived))
+            sent, own = lax.optimization_barrier((sent, own))
+            pass
         there = send(sent, "ctx", groups, hop)
-        sent, state, *before = step_call(
-            functools.partial(prefix_kernel, length, tokens, hop), place, there, state, before, dec
-        )
-    pays, locs = [], []
-    for chunk, (low, high), (sigp, y, y1) in zip(arrived, chunks, tables):
-        grad, z, pay = gradient_states(
-            [own, lent, *chunk], len(hops), high - low, low, sigp, dec, y, y1, length
-        )
-        pays.append(pay)
-        locs.append((grad, z, low))
-    sent, state, later = gather_sums(pays, before[0], chunks)
+        if hop == 1:
+            there, pairs = lax.optimization_barrier((there, pairs))
+        if hop != levels[-1]:
+            sent, after, *rest = prefix_step(
+                place, there, state, before, dec, tokens, length, hop, hop * 2 != levels[-1]
+            )
+            state, before = (rest + [None])[0], [after]
+    ends = there
+    for k in range(len(pays), len(chunks)):
+        pays, arrived[k] = lax.optimization_barrier((pays, arrived[k]))
+        take(arrived[k], *chunks[k], *tables[k])
+    sent, state = join_states(states, chunks)
     locs = [local_part(grad, z, dec, res, gain, length, low) for grad, z, low in locs]
-    for hop in levels[:-1]:
+    there = send(sent, "ctx", groups, levels[0])
+    sent, state, later, sums = merge(
+        place, there, state, ends, pays, dec, before, chunks, tokens, length, levels[0], levels[-1]
+    )
+    for hop in levels[1:]:
         there = send(sent, "ctx", groups, hop)
-        sent, state, later = step_call(
-            functools.partial(suffix_kernel, length, tokens, hop), place, there, state, [later], dec
-        )
-    there = send(sent, "ctx", groups, levels[-1])
-    out, ores, odec, oskip = finish(
-        place, there, state, later, dec, res, locs, chunks, tokens, length, levels[-1]
-    )
+        if hop != levels[-1]:
+            sent, later, sums, *state = tail_step(
+                place, there, state, later, sums, dec, tokens, length, hop, hop * 2 != levels[-1]
+            )
+            state = state[0] if state else None
+    moved, sums = sum_step(there, sums)
+    out = finish(place, there, later, dec, res, locs, chunks, tokens, length, levels[-1])
+    ores, odec, oskip = results(send(moved, "ctx", groups, levels[0]), sums, res, length)
     return (out, ores.T, odec.T, oskip[0])
 
 

time: 63.5 us -> 52.7 us (0.83)
  waiting for transfers between devices: 18.5 us -> 6.29 us
  starting transfers between devices: 13.7 us -> 18.9 us
  local copies, waits for them, and re-layouts: 2.82 us -> 0.23 us
  Pallas kernels: 27.3 us -> 26.3 us
    ppermute x9 -> x10, waiting for transfers between devices: 18.5 us -> 6.29 us  [send(): return lax.ppermute(x, axis, [(i, i ^ hop) for i in range(size)])]
    ppermute x9 -> x10, starting transfers between devices: 13.7 us -> 18.9 us  [send(): return lax.ppermute(x, axis, [(i, i ^ hop) for i in range(size)])]
    pallas_call x6 -> x10, Pallas kernels: 1.83 us -> 6.95 us  [the longest x2 3.67 us: filter_sums(): pl.pallas_call(functools.partial(filter_kernel, length, base), out_shape=...]
    pallas_call x2, Pallas kernels: 6.33 us -> 2.15 us  [gradient_states(): pl.pallas_call(functools.partial(gradient_kernel, length, base, lent, len...]
    unnamed x20 -> x10, local copies, waits for them, and re-layouts: 2.82 us -> 0.23 us
    pallas_call x1, Pallas kernels: 9.46 us -> 8.23 us  [project_and_scan(): pl.pallas_call(functools.partial(first_kernel, pieces, chunks, length), o...]
    pallas_call x1, Pallas kernels: 0.87 us -> 0.12 us  [pair_sums(): pl.pallas_call(functools.partial(pair_kernel, chunks, index), out_shape=[...]
  transfers between devices with their start and end apart: 9 -> 10, of which waited for: 7 -> 4; matrix products, arithmetic and copies ran while one was open for 0% -> 0% of each run, Pallas kernels for 21% -> 28%
where the time goes in v3:
time: 52.7 us; the launch traced here: 52.6 us
  Pallas kernels  26.3 us (50%)
  starting transfers between devices  18.9 us (36%)
  waiting for transfers between devices  6.29 us (12%)
  between operations  0.79 us (1%)
    ppermute x10, starting transfers between devices, send(): return lax.ppermute(x, axis, [(i, i ^ hop) for i in range(size)])  18.9 us
    pallas_call x1, Pallas kernels, project_and_scan(): pl.pallas_call(functools.partial(first_kernel, pieces, chunks, length), o...  8.23 us
    ppermute x10, waiting for transfers between devices, send(): return lax.ppermute(x, axis, [(i, i ^ hop) for i in range(size)])  6.29 us
    pallas_call x2, Pallas kernels, filter_sums(): pl.pallas_call(functools.partial(filter_kernel, length, base), out_shape=...  3.67 us
    pallas_call x1, Pallas kernels, project(): pl.pallas_call(functools.partial(project_kernel, pieces), out_shape=[jax....  3.55 us
    pallas_call x1, Pallas kernels, finish(): pl.pallas_call(functools.partial(finish_kernel, length, hop, chunks), out...  2.84 us
    pallas_call x2, Pallas kernels, local_part(): pl.pallas_call(functools.partial(local_kernel, length, base), out_shape=j...  2.47 us
    pallas_call x1, Pallas kernels, fetch(): pl.pallas_call(fetch_kernel, out_shape=jax.ShapeDtypeStruct((width, weigh...  2.3 us
  transfers between devices with their start and end apart: 10, of which 4 were waited for; matrix products, arithmetic and copies ran while one was open for 0% of the time, Pallas kernels for 28%

profile of v3, /device:TPU:0, one launch (start us, length us, event | category | flops | bytes accessed | tf_op | source)
XLA Modules:
  0.0 52.6 jit_solution(3760306899469969193)
XLA Ops:
  0.6 0.0 copy-start.1
  0.6 0.0 copy-start
  0.7 0.0 copy-start.3
  0.7 0.1 pad_add_fusion.blocks_ref
  0.7 2.3 %fetch.1.held_ref = bf16[1024,2048]{1,0:T(8,128)(2,1)S(1)} custom-call(s32[1]{0:T(128)} %bitcast.block_ref, bf16[4096,2048]{1,0:T(8,128)(2,1)} %w_ref.5), custom_call_target="tpu_custom_call" | custom-call | flops 3000000000 | bytes 1 | tf_op jit(solution)/shard_map/fetch/pallas_call | solution.py:594
  3.1 0.1 copy-done.1
  3.1 0.0 copy-done
  3.1 0.1 copy-done.3
  3.3 8.2 %project_and_scan.1 = (bf16[256,2048]{1,0:T(8,128)(2,1)S(1)}, bf16[256,1024]{1,0:T(8,128)(2,1)S(1)}, f32[32,1024]{1,0:T(8,128)S(1)}, bf16[32,1024]{1,0:T(8,128)(...) custom-call(s32[2]{0:T(128)S(1)} %pad_add_fusion.blocks_ref, ...), custom_call_target="tpu_custom_call" | custom-call | flops 8000000000 | bytes 1 | tf_op jit(solution)/shard_map/project_and_scan/pallas_call | solution.py:661
  11.5 0.5 collective-permute-start.1
  12.0 2.6 %collective-permute-start = (bf16[32,1024]{1,0:T(8,128)(2,1)S(1)}, bf16[32,1024]{1,0:T(8,128)(2,1)S(1)}, u32[]{:S(2)}, u32[]{:S(2)}) collective-permute-start(bf16[32,1024]{1,0:T(8,128)(2,1)S(1)} %get-tuple-element.56), channel_id=1, source_target_pairs={{0,4},{4,0},{8,12},{12,8},{16,20},{20,16},{24,28},{28,24},{1,5},{5... | collective-permute-start | bytes 196616 | tf_op jit(solution)/shard_map/ppermute | solution.py:700
  14.6 0.0 collective-permute-done.1.lent_ref.refs_1_
  14.6 0.1 pair_sums.1
  14.7 2.7 %collective-permute-start.3 = (bf16[256,512]{1,0:T(8,128)(2,1)S(1)}, bf16[256,512]{1,0:T(8,128)(2,1)S(1)}, u32[]{:S(2)}, u32[]{:S(2)}) collective-permute-start(bf16[256,512]{1,0:T(8,128)(2,1)S(1)} %get-tuple-element.61), channel_id=1, source_target_pairs={{0,2},{1,3},{2,0},{3,1},{4,6},{5,7},{6,4},{7,5},{8,10},{9,11},{10,... | collective-permute-start | bytes 786440 | tf_op jit(solution)/shard_map/ppermute | solution.py:700
  17.4 0.1 collective-permute-start.4
  17.5 0.0 collective-permute-done.there_ref
  17.5 0.1 prefix_step.2
  17.5 2.1 %collective-permute-start.2 = (bf16[32,1024]{1,0:T(8,128)(2,1)S(1)}, bf16[32,1024]{1,0:T(8,128)(2,1)S(1)}, u32[]{:S(2)}, u32[]{:S(2)}) collective-permute-start(bf16[32,1024]{1,0:T(8,128)(2,1)S(1)} %get-tuple-element.65), channel_id=1, source_target_pairs={{0,8},{4,12},{8,0},{12,4},{16,24},{20,28},{24,16},{28,20},{1,9},{5... | collective-permute-start | bytes 196616 | tf_op jit(solution)/shard_map/ppermute | solution.py:700
  19.6 3.6 %project.1.refs_0_ = bf16[256,1024]{1,0:T(8,128)(2,1)S(1)} custom-call(s32[1]{0:T(128)} %bitcast.3.blocks_ref, bf16[256,2048]{1,0:T(8,128)(2,1)S(1)} %copy-done.1, bf16[4096,2048]{1,0:T(8,128)(2,1)} %w_ref.5), custom_call_target="tpu_custom_call" | custom-call | flops 4000000000 | bytes 1 | tf_op jit(solution)/shard_map/project/pallas_call | solution.py:637
  23.2 0.0 copy-start.2
  23.2 0.0 copy-start.4
  23.2 0.0 collective-permute-done.2.there_ref
  23.2 0.1 prefix_step.3
  23.3 2.6 %collective-permute-start.6 = (bf16[32,1024]{1,0:T(8,128)(2,1)S(1)}, bf16[32,1024]{1,0:T(8,128)(2,1)S(1)}, u32[]{:S(2)}, u32[]{:S(2)}) collective-permute-start(bf16[32,1024]{1,0:T(8,128)(2,1)S(1)} %get-tuple-element.81), channel_id=1, source_target_pairs={{0,16},{4,20},{8,24},{12,28},{16,0},{20,4},{24,8},{28,12},{1,17},{... | collective-permute-start | bytes 196616 | tf_op jit(solution)/shard_map/ppermute | solution.py:700
  25.9 0.0 collective-permute-done.3.refs_2_
  25.9 1.1 %gradient_states.2 = (f32[256,512]{1,0:T(8,128)S(1)}, f32[4,256,128]{2,1,0:T(8,128)S(1)}, f32[16,512]{1,0:T(8,128)S(1)}) custom-call(bf16[256,1024]{1,0:T(8,128)(2,1)S(1)} %project.1.refs_0_, bf16[256,2048]{1,0:T(8,128)(2,1)S(1)} %collective-permute-done.1.lent_ref.refs_1_, bf16[256,512]{1,0:T(8,128)(2,1)S(1)} %collective-permute-done.3.refs_2_, ...), custom_call_target="tpu_custom_call" | custom-call | flops 1000000000 | bytes 1 | tf_op jit(solution)/shard_map/gradient_states/pallas_call | solution.py:162
  27.0 1.8 %filter_sums.2.refs_0_ = f32[64,512]{1,0:T(8,128)S(1)} custom-call(f32[256,512]{1,0:T(8,128)S(1)} %get-tuple-element.73.grad_ref, bf16[256,512]{1,0:T(8,128)(2,1)S(1)} %get-tuple-element.74.sigp_ref, f32[16,1024]{1,0:T(8,128)S(1)} %bitcast.15, bf16[256,512]{1,0:T(8,128)(2,1)S(1)} %get-tuple-element.75.y_ref, bf16[256,512]{1,0:T(8,128)(2,1)S(1)} %get-tuple-element.76.y1_ref), custom_call_target="tpu_custom_call" | custom-call | flops 3000000000 | bytes 1 | tf_op jit(solution)/shard_map/filter_sums/pallas_call | solution.py:234
  28.9 0.8 %collective-permute-done.4.refs_2_ = bf16[256,512]{1,0:T(8,128)(2,1)S(1)} collective-permute-done((bf16[256,512]{1,0:T(8,128)(2,1)S(1)}, bf16[256,512]{1,0:T(8,128)(2,1)S(1)}, u32[]{:S(2)}, u32[]{:S(2)}) %collective-permute-start.4) | collective-permute-done | bytes 262176 | tf_op jit(solution)/shard_map/ppermute | solution.py:700
  29.6 1.1 %gradient_states.3 = (f32[256,512]{1,0:T(8,128)S(1)}, f32[4,256,128]{2,1,0:T(8,128)S(1)}, f32[16,512]{1,0:T(8,128)S(1)}) custom-call(bf16[256,1024]{1,0:T(8,128)(2,1)S(1)} %project.1.refs_0_, bf16[256,2048]{1,0:T(8,128)(2,1)S(1)} %collective-permute-done.1.lent_ref.refs_1_, bf16[256,512]{1,0:T(8,128)(2,1)S(1)} %collective-permute-done.4.refs_2_, ...), custom_call_target="tpu_custom_call" | custom-call | flops 1000000000 | bytes 1 | tf_op jit(solution)/shard_map/gradient_states/pallas_call | solution.py:162
  30.7 1.8 %collective-permute-start.5 = (bf16[16,1024]{1,0:T(8,128)(2,1)S(1)}, bf16[16,1024]{1,0:T(8,128)(2,1)S(1)}, u32[]{:S(2)}, u32[]{:S(2)}) collective-permute-start(bf16[16,1024]{1,0:T(8,128)(2,1)S(1)} %get-tuple-element.79), channel_id=1, source_target_pairs={{0,4},{4,0},{8,12},{12,8},{16,20},{20,16},{24,28},{28,24},{1,5},{5... | collective-permute-start | bytes 98312 | tf_op jit(solution)/shard_map/ppermute | solution.py:700
  32.5 1.8 %filter_sums.3.refs_1_ = f32[64,512]{1,0:T(8,128)S(1)} custom-call(f32[256,512]{1,0:T(8,128)S(1)} %get-tuple-element.83.grad_ref, bf16[256,512]{1,0:T(8,128)(2,1)S(1)} %get-tuple-element.84.sigp_ref, f32[16,1024]{1,0:T(8,128)S(1)} %bitcast.17, bf16[256,512]{1,0:T(8,128)(2,1)S(1)} %get-tuple-element.85.y_ref, bf16[256,512]{1,0:T(8,128)(2,1)S(1)} %get-tuple-element.86.y1_ref), custom_call_target="tpu_custom_call" | custom-call | flops 3000000000 | bytes 1 | tf_op jit(solution)/shard_map/filter_sums/pallas_call | solution.py:234
  34.3 0.0 collective-permute-done.6.ends_ref
  34.3 0.4 collective-permute-done.5.there_ref
  34.7 0.1 merge.1
  34.8 1.9 %collective-permute-start.7 = (bf16[64,1024]{1,0:T(8,128)(2,1)S(1)}, bf16[64,1024]{1,0:T(8,128)(2,1)S(1)}, u32[]{:S(2)}, u32[]{:S(2)}) collective-permute-start(bf16[64,1024]{1,0:T(8,128)(2,1)S(1)} %get-tuple-element.88), channel_id=1, source_target_pairs={{0,8},{4,12},{8,0},{12,4},{16,24},{20,28},{24,16},{28,20},{1,9},{5... | collective-permute-start | bytes 393224 | tf_op jit(solution)/shard_map/ppermute | solution.py:700
  36.6 0.0 copy-done.2
  36.6 0.0 copy-done.4
  36.6 1.2 %local_part.3.refs_1_ = f32[256,512]{1,0:T(8,128)S(1)} custom-call(f32[256,512]{1,0:T(8,128)S(1)} %get-tuple-element.83.grad_ref, f32[4,256,128]{2,1,0:T(8,128)S(1)} %get-tuple-element.95.z_ref, f32[16,1024]{1,0:T(8,128)S(1)} %bitcast.19, f32[16,1024]{1,0:T(8,128)S(1)} %bitcast.23, f32[1,1024]{1,0:T(1,128)S(1)} %bitcast.27), custom_call_target="tpu_custom_call" | custom-call | flops 1500000000 | bytes 1 | tf_op jit(solution)/shard_map/local_part/pallas_call | solution.py:294
  37.9 1.9 %collective-permute-done.7.there_ref = bf16[64,1024]{1,0:T(8,128)(2,1)S(1)} collective-permute-done((bf16[64,1024]{1,0:T(8,128)(2,1)S(1)}, bf16[64,1024]{1,0:T(8,128)(2,1)S(1)}, u32[]{:S(2)}, u32[]{:S(2)}) %collective-permute-start.7) | collective-permute-done | bytes 131104 | tf_op jit(solution)/shard_map/ppermute | solution.py:700
  39.8 0.1 tail_step.1
  39.9 2.9 %collective-permute-start.8 = (bf16[64,1024]{1,0:T(8,128)(2,1)S(1)}, bf16[64,1024]{1,0:T(8,128)(2,1)S(1)}, u32[]{:S(2)}, u32[]{:S(2)}) collective-permute-start(bf16[64,1024]{1,0:T(8,128)(2,1)S(1)} %get-tuple-element.92), channel_id=1, source_target_pairs={{0,16},{4,20},{8,24},{12,28},{16,0},{20,4},{24,8},{28,12},{1,17},{... | collective-permute-start | bytes 393224 | tf_op jit(solution)/shard_map/ppermute | solution.py:700
  42.8 1.2 %local_part.2.refs_0_ = f32[256,512]{1,0:T(8,128)S(1)} custom-call(f32[256,512]{1,0:T(8,128)S(1)} %get-tuple-element.73.grad_ref, f32[4,256,128]{2,1,0:T(8,128)S(1)} %get-tuple-element.94.z_ref, f32[16,1024]{1,0:T(8,128)S(1)} %bitcast.21, f32[16,1024]{1,0:T(8,128)S(1)} %bitcast.24, f32[1,1024]{1,0:T(1,128)S(1)} %bitcast.28), custom_call_target="tpu_custom_call" | custom-call | flops 1500000000 | bytes 1 | tf_op jit(solution)/shard_map/local_part/pallas_call | solution.py:294
  44.0 3.2 %collective-permute-done.8.there_ref = bf16[64,1024]{1,0:T(8,128)(2,1)S(1)} collective-permute-done((bf16[64,1024]{1,0:T(8,128)(2,1)S(1)}, bf16[64,1024]{1,0:T(8,128)(2,1)S(1)}, u32[]{:S(2)}, u32[]{:S(2)}) %collective-permute-start.8) | collective-permute-done | bytes 131104 | tf_op jit(solution)/shard_map/ppermute | solution.py:700
  47.2 1.8 %collective-permute-start.9 = (bf16[48,1024]{1,0:T(8,128)(2,1)S(1)}, bf16[48,1024]{1,0:T(8,128)(2,1)S(1)}, u32[]{:S(2)}, u32[]{:S(2)}) collective-permute-start(bf16[48,1024]{1,0:T(8,128)(2,1)S(1)} %get-tuple-element.97), channel_id=1, source_target_pairs={{0,4},{4,0},{8,12},{12,8},{16,20},{20,16},{24,28},{28,24},{1,5},{5... | collective-permute-start | bytes 294920 | tf_op jit(solution)/shard_map/ppermute | solution.py:700
  49.1 2.8 %finish.1 = bf16[256,1024]{1,0:T(8,128)(2,1)} custom-call(s32[1]{0:T(128)} %bitcast.4.me_ref, bf16[64,1024]{1,0:T(8,128)(2,1)S(1)} %collective-permute-done.8.there_ref, f32[16,1024]{1,0:T(8,128)S(1)} %get-tuple-element.93.later_ref, f32[16,1024]{1,0:T(8,128)S(1)} %bitcast.22, f32[16,1024]{1,0:T(8,128)S(1)} %bitcast.25, f32[256,512]{1,0:T(8,128)S(1)} %local_part.2.refs_0_, ...), custom_call_target="tpu_custom_call" | custom-call | flops 3000000000 | bytes 1 | tf_op jit(solution)/shard_map/finish/pallas_call | solution.py:348
  51.9 0.0 collective-permute-done.9.there_ref
  51.9 0.7 %results.1 = (f32[16,1024]{1,0:T(8,128)}, f32[16,1024]{1,0:T(8,128)}, f32[1,1024]{1,0:T(1,128)}) custom-call(bf16[48,1024]{1,0:T(8,128)(2,1)S(1)} %collective-permute-done.9.there_ref, f32[48,1024]{1,0:T(8,128)S(1)} %get-tuple-element.98.sums_ref, f32[16,1024]{1,0:T(8,128)S(1)} %bitcast.26), custom_call_target="tpu_custom_call" | custom-call | flops 1 | bytes 1 | tf_op jit(solution)/shard_map/results/pallas_call | solution.py:512
  (2 shorter events, 0.0 us)
Async XLA Ops:
  0.6 2.5 %copy-start.1 = (bf16[256,2048]{1,0:T(8,128)(2,1)S(1)}, bf16[256,2048]{1,0:T(8,128)(2,1)}, u32[]{:S(2)}) copy-start(bf16[256,2048]{1,0:T(8,128)(2,1)} %up_hbm) | copy-start | bytes 3145732
  0.6 2.5 %copy-start = (f32[1024,16]{0,1:T(8,128)S(1)}, f32[1024,16]{0,1:T(8,128)}, u32[]{:S(2)}) copy-start(f32[1024,16]{0,1:T(8,128)} %param.10) | copy-start | bytes 196612
  0.7 2.6 %copy-start.3 = (bf16[256,1024]{1,0:T(8,128)(2,1)S(1)}, bf16[256,1024]{1,0:T(8,128)(2,1)}, u32[]{:S(2)}) copy-start(bf16[256,1024]{1,0:T(8,128)(2,1)} %sig_ref.1) | copy-start | bytes 1572868
  11.5 3.1 %collective-permute-start.1 = (bf16[256,2048]{1,0:T(8,128)(2,1)S(1)}, bf16[256,2048]{1,0:T(8,128)(2,1)S(1)}, u32[]{:S(2)}, u32[]{:S(2)}) collective-permute-start(bf16[256,2048]{1,0:T(8,128)(2,1)S(1)} %get-tuple-element.58), channel_id=1, source_target_pairs={{0,1},{1,0},{2,3},{3,2},{4,5},{5,4},{6,7},{7,6},{8,9},{9,8},{10,11... | collective-permute-start | bytes 3145736 | tf_op jit(solution)/shard_map/ppermute | solution.py:700
  12.0 5.5 %collective-permute-start = (bf16[32,1024]{1,0:T(8,128)(2,1)S(1)}, bf16[32,1024]{1,0:T(8,128)(2,1)S(1)}, u32[]{:S(2)}, u32[]{:S(2)}) collective-permute-start(bf16[32,1024]{1,0:T(8,128)(2,1)S(1)} %get-tuple-element.56), channel_id=1, source_target_pairs={{0,4},{4,0},{8,12},{12,8},{16,20},{20,16},{24,28},{28,24},{1,5},{5... | collective-permute-start | bytes 196616 | tf_op jit(solution)/shard_map/ppermute | solution.py:700
  14.7 11.2 %collective-permute-start.3 = (bf16[256,512]{1,0:T(8,128)(2,1)S(1)}, bf16[256,512]{1,0:T(8,128)(2,1)S(1)}, u32[]{:S(2)}, u32[]{:S(2)}) collective-permute-start(bf16[256,512]{1,0:T(8,128)(2,1)S(1)} %get-tuple-element.61), channel_id=1, source_target_pairs={{0,2},{1,3},{2,0},{3,1},{4,6},{5,7},{6,4},{7,5},{8,10},{9,11},{10,... | collective-permute-start | bytes 786440 | tf_op jit(solution)/shard_map/ppermute | solution.py:700
  17.4 12.2 %collective-permute-start.4 = (bf16[256,512]{1,0:T(8,128)(2,1)S(1)}, bf16[256,512]{1,0:T(8,128)(2,1)S(1)}, u32[]{:S(2)}, u32[]{:S(2)}) collective-permute-start(bf16[256,512]{1,0:T(8,128)(2,1)S(1)} %get-tuple-element.62), channel_id=1, source_target_pairs={{0,2},{1,3},{2,0},{3,1},{4,6},{5,7},{6,4},{7,5},{8,10},{9,11},{10,... | collective-permute-start | bytes 786440 | tf_op jit(solution)/shard_map/ppermute | solution.py:700
  17.5 5.6 %collective-permute-start.2 = (bf16[32,1024]{1,0:T(8,128)(2,1)S(1)}, bf16[32,1024]{1,0:T(8,128)(2,1)S(1)}, u32[]{:S(2)}, u32[]{:S(2)}) collective-permute-start(bf16[32,1024]{1,0:T(8,128)(2,1)S(1)} %get-tuple-element.65), channel_id=1, source_target_pairs={{0,8},{4,12},{8,0},{12,4},{16,24},{20,28},{24,16},{28,20},{1,9},{5... | collective-permute-start | bytes 196616 | tf_op jit(solution)/shard_map/ppermute | solution.py:700
  23.2 13.5 %copy-start.2 = (f32[1024,16]{0,1:T(8,128)S(1)}, f32[1024,16]{0,1:T(8,128)}, u32[]{:S(2)}) copy-start(f32[1024,16]{0,1:T(8,128)} %param.9) | copy-start | bytes 196612
  23.2 13.5 %copy-start.4 = (f32[1024]{0:T(1024)S(1)}, f32[1024]{0:T(1024)}, u32[]{:S(2)}) copy-start(f32[1024]{0:T(1024)} %param.11) | copy-start | bytes 12292
  23.3 11.0 %collective-permute-start.6 = (bf16[32,1024]{1,0:T(8,128)(2,1)S(1)}, bf16[32,1024]{1,0:T(8,128)(2,1)S(1)}, u32[]{:S(2)}, u32[]{:S(2)}) collective-permute-start(bf16[32,1024]{1,0:T(8,128)(2,1)S(1)} %get-tuple-element.81), channel_id=1, source_target_pairs={{0,16},{4,20},{8,24},{12,28},{16,0},{20,4},{24,8},{28,12},{1,17},{... | collective-permute-start | bytes 196616 | tf_op jit(solution)/shard_map/ppermute | solution.py:700
  30.7 4.0 %collective-permute-start.5 = (bf16[16,1024]{1,0:T(8,128)(2,1)S(1)}, bf16[16,1024]{1,0:T(8,128)(2,1)S(1)}, u32[]{:S(2)}, u32[]{:S(2)}) collective-permute-start(bf16[16,1024]{1,0:T(8,128)(2,1)S(1)} %get-tuple-element.79), channel_id=1, source_target_pairs={{0,4},{4,0},{8,12},{12,8},{16,20},{20,16},{24,28},{28,24},{1,5},{5... | collective-permute-start | bytes 98312 | tf_op jit(solution)/shard_map/ppermute | solution.py:700
  34.8 5.0 %collective-permute-start.7 = (bf16[64,1024]{1,0:T(8,128)(2,1)S(1)}, bf16[64,1024]{1,0:T(8,128)(2,1)S(1)}, u32[]{:S(2)}, u32[]{:S(2)}) collective-permute-start(bf16[64,1024]{1,0:T(8,128)(2,1)S(1)} %get-tuple-element.88), channel_id=1, source_target_pairs={{0,8},{4,12},{8,0},{12,4},{16,24},{20,28},{24,16},{28,20},{1,9},{5... | collective-permute-start | bytes 393224 | tf_op jit(solution)/shard_map/ppermute | solution.py:700
  39.9 7.3 %collective-permute-start.8 = (bf16[64,1024]{1,0:T(8,128)(2,1)S(1)}, bf16[64,1024]{1,0:T(8,128)(2,1)S(1)}, u32[]{:S(2)}, u32[]{:S(2)}) collective-permute-start(bf16[64,1024]{1,0:T(8,128)(2,1)S(1)} %get-tuple-element.92), channel_id=1, source_target_pairs={{0,16},{4,20},{8,24},{12,28},{16,0},{20,4},{24,8},{28,12},{1,17},{... | collective-permute-start | bytes 393224 | tf_op jit(solution)/shard_map/ppermute | solution.py:700
  47.2 4.7 %collective-permute-start.9 = (bf16[48,1024]{1,0:T(8,128)(2,1)S(1)}, bf16[48,1024]{1,0:T(8,128)(2,1)S(1)}, u32[]{:S(2)}, u32[]{:S(2)}) collective-permute-start(bf16[48,1024]{1,0:T(8,128)(2,1)S(1)} %get-tuple-element.97), channel_id=1, source_target_pairs={{0,4},{4,0},{8,12},{12,8},{16,20},{20,16},{24,28},{28,24},{1,5},{5... | collective-permute-start | bytes 294920 | tf_op jit(solution)/shard_map/ppermute | solution.py:700

commit v4 on v3

--- a/solution.py
+++ b/solution.py
@@ -17,19 +17,21 @@
 PROJECT_LIMIT = 43 * 1024 * 1024
 VM = pl.BlockSpec(memory_space=pltpu.VMEM)
 SM = pl.BlockSpec(memory_space=pltpu.SMEM)
+HBM = pl.BlockSpec(memory_space=pl.ANY)
 
 
 def interleave(tokens, transpose=False):
     steps = tokens // SUB
     row = lax.broadcasted_iota(jnp.int32, (tokens, tokens), 1 if transpose else 0)
     col = lax.broadcasted_iota(jnp.int32, (tokens, tokens), 0 if transpose else 1)
-    return jnp.where(col == (row % SUB) * steps + row // SUB, 1.0, 0.0).astype(BF16)
+    source = (row & (SUB - 1)) * steps + lax.shift_right_logical(row, SUB.bit_length() - 1)
+    return jnp.where(col == source, 1.0, 0.0).astype(BF16)
 
 
 def group_sums(groups, size):
     col = lax.broadcasted_iota(jnp.int32, (groups, groups * size), 1)
     row = lax.broadcasted_iota(jnp.int32, (groups, groups * size), 0)
-    return jnp.where(col // size == row, 1.0, 0.0).astype(F32)
+    return jnp.where(lax.shift_right_logical(col, size.bit_length() - 1) == row, 1.0, 0.0).astype(F32)
 
 
 def params(limit=VMEM_LIMIT):
@@ -118,16 +120,15 @@
         end_ref[modes : 2 * modes, there] = carry1
 
 
-def gradient_kernel(length, base, lent, parts, *refs):
+def gradient_kernel(length, base, parts, *refs):
     own_ref, lent_ref, *got_refs = refs[: 1 + parts]
     dec_ref, grad_ref, z_ref, state_ref, sbuf = refs[1 + parts :]
     tokens, width = grad_ref.shape
     modes = dec_ref.shape[0]
     steps = tokens // SUB
-    first_lent = own_ref.shape[1] * lent + base
     place = lax.broadcasted_iota(jnp.int32, (HALF, LANES), 0).astype(F32) * steps
     total = own_ref[:, base : base + width].astype(F32)
-    total = total + lent_ref[:, first_lent : first_lent + width].astype(F32)
+    total = total + lent_ref[:, base : base + width].astype(F32)
     for got in got_refs:
         total = total + got[...].astype(F32)
     grad_ref[...] = jnp.dot(
@@ -156,11 +157,11 @@
     state_ref[...] = jnp.dot(group_sums(modes, HALF), sbuf[...], preferred_element_type=F32)
 
 
-def gradient_states(pieces, lent, width, base, decays, length):
+def gradient_states(pieces, width, base, decays, length):
     tokens = pieces[0].shape[0]
     modes = decays.shape[0]
     return pl.pallas_call(
-        functools.partial(gradient_kernel, length, base, lent, len(pieces) - 1),
+        functools.partial(gradient_kernel, length, base, len(pieces) - 1),
         out_shape=(
             jax.ShapeDtypeStruct((tokens, width), F32),
             jax.ShapeDtypeStruct((width // LANES, modes * SUB, LANES), F32),
@@ -223,8 +224,9 @@
         res = res + term
         dec = dec + lag * term
         weight = weight * pole
-    for k, rows in enumerate((res, dec, first, jnp.broadcast_to(lags[0:1], (modes, width)))):
+    for k, rows in enumerate((res, dec, first)):
         pay_ref[k * modes : (k + 1) * modes, :] = rows
+    pay_ref[3 * modes :, :] = jnp.broadcast_to(lags[0:1], (8, width))
 
 
 def filter_sums(grad, sigp, decays, y, y1, length, base):
@@ -233,7 +235,7 @@
     buf = pltpu.VMEM((modes * HALF, width), F32)
     return pl.pallas_call(
         functools.partial(filter_kernel, length, base),
-        out_shape=jax.ShapeDtypeStruct((4 * modes, width), F32),
+        out_shape=jax.ShapeDtypeStruct((3 * modes + 8, width), F32),
         in_specs=[VM] * 5,
         out_specs=VM,
         scratch_shapes=[buf] * 3 + [pltpu.VMEM((tokens // SUB * HALF, width), F32)],
@@ -424,14 +426,16 @@
     next_ref[...] = state
     sent_ref[0:modes, :] = state.astype(BF16)
     for pay_ref, (low, high) in zip(pays, chunks):
-        res, dec, first, skip = [pay_ref[k * modes : (k + 1) * modes, :] for k in range(4)]
+        res, dec, first = [pay_ref[k * modes : (k + 1) * modes, :] for k in range(3)]
+        skip = pay_ref[3 * modes :, :]
         before, before1 = all_before[:, low:high], all_before1[:, low:high]
         start = state_ref[:, low:high]
         res = res + start * before
         dec = dec + first * before + start * before1
-        for k, value in enumerate((res, dec, skip)):
-            sums_ref[k * modes : (k + 1) * modes, low:high] = value
-            sent_ref[(k + 1) * modes : (k + 2) * modes, low:high] = value.astype(BF16)
+        for at, value in ((0, res), (modes, dec), (2 * modes, skip)):
+            end = at + value.shape[0]
+            sums_ref[at:end, low:high] = value
+            sent_ref[modes + at : modes + end, low:high] = value.astype(BF16)
 
 
 def merge(me, there, state, ends, pays, decays, before, chunks, tokens, length, hop, last):
@@ -440,8 +444,8 @@
     return pl.pallas_call(
         functools.partial(merge_kernel, length, tokens, hop, last, chunks),
         out_shape=tuple(
-            jax.ShapeDtypeStruct((k * modes, width), dtype)
-            for k, dtype in ((4, BF16), (1, F32), (1, F32), (3, F32))
+            jax.ShapeDtypeStruct((rows, width), dtype)
+            for rows, dtype in ((3 * modes + 8, BF16), (modes, F32), (modes, F32), (2 * modes + 8, F32))
         ),
         in_specs=[SM] + [VM] * len(args),
         out_specs=(VM,) * 4,
@@ -558,122 +562,129 @@
     )(*states)
 
 
-def start_weights(blocks_ref, w_ref, w_buf, sems):
-    width = w_buf.shape[1]
+def weight_copies(blocks_ref, w_ref, width, targets, sems):
     copies = []
-    for q in range(w_buf.shape[0]):
+    for q, target in enumerate(targets):
         start = pl.multiple_of(blocks_ref[q] * width, width)
-        copies.append(pltpu.make_async_copy(w_ref.at[pl.ds(start, width)], w_buf.at[q], sems.at[q]))
-        copies[-1].start()
+        copies.append(pltpu.make_async_copy(w_ref.at[pl.ds(start, width)], target, sems.at[q]))
     return copies
 
 
-def finish_weights(copies, up_ref, w_buf, outs):
-    width = w_buf.shape[-2]
+def project_block(up_ref, w_rows, out_ref):
+    width = w_rows.shape[0]
+    rows = min(width, 256)
+    for start in range(0, width, rows):
+        out_ref[:, start : start + rows] = lax.dot_general(
+            up_ref[...], w_rows[start : start + rows, :], (((1,), (1,)), ((), ())),
+            preferred_element_type=F32,
+        ).astype(out_ref.dtype)
+
+
+def fetch_kernel(blocks_ref, w_ref, o_ref, sems):
+    pieces = blocks_ref.shape[0]
+    width = o_ref.shape[0] // pieces
+    targets = [o_ref.at[q * width : (q + 1) * width, :] for q in range(pieces)]
+    copies = weight_copies(blocks_ref, w_ref, width, targets, sems)
+    for copy in copies:
+        copy.start()
     for copy in copies:
         copy.wait()
-    rows = min(width, 256)
-    for q, out in enumerate(outs):
-        block = w_buf.at[q] if len(w_buf.shape) == 3 else w_buf
-        for start in range(0, width, rows):
-            out[:, start : start + rows] = lax.dot_general(
-                up_ref[...], block[start : start + rows, :], (((1,), (1,)), ((), ())),
-                preferred_element_type=F32,
-            ).astype(out.dtype)
-
-
-def fetch_kernel(block_ref, w_ref, o_ref, sem):
-    width = o_ref.shape[0]
-    start = pl.multiple_of(block_ref[0] * width, width)
-    copy = pltpu.make_async_copy(w_ref.at[pl.ds(start, width)], o_ref, sem)
-    copy.start()
-    copy.wait()
-
-
-def fetch(weight, width, block):
+
+
+def fetch(weight, width, blocks):
+    pieces = blocks.shape[0]
     return pl.pallas_call(
         fetch_kernel,
-        out_shape=jax.ShapeDtypeStruct((width, weight.shape[1]), BF16),
-        in_specs=[SM, pl.BlockSpec(memory_space=pl.ANY)],
+        out_shape=jax.ShapeDtypeStruct((pieces * width, weight.shape[1]), BF16),
+        in_specs=[SM, HBM],
         out_specs=VM,
-        scratch_shapes=[pltpu.SemaphoreType.DMA],
+        scratch_shapes=[pltpu.SemaphoreType.DMA((pieces,))],
         compiler_params=params(PROJECT_LIMIT),
         cost_estimate=takes(3),
         name="fetch",
-    )(block, weight)
-
-
-def project_kernel(pieces, blocks_ref, up_hbm, w_ref, *refs):
-    outs, (w_buf, sems, up_ref, up_sem) = refs[:pieces], refs[pieces:]
-    copy = pltpu.make_async_copy(up_hbm, up_ref, up_sem)
-    copy.start()
-    copies = start_weights(blocks_ref, w_ref, w_buf, sems)
-    copy.wait()
-    finish_weights(copies, up_ref, w_buf, outs)
-
-
-def first_kernel(pieces, chunks, length, blocks_ref, held_ref, up_ref, w_ref, sig_ref, dec_ref, *refs):
-    lents = pieces // 2 + 1
-    lent_ref, *pairs = refs[:lents]
-    end_ref, sent_ref, *tables = refs[lents:-4]
+    )(blocks, weight)
+
+
+def multiply_kernel(up_ref, held_ref, o_ref):
+    project_block(up_ref, held_ref, o_ref)
+
+
+def multiply(up, held):
+    return pl.pallas_call(
+        multiply_kernel,
+        out_shape=jax.ShapeDtypeStruct((up.shape[0], held.shape[0]), BF16),
+        in_specs=[VM] * 2,
+        out_specs=VM,
+        compiler_params=params(),
+        cost_estimate=takes(1),
+        name="multiply",
+    )(up, held)
+
+
+def scan_kernel(pieces, chunks, length, blocks_ref, up_ref, w_ref, sig_ref, dec_ref, *refs):
+    outs, (end_ref, sent_ref, *tables) = refs[:pieces], refs[pieces:-4]
     w_buf, sems, ebuf, e1buf = refs[-4:]
     width = w_buf.shape[1]
-    outs = [lent_ref.at[:, k * width : (k + 1) * width] for k in range(lents)] + pairs
-    copies = start_weights(blocks_ref, w_ref, w_buf, sems)
+    copies = weight_copies(blocks_ref, w_ref, width, [w_buf.at[q] for q in range(pieces)], sems)
+    for copy in copies:
+        copy.start()
     for k, (low, high) in enumerate(chunks):
         signal_chunk(length, low, high, sig_ref, dec_ref, end_ref, *tables[3 * k : 3 * k + 3], ebuf, e1buf)
     sent_ref[...] = end_ref[...].astype(BF16)
-    finish_weights([], up_ref, held_ref, outs[:1])
-    finish_weights(copies, up_ref, w_buf, outs[1:])
-
-
-def weight_scratch(pieces, width, feats):
-    return [pltpu.VMEM((pieces, width, feats), BF16), pltpu.SemaphoreType.DMA((pieces,))]
-
-
-def project(up, weight, width, blocks):
-    tokens, feats = up.shape
-    pieces = blocks.shape[0]
-    return pl.pallas_call(
-        functools.partial(project_kernel, pieces),
-        out_shape=[jax.ShapeDtypeStruct((tokens, width), BF16)] * pieces,
-        in_specs=[SM] + [pl.BlockSpec(memory_space=pl.ANY)] * 2,
-        out_specs=[VM] * pieces,
-        scratch_shapes=weight_scratch(pieces, width, feats)
-        + [pltpu.VMEM(up.shape, up.dtype), pltpu.SemaphoreType.DMA],
-        compiler_params=params(PROJECT_LIMIT),
-        cost_estimate=takes(4),
-        name="project",
-    )(blocks, up, weight)
-
-
-def project_and_scan(up, weight, width, lead, rest, signal, decays, chunks, length):
+    for copy in copies:
+        copy.wait()
+    for q, out in enumerate(outs):
+        project_block(up_ref, w_buf.at[q], out)
+
+
+def project_and_scan(up, weight, width, blocks, signal, decays, chunks, length):
     tokens, feats = up.shape
     modes = decays.shape[0]
-    pieces = 1 + rest.shape[0]
-    lents = pieces // 2 + 1
-    shapes = [jax.ShapeDtypeStruct((tokens, lents * width), BF16)]
-    shapes += [jax.ShapeDtypeStruct((tokens, width), BF16)] * (pieces - lents)
+    pieces = blocks.shape[0]
+    shapes = [jax.ShapeDtypeStruct((tokens, width), BF16)] * pieces
     shapes += [jax.ShapeDtypeStruct((2 * modes, width), dtype) for dtype in (F32, BF16)]
     for low, high in chunks:
         states = jax.ShapeDtypeStruct((modes * SUB, high - low), BF16)
         shapes += [jax.ShapeDtypeStruct((tokens, high - low), BF16), states, states]
     out = pl.pallas_call(
-        functools.partial(first_kernel, pieces, chunks, length),
+        functools.partial(scan_kernel, pieces, chunks, length),
         out_shape=shapes,
-        in_specs=[SM, VM, VM, pl.BlockSpec(memory_space=pl.ANY), VM, VM],
+        in_specs=[SM, VM, HBM, VM, VM],
         out_specs=[VM] * len(shapes),
-        scratch_shapes=weight_scratch(pieces - 1, width, feats)
+        scratch_shapes=[
+            pltpu.VMEM((pieces, width, feats), BF16),
+            pltpu.SemaphoreType.DMA((pieces,)),
+        ]
         + [pltpu.VMEM((modes * SUB, LANES), F32)] * 2,
         compiler_params=params(PROJECT_LIMIT),
-        cost_estimate=takes(8),
+        cost_estimate=takes(6),
         name="project_and_scan",
-    )(rest, fetch(weight, width, lead), up, weight, signal, decays)
-    start = 1 + pieces - lents
-    tables = out[start + 2 :]
-    return out[0], out[1:start], out[start : start + 2], [
+    )(blocks, up, weight, signal, decays)
+    tables = out[pieces + 2 :]
+    return out[:pieces], out[pieces : pieces + 2], [
         tables[3 * k : 3 * k + 3] for k in range(len(chunks))
     ]
+
+
+def last_kernel(block_ref, up_ref, w_ref, o_ref, w_buf, sems):
+    (copy,) = weight_copies(block_ref, w_ref, w_buf.shape[0], [w_buf], sems)
+    copy.start()
+    copy.wait()
+    project_block(up_ref, w_buf, o_ref)
+
+
+def project_last(up, weight, width, block):
+    tokens, feats = up.shape
+    return pl.pallas_call(
+        last_kernel,
+        out_shape=jax.ShapeDtypeStruct((tokens, width), BF16),
+        in_specs=[SM, VM, HBM],
+        out_specs=VM,
+        scratch_shapes=[pltpu.VMEM((width, feats), BF16), pltpu.SemaphoreType.DMA((1,))],
+        compiler_params=params(PROJECT_LIMIT),
+        cost_estimate=takes(4),
+        name="project_last",
+    )(block, up, weight)
 
 
 def pair_kernel(chunks, lent, mine_ref, lent_ref, *outs):
@@ -721,23 +732,23 @@
     hops = range(2, blocks, 2)
     levels = [1 << k for k in range(groups.bit_length() - 1)]
 
-    wanted = [me ^ hop ^ 1 for hop in hops] + [me ^ 1] + [me ^ hop for hop in hops]
-    rest = jnp.stack(wanted[1:]).astype(jnp.int32)
-    lead, mine = [jnp.reshape(b, (1,)).astype(jnp.int32) for b in (wanted[0], me)]
-    lead, rest, mine, place = lax.optimization_barrier((lead, rest, mine, place))
-    lent, parts, (state, sent), tables = project_and_scan(
-        upstream, out_weight, width, lead, rest, signal, dec, chunks, length
+    index = lambda blocks: jnp.stack(blocks).astype(jnp.int32)
+    first, second, third = index([me ^ hop ^ 1 for hop in hops]), index([me ^ hop for hop in hops] + [me ^ 1]), index([me])
+    first, second, third, place = lax.optimization_barrier((first, second, third, place))
+    lent = send(multiply(upstream, fetch(out_weight, width, first)), "ch", blocks, 1)
+    (*parts, mine), (state, sent), tables = project_and_scan(
+        upstream, out_weight, width, second, signal, dec, chunks, length
     )
-    lent = send(lent, "ch", blocks, 1)
     pairs = [pair_sums(part, lent, index, chunks) for index, part in enumerate(parts)]
     upstream, pairs = lax.optimization_barrier((upstream, pairs))
     arrived = [[send(pair[k], "ch", blocks, hop) for pair, hop in zip(pairs, hops)] for k in range(len(chunks))]
-    (own,) = project(upstream, out_weight, width, mine)
+    own = project_last(upstream, out_weight, width, third)
+    lent = send(mine, "ch", blocks, 1)
 
     before, pays, states, locs = [], [], [], []
 
     def take(chunk, low, high, sigp, y, y1):
-        grad, z, own_state = gradient_states([own, lent, *chunk], len(hops), high - low, low, dec, length)
+        grad, z, own_state = gradient_states([own, lent, *chunk], high - low, low, dec, length)
         states.append(own_state)
         pays.append(filter_sums(grad, sigp, dec, y, y1, length, low))
         locs.append((grad, z, low))

time: 52.7 us -> 51.7 us (0.981)
  starting transfers between devices: 18.9 us -> 18.1 us
    ppermute x10 -> x11, starting transfers between devices: 18.9 us -> 18.1 us  [send(): return lax.ppermute(x, axis, [(i, i ^ hop) for i in range(size)])]
    pallas_call x5 -> x6, Pallas kernels: 16.2 us -> 16.2 us  [the longest x1 6.94 us: project_and_scan(): pl.pallas_call(functools.partial(scan_kernel, pieces, chunks, length), ou...]
    ppermute x10 -> x11, waiting for transfers between devices: 6.29 us -> 6.27 us  [send(): return lax.ppermute(x, axis, [(i, i ^ hop) for i in range(size)])]
  transfers between devices with their start and end apart: 10 -> 11, of which waited for: 4 -> 6; matrix products, arithmetic and copies ran while one was open for 0% -> 0% of each run, Pallas kernels for 28% -> 42%
where the time goes in v4:
time: 51.7 us; the launch traced here: 51.5 us
  Pallas kernels  26.2 us (51%)
  starting transfers between devices  18.1 us (35%)
  waiting for transfers between devices  6.27 us (12%)
  between operations  0.79 us (2%)
    ppermute x11, starting transfers between devices, send(): return lax.ppermute(x, axis, [(i, i ^ hop) for i in range(size)])  18.1 us
    pallas_call x1, Pallas kernels, project_and_scan(): pl.pallas_call(functools.partial(scan_kernel, pieces, chunks, length), ou...  6.94 us
    ppermute x11, waiting for transfers between devices, send(): return lax.ppermute(x, axis, [(i, i ^ hop) for i in range(size)])  6.27 us
    pallas_call x2, Pallas kernels, filter_sums(): pl.pallas_call(functools.partial(filter_kernel, length, base), out_shape=...  3.68 us
    pallas_call x1, Pallas kernels, project_last(): pl.pallas_call(last_kernel, out_shape=jax.ShapeDtypeStruct((tokens, width...  3.48 us
    pallas_call x1, Pallas kernels, finish(): pl.pallas_call(functools.partial(finish_kernel, length, hop, chunks), out...  2.84 us
    pallas_call x2, Pallas kernels, local_part(): pl.pallas_call(functools.partial(local_kernel, length, base), out_shape=j...  2.47 us
    pallas_call x1, Pallas kernels, fetch(): pl.pallas_call(fetch_kernel, out_shape=jax.ShapeDtypeStruct((pieces * wid...  2.3 us
  transfers between devices with their start and end apart: 11, of which 6 were waited for; matrix products, arithmetic and copies ran while one was open for 0% of the time, Pallas kernels for 42%

profile of v4, /device:TPU:0, one launch (start us, length us, event | category | flops | bytes accessed | tf_op | source)
XLA Modules:
  0.0 51.5 jit_solution(9998301937268930411)
XLA Ops:
  0.6 0.0 copy-start
  0.6 0.0 copy-start.1
  0.7 0.0 copy-start.3
  0.7 0.1 pad_add_fusion.blocks_ref
  0.7 2.3 %fetch.1.held_ref = bf16[1024,2048]{1,0:T(8,128)(2,1)S(1)} custom-call(s32[1]{0:T(128)} %bitcast.blocks_ref, bf16[4096,2048]{1,0:T(8,128)(2,1)} %w_ref.5), custom_call_target="tpu_custom_call" | custom-call | flops 3000000000 | bytes 1 | tf_op jit(solution)/shard_map/fetch/pallas_call | solution.py:596
  3.0 0.1 copy-done
  3.1 1.3 %multiply.1 = bf16[256,1024]{1,0:T(8,128)(2,1)S(1)} custom-call(bf16[256,2048]{1,0:T(8,128)(2,1)S(1)} %copy-done, bf16[1024,2048]{1,0:T(8,128)(2,1)S(1)} %fetch.1.held_ref), custom_call_target="tpu_custom_call" | custom-call | flops 1000000000 | bytes 1 | tf_op jit(solution)/shard_map/multiply/pallas_call | solution.py:613
  4.4 0.5 %collective-permute-start.1 = (bf16[256,1024]{1,0:T(8,128)(2,1)S(1)}, bf16[256,1024]{1,0:T(8,128)(2,1)S(1)}, u32[]{:S(2)}, u32[]{:S(2)}) collective-permute-start(bf16[256,1024]{1,0:T(8,128)(2,1)S(1)} %multiply.1), channel_id=1, source_target_pairs={{0,1},{1,0},{2,3},{3,2},{4,5},{5,4},{6,7},{7,6},{8,9},{9,8},{10,11... | collective-permute-start | bytes 1572872 | tf_op jit(solution)/shard_map/ppermute | solution.py:711
  4.9 0.0 copy-done.1
  4.9 0.0 copy-done.3
  4.9 6.9 %project_and_scan.1 = (bf16[256,1024]{1,0:T(8,128)(2,1)S(1)}, bf16[256,1024]{1,0:T(8,128)(2,1)S(1)}, f32[32,1024]{1,0:T(8,128)S(1)}, bf16[32,1024]{1,0:T(8,128)(...) custom-call(s32[2]{0:T(128)S(1)} %pad_add_fusion.blocks_ref, ...), custom_call_target="tpu_custom_call" | custom-call | flops 6000000000 | bytes 1 | tf_op jit(solution)/shard_map/project_and_scan/pallas_call | solution.py:649
  11.9 0.1 collective-permute-start.3
  12.0 2.9 %collective-permute-start = (bf16[32,1024]{1,0:T(8,128)(2,1)S(1)}, bf16[32,1024]{1,0:T(8,128)(2,1)S(1)}, u32[]{:S(2)}, u32[]{:S(2)}) collective-permute-start(bf16[32,1024]{1,0:T(8,128)(2,1)S(1)} %get-tuple-element.55), channel_id=1, source_target_pairs={{0,4},{4,0},{8,12},{12,8},{16,20},{20,16},{24,28},{28,24},{1,5},{5... | collective-permute-start | bytes 196616 | tf_op jit(solution)/shard_map/ppermute | solution.py:711
  14.9 0.0 collective-permute-done.1.lent_ref
  14.9 0.1 pair_sums.1
  15.1 1.6 %collective-permute-start.4 = (bf16[256,512]{1,0:T(8,128)(2,1)S(1)}, bf16[256,512]{1,0:T(8,128)(2,1)S(1)}, u32[]{:S(2)}, u32[]{:S(2)}) collective-permute-start(bf16[256,512]{1,0:T(8,128)(2,1)S(1)} %get-tuple-element.60), channel_id=1, source_target_pairs={{0,2},{1,3},{2,0},{3,1},{4,6},{5,7},{6,4},{7,5},{8,10},{9,11},{10,... | collective-permute-start | bytes 786440 | tf_op jit(solution)/shard_map/ppermute | solution.py:711
  16.7 0.5 collective-permute-start.5
  17.2 0.1 collective-permute-done.there_ref
  17.3 0.1 prefix_step.2
  17.3 2.1 %collective-permute-start.2 = (bf16[32,1024]{1,0:T(8,128)(2,1)S(1)}, bf16[32,1024]{1,0:T(8,128)(2,1)S(1)}, u32[]{:S(2)}, u32[]{:S(2)}) collective-permute-start(bf16[32,1024]{1,0:T(8,128)(2,1)S(1)} %get-tuple-element.64), channel_id=1, source_target_pairs={{0,8},{4,12},{8,0},{12,4},{16,24},{20,28},{24,16},{28,20},{1,9},{5... | collective-permute-start | bytes 196616 | tf_op jit(solution)/shard_map/ppermute | solution.py:711
  19.4 3.5 %project_last.1.refs_0_ = bf16[256,1024]{1,0:T(8,128)(2,1)S(1)} custom-call(s32[1]{0:T(128)} %bitcast.3.block_ref, bf16[256,2048]{1,0:T(8,128)(2,1)S(1)} %copy-done, bf16[4096,2048]{1,0:T(8,128)(2,1)} %w_ref.5), custom_call_target="tpu_custom_call" | custom-call | flops 4000000000 | bytes 1 | tf_op jit(solution)/shard_map/project_last/pallas_call | solution.py:678
  22.9 0.0 copy-start.2
  22.9 0.0 copy-start.4
  22.9 0.0 collective-permute-done.2.there_ref
  22.9 0.1 prefix_step.3
  23.0 2.7 %collective-permute-start.7 = (bf16[32,1024]{1,0:T(8,128)(2,1)S(1)}, bf16[32,1024]{1,0:T(8,128)(2,1)S(1)}, u32[]{:S(2)}, u32[]{:S(2)}) collective-permute-start(bf16[32,1024]{1,0:T(8,128)(2,1)S(1)} %get-tuple-element.81), channel_id=1, source_target_pairs={{0,16},{4,20},{8,24},{12,28},{16,0},{20,4},{24,8},{28,12},{1,17},{... | collective-permute-start | bytes 196616 | tf_op jit(solution)/shard_map/ppermute | solution.py:711
  25.7 0.0 collective-permute-done.4.refs_2_
  25.7 0.0 collective-permute-done.3.refs_1_
  25.7 1.1 %gradient_states.2 = (f32[256,512]{1,0:T(8,128)S(1)}, f32[4,256,128]{2,1,0:T(8,128)S(1)}, f32[16,512]{1,0:T(8,128)S(1)}) custom-call(bf16[256,1024]{1,0:T(8,128)(2,1)S(1)} %project_last.1.refs_0_, bf16[256,1024]{1,0:T(8,128)(2,1)S(1)} %collective-permute-done.3.refs_1_, bf16[256,512]{1,0:T(8,128)(2,1)S(1)} %collective-permute-done.4.refs_2_, ...), custom_call_target="tpu_custom_call" | custom-call | flops 1000000000 | bytes 1 | tf_op jit(solution)/shard_map/gradient_states/pallas_call | solution.py:163
  26.8 1.8 %filter_sums.2.refs_0_ = f32[56,512]{1,0:T(8,128)S(1)} custom-call(f32[256,512]{1,0:T(8,128)S(1)} %get-tuple-element.73.grad_ref, bf16[256,512]{1,0:T(8,128)(2,1)S(1)} %get-tuple-element.74.sigp_ref, f32[16,1024]{1,0:T(8,128)S(1)} %bitcast.15, bf16[256,512]{1,0:T(8,128)(2,1)S(1)} %get-tuple-element.75.y_ref, bf16[256,512]{1,0:T(8,128)(2,1)S(1)} %get-tuple-element.76.y1_ref), custom_call_target="tpu_custom_call" | custom-call | flops 3000000000 | bytes 1 | tf_op jit(solution)/shard_map/filter_sums/pallas_call | solution.py:236
  28.6 0.1 collective-permute-done.5.refs_2_
  28.8 1.1 %gradient_states.3 = (f32[256,512]{1,0:T(8,128)S(1)}, f32[4,256,128]{2,1,0:T(8,128)S(1)}, f32[16,512]{1,0:T(8,128)S(1)}) custom-call(bf16[256,1024]{1,0:T(8,128)(2,1)S(1)} %project_last.1.refs_0_, bf16[256,1024]{1,0:T(8,128)(2,1)S(1)} %collective-permute-done.3.refs_1_, bf16[256,512]{1,0:T(8,128)(2,1)S(1)} %collective-permute-done.5.refs_2_, ...), custom_call_target="tpu_custom_call" | custom-call | flops 1000000000 | bytes 1 | tf_op jit(solution)/shard_map/gradient_states/pallas_call | solution.py:163
  29.8 1.4 %collective-permute-start.6 = (bf16[16,1024]{1,0:T(8,128)(2,1)S(1)}, bf16[16,1024]{1,0:T(8,128)(2,1)S(1)}, u32[]{:S(2)}, u32[]{:S(2)}) collective-permute-start(bf16[16,1024]{1,0:T(8,128)(2,1)S(1)} %get-tuple-element.79), channel_id=1, source_target_pairs={{0,4},{4,0},{8,12},{12,8},{16,20},{20,16},{24,28},{28,24},{1,5},{5... | collective-permute-start | bytes 98312 | tf_op jit(solution)/shard_map/ppermute | solution.py:711
  31.3 1.8 %filter_sums.3.refs_1_ = f32[56,512]{1,0:T(8,128)S(1)} custom-call(f32[256,512]{1,0:T(8,128)S(1)} %get-tuple-element.83.grad_ref, bf16[256,512]{1,0:T(8,128)(2,1)S(1)} %get-tuple-element.84.sigp_ref, f32[16,1024]{1,0:T(8,128)S(1)} %bitcast.17, bf16[256,512]{1,0:T(8,128)(2,1)S(1)} %get-tuple-element.85.y_ref, bf16[256,512]{1,0:T(8,128)(2,1)S(1)} %get-tuple-element.86.y1_ref), custom_call_target="tpu_custom_call" | custom-call | flops 3000000000 | bytes 1 | tf_op jit(solution)/shard_map/filter_sums/pallas_call | solution.py:236
  33.1 0.0 collective-permute-done.7.ends_ref
  33.1 0.7 %collective-permute-done.6.there_ref = bf16[16,1024]{1,0:T(8,128)(2,1)S(1)} collective-permute-done((bf16[16,1024]{1,0:T(8,128)(2,1)S(1)}, bf16[16,1024]{1,0:T(8,128)(2,1)S(1)}, u32[]{:S(2)}, u32[]{:S(2)}) %collective-permute-start.6) | collective-permute-done | bytes 32800 | tf_op jit(solution)/shard_map/ppermute | solution.py:711
  33.8 0.1 merge.1
  33.9 1.6 %collective-permute-start.8 = (bf16[56,1024]{1,0:T(8,128)(2,1)S(1)}, bf16[56,1024]{1,0:T(8,128)(2,1)S(1)}, u32[]{:S(2)}, u32[]{:S(2)}) collective-permute-start(bf16[56,1024]{1,0:T(8,128)(2,1)S(1)} %get-tuple-element.88), channel_id=1, source_target_pairs={{0,8},{4,12},{8,0},{12,4},{16,24},{20,28},{24,16},{28,20},{1,9},{5... | collective-permute-start | bytes 344072 | tf_op jit(solution)/shard_map/ppermute | solution.py:711
  35.6 1.2 %local_part.3.refs_1_ = f32[256,512]{1,0:T(8,128)S(1)} custom-call(f32[256,512]{1,0:T(8,128)S(1)} %get-tuple-element.83.grad_ref, f32[4,256,128]{2,1,0:T(8,128)S(1)} %get-tuple-element.95.z_ref, f32[16,1024]{1,0:T(8,128)S(1)} %bitcast.19, f32[16,1024]{1,0:T(8,128)S(1)} %bitcast.23, f32[1,1024]{1,0:T(1,128)S(1)} %bitcast.27), custom_call_target="tpu_custom_call" | custom-call | flops 1500000000 | bytes 1 | tf_op jit(solution)/shard_map/local_part/pallas_call | solution.py:296
  36.8 2.0 %collective-permute-done.8.there_ref = bf16[56,1024]{1,0:T(8,128)(2,1)S(1)} collective-permute-done((bf16[56,1024]{1,0:T(8,128)(2,1)S(1)}, bf16[56,1024]{1,0:T(8,128)(2,1)S(1)}, u32[]{:S(2)}, u32[]{:S(2)}) %collective-permute-start.8) | collective-permute-done | bytes 114720 | tf_op jit(solution)/shard_map/ppermute | solution.py:711
  38.8 0.1 tail_step.1
  38.8 3.5 %collective-permute-start.9 = (bf16[56,1024]{1,0:T(8,128)(2,1)S(1)}, bf16[56,1024]{1,0:T(8,128)(2,1)S(1)}, u32[]{:S(2)}, u32[]{:S(2)}) collective-permute-start(bf16[56,1024]{1,0:T(8,128)(2,1)S(1)} %get-tuple-element.92), channel_id=1, source_target_pairs={{0,16},{4,20},{8,24},{12,28},{16,0},{20,4},{24,8},{28,12},{1,17},{... | collective-permute-start | bytes 344072 | tf_op jit(solution)/shard_map/ppermute | solution.py:711
  42.3 1.2 %local_part.2.refs_0_ = f32[256,512]{1,0:T(8,128)S(1)} custom-call(f32[256,512]{1,0:T(8,128)S(1)} %get-tuple-element.73.grad_ref, f32[4,256,128]{2,1,0:T(8,128)S(1)} %get-tuple-element.94.z_ref, f32[16,1024]{1,0:T(8,128)S(1)} %bitcast.21, f32[16,1024]{1,0:T(8,128)S(1)} %bitcast.24, f32[1,1024]{1,0:T(1,128)S(1)} %bitcast.28), custom_call_target="tpu_custom_call" | custom-call | flops 1500000000 | bytes 1 | tf_op jit(solution)/shard_map/local_part/pallas_call | solution.py:296
  43.6 2.8 %collective-permute-done.9.there_ref = bf16[56,1024]{1,0:T(8,128)(2,1)S(1)} collective-permute-done((bf16[56,1024]{1,0:T(8,128)(2,1)S(1)}, bf16[56,1024]{1,0:T(8,128)(2,1)S(1)}, u32[]{:S(2)}, u32[]{:S(2)}) %collective-permute-start.9) | collective-permute-done | bytes 114720 | tf_op jit(solution)/shard_map/ppermute | solution.py:711
  46.4 1.1 %collective-permute-start.10 = (bf16[40,1024]{1,0:T(8,128)(2,1)S(1)}, bf16[40,1024]{1,0:T(8,128)(2,1)S(1)}, u32[]{:S(2)}, u32[]{:S(2)}) collective-permute-start(bf16[40,1024]{1,0:T(8,128)(2,1)S(1)} %get-tuple-element.97), channel_id=1, source_target_pairs={{0,4},{4,0},{8,12},{12,8},{16,20},{20,16},{24,28},{28,24},{1,5},{5... | collective-permute-start | bytes 245768 | tf_op jit(solution)/shard_map/ppermute | solution.py:711
  47.5 2.8 %finish.1 = bf16[256,1024]{1,0:T(8,128)(2,1)} custom-call(s32[1]{0:T(128)} %bitcast.4.me_ref, bf16[56,1024]{1,0:T(8,128)(2,1)S(1)} %collective-permute-done.9.there_ref, f32[16,1024]{1,0:T(8,128)S(1)} %get-tuple-element.93.later_ref, f32[16,1024]{1,0:T(8,128)S(1)} %bitcast.22, f32[16,1024]{1,0:T(8,128)S(1)} %bitcast.25, f32[256,512]{1,0:T(8,128)S(1)} %local_part.2.refs_0_, ...), custom_call_target="tpu_custom_call" | custom-call | flops 3000000000 | bytes 1 | tf_op jit(solution)/shard_map/finish/pallas_call | solution.py:350
  50.3 0.6 %collective-permute-done.10.there_ref = bf16[40,1024]{1,0:T(8,128)(2,1)S(1)} collective-permute-done((bf16[40,1024]{1,0:T(8,128)(2,1)S(1)}, bf16[40,1024]{1,0:T(8,128)(2,1)S(1)}, u32[]{:S(2)}, u32[]{:S(2)}) %collective-permute-start.10) | collective-permute-done | bytes 81952 | tf_op jit(solution)/shard_map/ppermute | solution.py:711
  50.9 0.7 %results.1 = (f32[16,1024]{1,0:T(8,128)}, f32[16,1024]{1,0:T(8,128)}, f32[1,1024]{1,0:T(1,128)}) custom-call(bf16[40,1024]{1,0:T(8,128)(2,1)S(1)} %collective-permute-done.10.there_ref, f32[40,1024]{1,0:T(8,128)S(1)} %get-tuple-element.98.sums_ref, f32[16,1024]{1,0:T(8,128)S(1)} %bitcast.26), custom_call_target="tpu_custom_call" | custom-call | flops 1 | bytes 1 | tf_op jit(solution)/shard_map/results/pallas_call | solution.py:516
  (4 shorter events, 0.0 us)
Async XLA Ops:
  0.6 2.5 %copy-start = (bf16[256,2048]{1,0:T(8,128)(2,1)S(1)}, bf16[256,2048]{1,0:T(8,128)(2,1)}, u32[]{:S(2)}) copy-start(bf16[256,2048]{1,0:T(8,128)(2,1)} %up_ref.4) | copy-start | bytes 3145732
  0.6 4.3 %copy-start.1 = (f32[1024,16]{0,1:T(8,128)S(1)}, f32[1024,16]{0,1:T(8,128)}, u32[]{:S(2)}) copy-start(f32[1024,16]{0,1:T(8,128)} %param.10) | copy-start | bytes 196612
  0.7 4.3 %copy-start.3 = (bf16[256,1024]{1,0:T(8,128)(2,1)S(1)}, bf16[256,1024]{1,0:T(8,128)(2,1)}, u32[]{:S(2)}) copy-start(bf16[256,1024]{1,0:T(8,128)(2,1)} %sig_ref.1) | copy-start | bytes 1572868
  4.4 10.5 %collective-permute-start.1 = (bf16[256,1024]{1,0:T(8,128)(2,1)S(1)}, bf16[256,1024]{1,0:T(8,128)(2,1)S(1)}, u32[]{:S(2)}, u32[]{:S(2)}) collective-permute-start(bf16[256,1024]{1,0:T(8,128)(2,1)S(1)} %multiply.1), channel_id=1, source_target_pairs={{0,1},{1,0},{2,3},{3,2},{4,5},{5,4},{6,7},{7,6},{8,9},{9,8},{10,11... | collective-permute-start | bytes 1572872 | tf_op jit(solution)/shard_map/ppermute | solution.py:711
  11.9 13.8 %collective-permute-start.3 = (bf16[256,1024]{1,0:T(8,128)(2,1)S(1)}, bf16[256,1024]{1,0:T(8,128)(2,1)S(1)}, u32[]{:S(2)}, u32[]{:S(2)}) collective-permute-start(bf16[256,1024]{1,0:T(8,128)(2,1)S(1)} %get-tuple-element.71), channel_id=1, source_target_pairs={{0,1},{1,0},{2,3},{3,2},{4,5},{5,4},{6,7},{7,6},{8,9},{9,8},{10,11... | collective-permute-start | bytes 1572872 | tf_op jit(solution)/shard_map/ppermute | solution.py:711
  12.0 5.3 %collective-permute-start = (bf16[32,1024]{1,0:T(8,128)(2,1)S(1)}, bf16[32,1024]{1,0:T(8,128)(2,1)S(1)}, u32[]{:S(2)}, u32[]{:S(2)}) collective-permute-start(bf16[32,1024]{1,0:T(8,128)(2,1)S(1)} %get-tuple-element.55), channel_id=1, source_target_pairs={{0,4},{4,0},{8,12},{12,8},{16,20},{20,16},{24,28},{28,24},{1,5},{5... | collective-permute-start | bytes 196616 | tf_op jit(solution)/shard_map/ppermute | solution.py:711
  15.1 10.6 %collective-permute-start.4 = (bf16[256,512]{1,0:T(8,128)(2,1)S(1)}, bf16[256,512]{1,0:T(8,128)(2,1)S(1)}, u32[]{:S(2)}, u32[]{:S(2)}) collective-permute-start(bf16[256,512]{1,0:T(8,128)(2,1)S(1)} %get-tuple-element.60), channel_id=1, source_target_pairs={{0,2},{1,3},{2,0},{3,1},{4,6},{5,7},{6,4},{7,5},{8,10},{9,11},{10,... | collective-permute-start | bytes 786440 | tf_op jit(solution)/shard_map/ppermute | solution.py:711
  16.7 12.1 %collective-permute-start.5 = (bf16[256,512]{1,0:T(8,128)(2,1)S(1)}, bf16[256,512]{1,0:T(8,128)(2,1)S(1)}, u32[]{:S(2)}, u32[]{:S(2)}) collective-permute-start(bf16[256,512]{1,0:T(8,128)(2,1)S(1)} %get-tuple-element.61), channel_id=1, source_target_pairs={{0,2},{1,3},{2,0},{3,1},{4,6},{5,7},{6,4},{7,5},{8,10},{9,11},{10,... | collective-permute-start | bytes 786440 | tf_op jit(solution)/shard_map/ppermute | solution.py:711
  17.3 5.6 %collective-permute-start.2 = (bf16[32,1024]{1,0:T(8,128)(2,1)S(1)}, bf16[32,1024]{1,0:T(8,128)(2,1)S(1)}, u32[]{:S(2)}, u32[]{:S(2)}) collective-permute-start(bf16[32,1024]{1,0:T(8,128)(2,1)S(1)} %get-tuple-element.64), channel_id=1, source_target_pairs={{0,8},{4,12},{8,0},{12,4},{16,24},{20,28},{24,16},{28,20},{1,9},{5... | collective-permute-start | bytes 196616 | tf_op jit(solution)/shard_map/ppermute | solution.py:711
  22.9 12.7 %copy-start.2 = (f32[1024,16]{0,1:T(8,128)S(1)}, f32[1024,16]{0,1:T(8,128)}, u32[]{:S(2)}) copy-start(f32[1024,16]{0,1:T(8,128)} %param.9) | copy-start | bytes 196612
  22.9 12.7 %copy-start.4 = (f32[1024]{0:T(1024)S(1)}, f32[1024]{0:T(1024)}, u32[]{:S(2)}) copy-start(f32[1024]{0:T(1024)} %param.11) | copy-start | bytes 12292
  23.0 10.1 %collective-permute-start.7 = (bf16[32,1024]{1,0:T(8,128)(2,1)S(1)}, bf16[32,1024]{1,0:T(8,128)(2,1)S(1)}, u32[]{:S(2)}, u32[]{:S(2)}) collective-permute-start(bf16[32,1024]{1,0:T(8,128)(2,1)S(1)} %get-tuple-element.81), channel_id=1, source_target_pairs={{0,16},{4,20},{8,24},{12,28},{16,0},{20,4},{24,8},{28,12},{1,17},{... | collective-permute-start | bytes 196616 | tf_op jit(solution)/shard_map/ppermute | solution.py:711
  29.8 4.0 %collective-permute-start.6 = (bf16[16,1024]{1,0:T(8,128)(2,1)S(1)}, bf16[16,1024]{1,0:T(8,128)(2,1)S(1)}, u32[]{:S(2)}, u32[]{:S(2)}) collective-permute-start(bf16[16,1024]{1,0:T(8,128)(2,1)S(1)} %get-tuple-element.79), channel_id=1, source_target_pairs={{0,4},{4,0},{8,12},{12,8},{16,20},{20,16},{24,28},{28,24},{1,5},{5... | collective-permute-start | bytes 98312 | tf_op jit(solution)/shard_map/ppermute | solution.py:711
  33.9 4.9 %collective-permute-start.8 = (bf16[56,1024]{1,0:T(8,128)(2,1)S(1)}, bf16[56,1024]{1,0:T(8,128)(2,1)S(1)}, u32[]{:S(2)}, u32[]{:S(2)}) collective-permute-start(bf16[56,1024]{1,0:T(8,128)(2,1)S(1)} %get-tuple-element.88), channel_id=1, source_target_pairs={{0,8},{4,12},{8,0},{12,4},{16,24},{20,28},{24,16},{28,20},{1,9},{5... | collective-permute-start | bytes 344072 | tf_op jit(solution)/shard_map/ppermute | solution.py:711
  38.8 7.5 %collective-permute-start.9 = (bf16[56,1024]{1,0:T(8,128)(2,1)S(1)}, bf16[56,1024]{1,0:T(8,128)(2,1)S(1)}, u32[]{:S(2)}, u32[]{:S(2)}) collective-permute-start(bf16[56,1024]{1,0:T(8,128)(2,1)S(1)} %get-tuple-element.92), channel_id=1, source_target_pairs={{0,16},{4,20},{8,24},{12,28},{16,0},{20,4},{24,8},{28,12},{1,17},{... | collective-permute-start | bytes 344072 | tf_op jit(solution)/shard_map/ppermute | solution.py:711
  46.4 4.5 %collective-permute-start.10 = (bf16[40,1024]{1,0:T(8,128)(2,1)S(1)}, bf16[40,1024]{1,0:T(8,128)(2,1)S(1)}, u32[]{:S(2)}, u32[]{:S(2)}) collective-permute-start(bf16[40,1024]{1,0:T(8,128)(2,1)S(1)} %get-tuple-element.97), channel_id=1, source_target_pairs={{0,4},{4,0},{8,12},{12,8},{16,20},{20,16},{24,28},{28,24},{1,5},{5... | collective-permute-start | bytes 245768 | tf_op jit(solution)/shard_map/ppermute | solution.py:711

commit v5 on v4

--- a/solution.py
+++ b/solution.py
@@ -254,7 +254,7 @@
     return outs
 
 
-def local_kernel(length, base, grad_ref, z_ref, dec_ref, res_ref, gain_ref, loc_ref, cbuf):
+def local_kernel(length, base, grad_ref, z_ref, dec_ref, res_ref, gain_ref, loc_ref, cbuf, zbuf):
     tokens, width = grad_ref.shape
     modes = dec_ref.shape[0]
     steps = tokens // SUB
@@ -267,12 +267,13 @@
         pole_all = jnp.exp(-rate)
         weight = res_ref[:, lanes] * (1.0 / math.sqrt(length))
         gain = spread(gain_ref[:, lanes])
+        zbuf[...] = z_ref[block]
         sums = jnp.zeros((modes, LANES), F32)
         for j in reversed(range(SUB)):
             pick = pl.ds(j, modes, stride=SUB)
             back = jnp.exp(rate * (steps * (j + 1) - 1))
             cbuf[pick, :] = weight * (back * sums)
-            sums = sums + z_ref[block, pick, :]
+            sums = sums + zbuf[pick, :]
         filt = []
         for _ in range(steps):
             filt.append(spread(jnp.sum(weight, axis=0, keepdims=True)))
@@ -298,7 +299,7 @@
         out_shape=jax.ShapeDtypeStruct((tokens, width), F32),
         in_specs=[VM] * 5,
         out_specs=VM,
-        scratch_shapes=[pltpu.VMEM((modes * SUB, LANES), F32)],
+        scratch_shapes=[pltpu.VMEM((modes * SUB, LANES), F32)] * 2,
         compiler_params=params(),
         cost_estimate=takes(1.5),
         name="local_part",
@@ -307,7 +308,7 @@
 
 def finish_kernel(length, hop, chunks, me_ref, there_ref, later_ref, dec_ref, res_ref, *refs):
     locs = refs[: len(chunks)]
-    o_ref, vals = refs[len(chunks) :]
+    o_ref, vals, work = refs[len(chunks) :]
     tokens = o_ref.shape[0]
     modes = dec_ref.shape[0]
     steps = tokens // SUB
@@ -336,13 +337,11 @@
                     ]
                     outs = carry_out(outs, poles, starts)
                 for i in range(steps):
-                    loc_ref[rows_of(i, half), here] = outs[i]
-
-    turn = interleave(tokens, transpose=True)
-    for loc_ref, (low, high) in zip(locs, chunks):
-        o_ref[:, low:high] = jnp.dot(
-            turn, loc_ref[...].astype(BF16), preferred_element_type=F32
-        ).astype(BF16)
+                    work[rows_of(i, half), lanes] = outs[i]
+
+    o_ref[...] = jnp.dot(
+        interleave(tokens, transpose=True), work[...].astype(BF16), preferred_element_type=F32
+    ).astype(BF16)
 
 
 def finish(me, there, later, decays, residues, locs, chunks, tokens, length, hop):
@@ -352,7 +351,7 @@
         out_shape=jax.ShapeDtypeStruct((tokens, width), BF16),
         in_specs=[SM] + [VM] * (4 + len(locs)),
         out_specs=VM,
-        scratch_shapes=[pltpu.VMEM((modes, width), F32)],
+        scratch_shapes=[pltpu.VMEM((modes, width), F32), pltpu.VMEM((tokens, width), F32)],
         compiler_params=params(),
         cost_estimate=takes(3),
         name="finish",

time: 51.7 us -> 51.7 us (level)
  transfers between devices with their start and end apart: 11 -> 11, of which waited for: 6 -> 6; matrix products, arithmetic and copies ran while one was open for 0% -> 0% of each run, Pallas kernels for 42% -> 43%
where the time goes in v5:
time: 51.7 us; the launch traced here: 51.5 us
  Pallas kernels  26.3 us (51%)
  starting transfers between devices  18.1 us (35%)
  waiting for transfers between devices  6.21 us (12%)
  between operations  0.79 us (2%)
    ppermute x11, starting transfers between devices, send(): return lax.ppermute(x, axis, [(i, i ^ hop) for i in range(size)])  18.1 us
    pallas_call x1, Pallas kernels, project_and_scan(): pl.pallas_call(functools.partial(scan_kernel, pieces, chunks, length), ou...  6.94 us
    ppermute x11, waiting for transfers between devices, send(): return lax.ppermute(x, axis, [(i, i ^ hop) for i in range(size)])  6.21 us
    pallas_call x2, Pallas kernels, filter_sums(): pl.pallas_call(functools.partial(filter_kernel, length, base), out_shape=...  3.68 us
    pallas_call x1, Pallas kernels, project_last(): pl.pallas_call(last_kernel, out_shape=jax.ShapeDtypeStruct((tokens, width...  3.48 us
    pallas_call x1, Pallas kernels, finish(): pl.pallas_call(functools.partial(finish_kernel, length, hop, chunks), out...  2.85 us
    pallas_call x2, Pallas kernels, local_part(): pl.pallas_call(functools.partial(local_kernel, length, base), out_shape=j...  2.53 us
    pallas_call x1, Pallas kernels, fetch(): pl.pallas_call(fetch_kernel, out_shape=jax.ShapeDtypeStruct((pieces * wid...  2.3 us
  transfers between devices with their start and end apart: 11, of which 6 were waited for; matrix products, arithmetic and copies ran while one was open for 0% of the time, Pallas kernels for 43%

profile of v5, /device:TPU:0, one launch (start us, length us, event | category | flops | bytes accessed | tf_op | source)
XLA Modules:
  0.0 51.5 jit_solution(9937027385161819781)
XLA Ops:
  0.6 0.0 copy-start
  0.6 0.0 copy-start.1
  0.7 0.0 copy-start.3
  0.7 0.1 pad_add_fusion.blocks_ref
  0.7 2.3 %fetch.1.held_ref = bf16[1024,2048]{1,0:T(8,128)(2,1)S(1)} custom-call(s32[1]{0:T(128)} %bitcast.blocks_ref, bf16[4096,2048]{1,0:T(8,128)(2,1)} %w_ref.5), custom_call_target="tpu_custom_call" | custom-call | flops 3000000000 | bytes 1 | tf_op jit(solution)/shard_map/fetch/pallas_call | solution.py:595
  3.0 0.1 copy-done
  3.1 1.3 %multiply.1 = bf16[256,1024]{1,0:T(8,128)(2,1)S(1)} custom-call(bf16[256,2048]{1,0:T(8,128)(2,1)S(1)} %copy-done, bf16[1024,2048]{1,0:T(8,128)(2,1)S(1)} %fetch.1.held_ref), custom_call_target="tpu_custom_call" | custom-call | flops 1000000000 | bytes 1 | tf_op jit(solution)/shard_map/multiply/pallas_call | solution.py:612
  4.4 0.5 %collective-permute-start.1 = (bf16[256,1024]{1,0:T(8,128)(2,1)S(1)}, bf16[256,1024]{1,0:T(8,128)(2,1)S(1)}, u32[]{:S(2)}, u32[]{:S(2)}) collective-permute-start(bf16[256,1024]{1,0:T(8,128)(2,1)S(1)} %multiply.1), channel_id=1, source_target_pairs={{0,1},{1,0},{2,3},{3,2},{4,5},{5,4},{6,7},{7,6},{8,9},{9,8},{10,11... | collective-permute-start | bytes 1572872 | tf_op jit(solution)/shard_map/ppermute | solution.py:710
  4.9 0.0 copy-done.1
  4.9 0.0 copy-done.3
  4.9 6.9 %project_and_scan.1 = (bf16[256,1024]{1,0:T(8,128)(2,1)S(1)}, bf16[256,1024]{1,0:T(8,128)(2,1)S(1)}, f32[32,1024]{1,0:T(8,128)S(1)}, bf16[32,1024]{1,0:T(8,128)(...) custom-call(s32[2]{0:T(128)S(1)} %pad_add_fusion.blocks_ref, ...), custom_call_target="tpu_custom_call" | custom-call | flops 6000000000 | bytes 1 | tf_op jit(solution)/shard_map/project_and_scan/pallas_call | solution.py:648
  11.9 0.1 collective-permute-start.3
  12.0 2.9 %collective-permute-start = (bf16[32,1024]{1,0:T(8,128)(2,1)S(1)}, bf16[32,1024]{1,0:T(8,128)(2,1)S(1)}, u32[]{:S(2)}, u32[]{:S(2)}) collective-permute-start(bf16[32,1024]{1,0:T(8,128)(2,1)S(1)} %get-tuple-element.55), channel_id=1, source_target_pairs={{0,4},{4,0},{8,12},{12,8},{16,20},{20,16},{24,28},{28,24},{1,5},{5... | collective-permute-start | bytes 196616 | tf_op jit(solution)/shard_map/ppermute | solution.py:710
  14.9 0.0 collective-permute-done.1.lent_ref
  14.9 0.1 pair_sums.1
  15.1 1.6 %collective-permute-start.4 = (bf16[256,512]{1,0:T(8,128)(2,1)S(1)}, bf16[256,512]{1,0:T(8,128)(2,1)S(1)}, u32[]{:S(2)}, u32[]{:S(2)}) collective-permute-start(bf16[256,512]{1,0:T(8,128)(2,1)S(1)} %get-tuple-element.60), channel_id=1, source_target_pairs={{0,2},{1,3},{2,0},{3,1},{4,6},{5,7},{6,4},{7,5},{8,10},{9,11},{10,... | collective-permute-start | bytes 786440 | tf_op jit(solution)/shard_map/ppermute | solution.py:710
  16.7 0.5 collective-permute-start.5
  17.2 0.1 collective-permute-done.there_ref
  17.3 0.1 prefix_step.2
  17.3 2.1 %collective-permute-start.2 = (bf16[32,1024]{1,0:T(8,128)(2,1)S(1)}, bf16[32,1024]{1,0:T(8,128)(2,1)S(1)}, u32[]{:S(2)}, u32[]{:S(2)}) collective-permute-start(bf16[32,1024]{1,0:T(8,128)(2,1)S(1)} %get-tuple-element.64), channel_id=1, source_target_pairs={{0,8},{4,12},{8,0},{12,4},{16,24},{20,28},{24,16},{28,20},{1,9},{5... | collective-permute-start | bytes 196616 | tf_op jit(solution)/shard_map/ppermute | solution.py:710
  19.4 3.5 %project_last.1.refs_0_ = bf16[256,1024]{1,0:T(8,128)(2,1)S(1)} custom-call(s32[1]{0:T(128)} %bitcast.3.block_ref, bf16[256,2048]{1,0:T(8,128)(2,1)S(1)} %copy-done, bf16[4096,2048]{1,0:T(8,128)(2,1)} %w_ref.5), custom_call_target="tpu_custom_call" | custom-call | flops 4000000000 | bytes 1 | tf_op jit(solution)/shard_map/project_last/pallas_call | solution.py:677
  22.9 0.0 copy-start.2
  22.9 0.0 copy-start.4
  22.9 0.0 collective-permute-done.2.there_ref
  22.9 0.1 prefix_step.3
  23.0 2.7 %collective-permute-start.7 = (bf16[32,1024]{1,0:T(8,128)(2,1)S(1)}, bf16[32,1024]{1,0:T(8,128)(2,1)S(1)}, u32[]{:S(2)}, u32[]{:S(2)}) collective-permute-start(bf16[32,1024]{1,0:T(8,128)(2,1)S(1)} %get-tuple-element.81), channel_id=1, source_target_pairs={{0,16},{4,20},{8,24},{12,28},{16,0},{20,4},{24,8},{28,12},{1,17},{... | collective-permute-start | bytes 196616 | tf_op jit(solution)/shard_map/ppermute | solution.py:710
  25.7 0.0 collective-permute-done.4.refs_2_
  25.7 0.0 collective-permute-done.3.refs_1_
  25.7 1.1 %gradient_states.2 = (f32[256,512]{1,0:T(8,128)S(1)}, f32[4,256,128]{2,1,0:T(8,128)S(1)}, f32[16,512]{1,0:T(8,128)S(1)}) custom-call(bf16[256,1024]{1,0:T(8,128)(2,1)S(1)} %project_last.1.refs_0_, bf16[256,1024]{1,0:T(8,128)(2,1)S(1)} %collective-permute-done.3.refs_1_, bf16[256,512]{1,0:T(8,128)(2,1)S(1)} %collective-permute-done.4.refs_2_, ...), custom_call_target="tpu_custom_call" | custom-call | flops 1000000000 | bytes 1 | tf_op jit(solution)/shard_map/gradient_states/pallas_call | solution.py:163
  26.8 1.8 %filter_sums.2.refs_0_ = f32[56,512]{1,0:T(8,128)S(1)} custom-call(f32[256,512]{1,0:T(8,128)S(1)} %get-tuple-element.73.grad_ref, bf16[256,512]{1,0:T(8,128)(2,1)S(1)} %get-tuple-element.74.sigp_ref, f32[16,1024]{1,0:T(8,128)S(1)} %bitcast.15, bf16[256,512]{1,0:T(8,128)(2,1)S(1)} %get-tuple-element.75.y_ref, bf16[256,512]{1,0:T(8,128)(2,1)S(1)} %get-tuple-element.76.y1_ref), custom_call_target="tpu_custom_call" | custom-call | flops 3000000000 | bytes 1 | tf_op jit(solution)/shard_map/filter_sums/pallas_call | solution.py:236
  28.6 0.1 collective-permute-done.5.refs_2_
  28.8 1.1 %gradient_states.3 = (f32[256,512]{1,0:T(8,128)S(1)}, f32[4,256,128]{2,1,0:T(8,128)S(1)}, f32[16,512]{1,0:T(8,128)S(1)}) custom-call(bf16[256,1024]{1,0:T(8,128)(2,1)S(1)} %project_last.1.refs_0_, bf16[256,1024]{1,0:T(8,128)(2,1)S(1)} %collective-permute-done.3.refs_1_, bf16[256,512]{1,0:T(8,128)(2,1)S(1)} %collective-permute-done.5.refs_2_, ...), custom_call_target="tpu_custom_call" | custom-call | flops 1000000000 | bytes 1 | tf_op jit(solution)/shard_map/gradient_states/pallas_call | solution.py:163
  29.8 1.4 %collective-permute-start.6 = (bf16[16,1024]{1,0:T(8,128)(2,1)S(1)}, bf16[16,1024]{1,0:T(8,128)(2,1)S(1)}, u32[]{:S(2)}, u32[]{:S(2)}) collective-permute-start(bf16[16,1024]{1,0:T(8,128)(2,1)S(1)} %get-tuple-element.79), channel_id=1, source_target_pairs={{0,4},{4,0},{8,12},{12,8},{16,20},{20,16},{24,28},{28,24},{1,5},{5... | collective-permute-start | bytes 98312 | tf_op jit(solution)/shard_map/ppermute | solution.py:710
  31.3 1.8 %filter_sums.3.refs_1_ = f32[56,512]{1,0:T(8,128)S(1)} custom-call(f32[256,512]{1,0:T(8,128)S(1)} %get-tuple-element.83.grad_ref, bf16[256,512]{1,0:T(8,128)(2,1)S(1)} %get-tuple-element.84.sigp_ref, f32[16,1024]{1,0:T(8,128)S(1)} %bitcast.17, bf16[256,512]{1,0:T(8,128)(2,1)S(1)} %get-tuple-element.85.y_ref, bf16[256,512]{1,0:T(8,128)(2,1)S(1)} %get-tuple-element.86.y1_ref), custom_call_target="tpu_custom_call" | custom-call | flops 3000000000 | bytes 1 | tf_op jit(solution)/shard_map/filter_sums/pallas_call | solution.py:236
  33.1 0.0 collective-permute-done.7.ends_ref
  33.1 0.7 %collective-permute-done.6.there_ref = bf16[16,1024]{1,0:T(8,128)(2,1)S(1)} collective-permute-done((bf16[16,1024]{1,0:T(8,128)(2,1)S(1)}, bf16[16,1024]{1,0:T(8,128)(2,1)S(1)}, u32[]{:S(2)}, u32[]{:S(2)}) %collective-permute-start.6) | collective-permute-done | bytes 32800 | tf_op jit(solution)/shard_map/ppermute | solution.py:710
  33.8 0.1 merge.1
  33.9 1.6 %collective-permute-start.8 = (bf16[56,1024]{1,0:T(8,128)(2,1)S(1)}, bf16[56,1024]{1,0:T(8,128)(2,1)S(1)}, u32[]{:S(2)}, u32[]{:S(2)}) collective-permute-start(bf16[56,1024]{1,0:T(8,128)(2,1)S(1)} %get-tuple-element.88), channel_id=1, source_target_pairs={{0,8},{4,12},{8,0},{12,4},{16,24},{20,28},{24,16},{28,20},{1,9},{5... | collective-permute-start | bytes 344072 | tf_op jit(solution)/shard_map/ppermute | solution.py:710
  35.6 1.3 %local_part.3.refs_1_ = f32[256,512]{1,0:T(8,128)S(1)} custom-call(f32[256,512]{1,0:T(8,128)S(1)} %get-tuple-element.83.grad_ref, f32[4,256,128]{2,1,0:T(8,128)S(1)} %get-tuple-element.95.z_ref, f32[16,1024]{1,0:T(8,128)S(1)} %bitcast.19, f32[16,1024]{1,0:T(8,128)S(1)} %bitcast.23, f32[1,1024]{1,0:T(1,128)S(1)} %bitcast.27), custom_call_target="tpu_custom_call" | custom-call | flops 1500000000 | bytes 1 | tf_op jit(solution)/shard_map/local_part/pallas_call | solution.py:297
  36.8 1.9 %collective-permute-done.8.there_ref = bf16[56,1024]{1,0:T(8,128)(2,1)S(1)} collective-permute-done((bf16[56,1024]{1,0:T(8,128)(2,1)S(1)}, bf16[56,1024]{1,0:T(8,128)(2,1)S(1)}, u32[]{:S(2)}, u32[]{:S(2)}) %collective-permute-start.8) | collective-permute-done | bytes 114720 | tf_op jit(solution)/shard_map/ppermute | solution.py:710
  38.8 0.1 tail_step.1
  38.8 3.5 %collective-permute-start.9 = (bf16[56,1024]{1,0:T(8,128)(2,1)S(1)}, bf16[56,1024]{1,0:T(8,128)(2,1)S(1)}, u32[]{:S(2)}, u32[]{:S(2)}) collective-permute-start(bf16[56,1024]{1,0:T(8,128)(2,1)S(1)} %get-tuple-element.92), channel_id=1, source_target_pairs={{0,16},{4,20},{8,24},{12,28},{16,0},{20,4},{24,8},{28,12},{1,17},{... | collective-permute-start | bytes 344072 | tf_op jit(solution)/shard_map/ppermute | solution.py:710
  42.3 1.3 %local_part.2.refs_0_ = f32[256,512]{1,0:T(8,128)S(1)} custom-call(f32[256,512]{1,0:T(8,128)S(1)} %get-tuple-element.73.grad_ref, f32[4,256,128]{2,1,0:T(8,128)S(1)} %get-tuple-element.94.z_ref, f32[16,1024]{1,0:T(8,128)S(1)} %bitcast.21, f32[16,1024]{1,0:T(8,128)S(1)} %bitcast.24, f32[1,1024]{1,0:T(1,128)S(1)} %bitcast.28), custom_call_target="tpu_custom_call" | custom-call | flops 1500000000 | bytes 1 | tf_op jit(solution)/shard_map/local_part/pallas_call | solution.py:297
  43.6 2.7 %collective-permute-done.9.there_ref = bf16[56,1024]{1,0:T(8,128)(2,1)S(1)} collective-permute-done((bf16[56,1024]{1,0:T(8,128)(2,1)S(1)}, bf16[56,1024]{1,0:T(8,128)(2,1)S(1)}, u32[]{:S(2)}, u32[]{:S(2)}) %collective-permute-start.9) | collective-permute-done | bytes 114720 | tf_op jit(solution)/shard_map/ppermute | solution.py:710
  46.4 1.1 %collective-permute-start.10 = (bf16[40,1024]{1,0:T(8,128)(2,1)S(1)}, bf16[40,1024]{1,0:T(8,128)(2,1)S(1)}, u32[]{:S(2)}, u32[]{:S(2)}) collective-permute-start(bf16[40,1024]{1,0:T(8,128)(2,1)S(1)} %get-tuple-element.97), channel_id=1, source_target_pairs={{0,4},{4,0},{8,12},{12,8},{16,20},{20,16},{24,28},{28,24},{1,5},{5... | collective-permute-start | bytes 245768 | tf_op jit(solution)/shard_map/ppermute | solution.py:710
  47.5 2.8 %finish.1 = bf16[256,1024]{1,0:T(8,128)(2,1)} custom-call(s32[1]{0:T(128)} %bitcast.4.me_ref, bf16[56,1024]{1,0:T(8,128)(2,1)S(1)} %collective-permute-done.9.there_ref, f32[16,1024]{1,0:T(8,128)S(1)} %get-tuple-element.93.later_ref, f32[16,1024]{1,0:T(8,128)S(1)} %bitcast.22, f32[16,1024]{1,0:T(8,128)S(1)} %bitcast.25, f32[256,512]{1,0:T(8,128)S(1)} %local_part.2.refs_0_, ...), custom_call_target="tpu_custom_call" | custom-call | flops 3000000000 | bytes 1 | tf_op jit(solution)/shard_map/finish/pallas_call | solution.py:349
  50.3 0.6 %collective-permute-done.10.there_ref = bf16[40,1024]{1,0:T(8,128)(2,1)S(1)} collective-permute-done((bf16[40,1024]{1,0:T(8,128)(2,1)S(1)}, bf16[40,1024]{1,0:T(8,128)(2,1)S(1)}, u32[]{:S(2)}, u32[]{:S(2)}) %collective-permute-start.10) | collective-permute-done | bytes 81952 | tf_op jit(solution)/shard_map/ppermute | solution.py:710
  50.9 0.7 %results.1 = (f32[16,1024]{1,0:T(8,128)}, f32[16,1024]{1,0:T(8,128)}, f32[1,1024]{1,0:T(1,128)}) custom-call(bf16[40,1024]{1,0:T(8,128)(2,1)S(1)} %collective-permute-done.10.there_ref, f32[40,1024]{1,0:T(8,128)S(1)} %get-tuple-element.98.sums_ref, f32[16,1024]{1,0:T(8,128)S(1)} %bitcast.26), custom_call_target="tpu_custom_call" | custom-call | flops 1 | bytes 1 | tf_op jit(solution)/shard_map/results/pallas_call | solution.py:515
  (4 shorter events, 0.0 us)
Async XLA Ops:
  0.6 2.5 %copy-start = (bf16[256,2048]{1,0:T(8,128)(2,1)S(1)}, bf16[256,2048]{1,0:T(8,128)(2,1)}, u32[]{:S(2)}) copy-start(bf16[256,2048]{1,0:T(8,128)(2,1)} %up_ref.4) | copy-start | bytes 3145732
  0.6 4.3 %copy-start.1 = (f32[1024,16]{0,1:T(8,128)S(1)}, f32[1024,16]{0,1:T(8,128)}, u32[]{:S(2)}) copy-start(f32[1024,16]{0,1:T(8,128)} %param.10) | copy-start | bytes 196612
  0.7 4.3 %copy-start.3 = (bf16[256,1024]{1,0:T(8,128)(2,1)S(1)}, bf16[256,1024]{1,0:T(8,128)(2,1)}, u32[]{:S(2)}) copy-start(bf16[256,1024]{1,0:T(8,128)(2,1)} %sig_ref.1) | copy-start | bytes 1572868
  4.4 10.5 %collective-permute-start.1 = (bf16[256,1024]{1,0:T(8,128)(2,1)S(1)}, bf16[256,1024]{1,0:T(8,128)(2,1)S(1)}, u32[]{:S(2)}, u32[]{:S(2)}) collective-permute-start(bf16[256,1024]{1,0:T(8,128)(2,1)S(1)} %multiply.1), channel_id=1, source_target_pairs={{0,1},{1,0},{2,3},{3,2},{4,5},{5,4},{6,7},{7,6},{8,9},{9,8},{10,11... | collective-permute-start | bytes 1572872 | tf_op jit(solution)/shard_map/ppermute | solution.py:710
  11.9 13.8 %collective-permute-start.3 = (bf16[256,1024]{1,0:T(8,128)(2,1)S(1)}, bf16[256,1024]{1,0:T(8,128)(2,1)S(1)}, u32[]{:S(2)}, u32[]{:S(2)}) collective-permute-start(bf16[256,1024]{1,0:T(8,128)(2,1)S(1)} %get-tuple-element.71), channel_id=1, source_target_pairs={{0,1},{1,0},{2,3},{3,2},{4,5},{5,4},{6,7},{7,6},{8,9},{9,8},{10,11... | collective-permute-start | bytes 1572872 | tf_op jit(solution)/shard_map/ppermute | solution.py:710
  12.0 5.3 %collective-permute-start = (bf16[32,1024]{1,0:T(8,128)(2,1)S(1)}, bf16[32,1024]{1,0:T(8,128)(2,1)S(1)}, u32[]{:S(2)}, u32[]{:S(2)}) collective-permute-start(bf16[32,1024]{1,0:T(8,128)(2,1)S(1)} %get-tuple-element.55), channel_id=1, source_target_pairs={{0,4},{4,0},{8,12},{12,8},{16,20},{20,16},{24,28},{28,24},{1,5},{5... | collective-permute-start | bytes 196616 | tf_op jit(solution)/shard_map/ppermute | solution.py:710
  15.1 10.6 %collective-permute-start.4 = (bf16[256,512]{1,0:T(8,128)(2,1)S(1)}, bf16[256,512]{1,0:T(8,128)(2,1)S(1)}, u32[]{:S(2)}, u32[]{:S(2)}) collective-permute-start(bf16[256,512]{1,0:T(8,128)(2,1)S(1)} %get-tuple-element.60), channel_id=1, source_target_pairs={{0,2},{1,3},{2,0},{3,1},{4,6},{5,7},{6,4},{7,5},{8,10},{9,11},{10,... | collective-permute-start | bytes 786440 | tf_op jit(solution)/shard_map/ppermute | solution.py:710
  16.7 12.1 %collective-permute-start.5 = (bf16[256,512]{1,0:T(8,128)(2,1)S(1)}, bf16[256,512]{1,0:T(8,128)(2,1)S(1)}, u32[]{:S(2)}, u32[]{:S(2)}) collective-permute-start(bf16[256,512]{1,0:T(8,128)(2,1)S(1)} %get-tuple-element.61), channel_id=1, source_target_pairs={{0,2},{1,3},{2,0},{3,1},{4,6},{5,7},{6,4},{7,5},{8,10},{9,11},{10,... | collective-permute-start | bytes 786440 | tf_op jit(solution)/shard_map/ppermute | solution.py:710
  17.3 5.6 %collective-permute-start.2 = (bf16[32,1024]{1,0:T(8,128)(2,1)S(1)}, bf16[32,1024]{1,0:T(8,128)(2,1)S(1)}, u32[]{:S(2)}, u32[]{:S(2)}) collective-permute-start(bf16[32,1024]{1,0:T(8,128)(2,1)S(1)} %get-tuple-element.64), channel_id=1, source_target_pairs={{0,8},{4,12},{8,0},{12,4},{16,24},{20,28},{24,16},{28,20},{1,9},{5... | collective-permute-start | bytes 196616 | tf_op jit(solution)/shard_map/ppermute | solution.py:710
  22.9 12.7 %copy-start.2 = (f32[1024,16]{0,1:T(8,128)S(1)}, f32[1024,16]{0,1:T(8,128)}, u32[]{:S(2)}) copy-start(f32[1024,16]{0,1:T(8,128)} %param.9) | copy-start | bytes 196612
  22.9 12.7 %copy-start.4 = (f32[1024]{0:T(1024)S(1)}, f32[1024]{0:T(1024)}, u32[]{:S(2)}) copy-start(f32[1024]{0:T(1024)} %param.11) | copy-start | bytes 12292
  23.0 10.1 %collective-permute-start.7 = (bf16[32,1024]{1,0:T(8,128)(2,1)S(1)}, bf16[32,1024]{1,0:T(8,128)(2,1)S(1)}, u32[]{:S(2)}, u32[]{:S(2)}) collective-permute-start(bf16[32,1024]{1,0:T(8,128)(2,1)S(1)} %get-tuple-element.81), channel_id=1, source_target_pairs={{0,16},{4,20},{8,24},{12,28},{16,0},{20,4},{24,8},{28,12},{1,17},{... | collective-permute-start | bytes 196616 | tf_op jit(solution)/shard_map/ppermute | solution.py:710
  29.8 4.0 %collective-permute-start.6 = (bf16[16,1024]{1,0:T(8,128)(2,1)S(1)}, bf16[16,1024]{1,0:T(8,128)(2,1)S(1)}, u32[]{:S(2)}, u32[]{:S(2)}) collective-permute-start(bf16[16,1024]{1,0:T(8,128)(2,1)S(1)} %get-tuple-element.79), channel_id=1, source_target_pairs={{0,4},{4,0},{8,12},{12,8},{16,20},{20,16},{24,28},{28,24},{1,5},{5... | collective-permute-start | bytes 98312 | tf_op jit(solution)/shard_map/ppermute | solution.py:710
  33.9 4.9 %collective-permute-start.8 = (bf16[56,1024]{1,0:T(8,128)(2,1)S(1)}, bf16[56,1024]{1,0:T(8,128)(2,1)S(1)}, u32[]{:S(2)}, u32[]{:S(2)}) collective-permute-start(bf16[56,1024]{1,0:T(8,128)(2,1)S(1)} %get-tuple-element.88), channel_id=1, source_target_pairs={{0,8},{4,12},{8,0},{12,4},{16,24},{20,28},{24,16},{28,20},{1,9},{5... | collective-permute-start | bytes 344072 | tf_op jit(solution)/shard_map/ppermute | solution.py:710
  38.8 7.5 %collective-permute-start.9 = (bf16[56,1024]{1,0:T(8,128)(2,1)S(1)}, bf16[56,1024]{1,0:T(8,128)(2,1)S(1)}, u32[]{:S(2)}, u32[]{:S(2)}) collective-permute-start(bf16[56,1024]{1,0:T(8,128)(2,1)S(1)} %get-tuple-element.92), channel_id=1, source_target_pairs={{0,16},{4,20},{8,24},{12,28},{16,0},{20,4},{24,8},{28,12},{1,17},{... | collective-permute-start | bytes 344072 | tf_op jit(solution)/shard_map/ppermute | solution.py:710
  46.4 4.5 %collective-permute-start.10 = (bf16[40,1024]{1,0:T(8,128)(2,1)S(1)}, bf16[40,1024]{1,0:T(8,128)(2,1)S(1)}, u32[]{:S(2)}, u32[]{:S(2)}) collective-permute-start(bf16[40,1024]{1,0:T(8,128)(2,1)S(1)} %get-tuple-element.97), channel_id=1, source_target_pairs={{0,4},{4,0},{8,12},{12,8},{16,20},{20,16},{24,28},{28,24},{1,5},{5... | collective-permute-start | bytes 245768 | tf_op jit(solution)/shard_map/ppermute | solution.py:710

commit v6 on v5

--- a/solution.py
+++ b/solution.py
@@ -254,10 +254,11 @@
     return outs
 
 
-def local_kernel(length, base, grad_ref, z_ref, dec_ref, res_ref, gain_ref, loc_ref, cbuf, zbuf):
+def local_kernel(length, base, grad_ref, z_ref, dec_ref, res_ref, gain_ref, loc_ref, reach_ref, cbuf, zbuf):
     tokens, width = grad_ref.shape
     modes = dec_ref.shape[0]
     steps = tokens // SUB
+    ahead = (SUB - 1 - lax.broadcasted_iota(jnp.int32, (HALF, LANES), 0)).astype(F32) * steps
 
     @pl.loop(0, width // LANES)
     def _(block):
@@ -268,6 +269,13 @@
         weight = res_ref[:, lanes] * (1.0 / math.sqrt(length))
         gain = spread(gain_ref[:, lanes])
         zbuf[...] = z_ref[block]
+        lead = weight * pole_all
+        for n in range(modes):
+            for half in range(2):
+                left = ahead - half * HALF * steps
+                reach_ref[rows_of(n, half), here] = spread(lead[n : n + 1]) * jnp.exp(
+                    spread(-rate[n : n + 1]) * left
+                )
         sums = jnp.zeros((modes, LANES), F32)
         for j in reversed(range(SUB)):
             pick = pl.ds(j, modes, stride=SUB)
@@ -296,9 +304,12 @@
     modes = decays.shape[0]
     return pl.pallas_call(
         functools.partial(local_kernel, length, base),
-        out_shape=jax.ShapeDtypeStruct((tokens, width), F32),
+        out_shape=(
+            jax.ShapeDtypeStruct((tokens, width), F32),
+            jax.ShapeDtypeStruct((modes * SUB, width), F32),
+        ),
         in_specs=[VM] * 5,
-        out_specs=VM,
+        out_specs=(VM,) * 2,
         scratch_shapes=[pltpu.VMEM((modes * SUB, LANES), F32)] * 2,
         compiler_params=params(),
         cost_estimate=takes(1.5),
@@ -306,35 +317,29 @@
     )(grad, z, decays, residues, gain)
 
 
-def finish_kernel(length, hop, chunks, me_ref, there_ref, later_ref, dec_ref, res_ref, *refs):
-    locs = refs[: len(chunks)]
-    o_ref, vals, work = refs[len(chunks) :]
+def finish_kernel(length, hop, chunks, me_ref, there_ref, later_ref, dec_ref, *refs):
+    locs, reaches = refs[: len(chunks)], refs[len(chunks) : 2 * len(chunks)]
+    o_ref, vals, work = refs[2 * len(chunks) :]
     tokens = o_ref.shape[0]
     modes = dec_ref.shape[0]
     steps = tokens // SUB
-    scale = 1.0 / math.sqrt(length)
-    ahead = (SUB - 1 - lax.broadcasted_iota(jnp.int32, (HALF, LANES), 0)).astype(F32) * steps
     vals[...] = later_step(
         me_ref, there_ref.at[0:modes, :], later_ref[...], dec_ref, length, tokens, hop
     )
 
-    for loc_ref, (low, high) in zip(locs, chunks):
+    for loc_ref, reach_ref, (low, high) in zip(locs, reaches, chunks):
         @pl.loop(0, (high - low) // LANES)
         def _(block):
             here = lane_block(block)
             lanes = lane_block(block + low // LANES)
-            rate = dec_ref[:, lanes] * (-1.0 / length)
-            pole_all = jnp.exp(rate)
-            lead = scale * res_ref[:, lanes] * pole_all * vals[:, lanes]
+            pole_all = jnp.exp(dec_ref[:, lanes] * (-1.0 / length))
+            later = vals[:, lanes]
             for half in range(2):
                 outs = [loc_ref[rows_of(i, half), here] for i in range(steps)]
                 for first in range(0, modes, 8):
                     picked = range(first, first + 8)
                     poles = [spread(pole_all[n : n + 1]) for n in picked]
-                    starts = [
-                        spread(lead[n : n + 1]) * jnp.exp(spread(rate[n : n + 1]) * (ahead - half * HALF * steps))
-                        for n in picked
-                    ]
+                    starts = [spread(later[n : n + 1]) * reach_ref[rows_of(n, half), here] for n in picked]
                     outs = carry_out(outs, poles, starts)
                 for i in range(steps):
                     work[rows_of(i, half), lanes] = outs[i]
@@ -344,18 +349,18 @@
     ).astype(BF16)
 
 
-def finish(me, there, later, decays, residues, locs, chunks, tokens, length, hop):
+def finish(me, there, later, decays, locs, reaches, chunks, tokens, length, hop):
     modes, width = decays.shape
     return pl.pallas_call(
         functools.partial(finish_kernel, length, hop, chunks),
         out_shape=jax.ShapeDtypeStruct((tokens, width), BF16),
-        in_specs=[SM] + [VM] * (4 + len(locs)),
+        in_specs=[SM] + [VM] * (3 + 2 * len(locs)),
         out_specs=VM,
         scratch_shapes=[pltpu.VMEM((modes, width), F32), pltpu.VMEM((tokens, width), F32)],
         compiler_params=params(),
         cost_estimate=takes(3),
         name="finish",
-    )(me, there, later, decays, residues, *locs)
+    )(me, there, later, decays, *locs, *reaches)
 
 
 def place_bits(me_ref, hop):
@@ -769,7 +774,7 @@
         pays, arrived[k] = lax.optimization_barrier((pays, arrived[k]))
         take(arrived[k], *chunks[k], *tables[k])
     sent, state = join_states(states, chunks)
-    locs = [local_part(grad, z, dec, res, gain, length, low) for grad, z, low in locs]
+    locs, reaches = zip(*[local_part(grad, z, dec, res, gain, length, low) for grad, z, low in locs])
     there = send(sent, "ctx", groups, levels[0])
     sent, state, later, sums = merge(
         place, there, state, ends, pays, dec, before, chunks, tokens, length, levels[0], levels[-1]
@@ -782,7 +787,7 @@
             )
             state = state[0] if state else None
     moved, sums = sum_step(there, sums)
-    out = finish(place, there, later, dec, res, locs, chunks, tokens, length, levels[-1])
+    out = finish(place, there, later, dec, locs, reaches, chunks, tokens, length, levels[-1])
     ores, odec, oskip = results(send(moved, "ctx", groups, levels[0]), sums, res, length)
     return (out, ores.T, odec.T, oskip[0])
 

time: 51.7 us -> 51.7 us (level)
  no operation moved by 1% of the time
where the time goes in v6:
time: 51.7 us; the launch traced here: 51.5 us
  Pallas kernels  26.4 us (51%)
  starting transfers between devices  18.1 us (35%)
  waiting for transfers between devices  6.06 us (12%)
  between operations  0.79 us (2%)
    ppermute x11, starting transfers between devices, send(): return lax.ppermute(x, axis, [(i, i ^ hop) for i in range(size)])  18.1 us
    pallas_call x1, Pallas kernels, project_and_scan(): pl.pallas_call(functools.partial(scan_kernel, pieces, chunks, length), ou...  6.94 us
    ppermute x11, waiting for transfers between devices, send(): return lax.ppermute(x, axis, [(i, i ^ hop) for i in range(size)])  6.06 us
    pallas_call x2, Pallas kernels, filter_sums(): pl.pallas_call(functools.partial(filter_kernel, length, base), out_shape=...  3.68 us
    pallas_call x1, Pallas kernels, project_last(): pl.pallas_call(last_kernel, out_shape=jax.ShapeDtypeStruct((tokens, width...  3.48 us
    pallas_call x1, Pallas kernels, finish(): pl.pallas_call(functools.partial(finish_kernel, length, hop, chunks), out...  2.83 us
    pallas_call x2, Pallas kernels, local_part(): pl.pallas_call(functools.partial(local_kernel, length, base), out_shape=(...  2.7 us
    pallas_call x1, Pallas kernels, fetch(): pl.pallas_call(fetch_kernel, out_shape=jax.ShapeDtypeStruct((pieces * wid...  2.3 us
  transfers between devices with their start and end apart: 11, of which 6 were waited for; matrix products, arithmetic and copies ran while one was open for 0% of the time, Pallas kernels for 43%

profile of v6, /device:TPU:0, one launch (start us, length us, event | category | flops | bytes accessed | tf_op | source)
XLA Modules:
  0.0 51.5 jit_solution(15268933674873477567)
XLA Ops:
  0.6 0.0 copy-start
  0.6 0.0 copy-start.1
  0.7 0.0 copy-start.3
  0.7 0.1 pad_add_fusion.blocks_ref
  0.7 2.3 %fetch.1.held_ref = bf16[1024,2048]{1,0:T(8,128)(2,1)S(1)} custom-call(s32[1]{0:T(128)} %bitcast.blocks_ref, bf16[4096,2048]{1,0:T(8,128)(2,1)} %w_ref.5), custom_call_target="tpu_custom_call" | custom-call | flops 3000000000 | bytes 1 | tf_op jit(solution)/shard_map/fetch/pallas_call | solution.py:600
  3.0 0.1 copy-done
  3.1 1.3 %multiply.1 = bf16[256,1024]{1,0:T(8,128)(2,1)S(1)} custom-call(bf16[256,2048]{1,0:T(8,128)(2,1)S(1)} %copy-done, bf16[1024,2048]{1,0:T(8,128)(2,1)S(1)} %fetch.1.held_ref), custom_call_target="tpu_custom_call" | custom-call | flops 1000000000 | bytes 1 | tf_op jit(solution)/shard_map/multiply/pallas_call | solution.py:617
  4.4 0.5 %collective-permute-start.1 = (bf16[256,1024]{1,0:T(8,128)(2,1)S(1)}, bf16[256,1024]{1,0:T(8,128)(2,1)S(1)}, u32[]{:S(2)}, u32[]{:S(2)}) collective-permute-start(bf16[256,1024]{1,0:T(8,128)(2,1)S(1)} %multiply.1), channel_id=1, source_target_pairs={{0,1},{1,0},{2,3},{3,2},{4,5},{5,4},{6,7},{7,6},{8,9},{9,8},{10,11... | collective-permute-start | bytes 1572872 | tf_op jit(solution)/shard_map/ppermute | solution.py:715
  4.9 0.0 copy-done.1
  4.9 0.0 copy-done.3
  4.9 6.9 %project_and_scan.1 = (bf16[256,1024]{1,0:T(8,128)(2,1)S(1)}, bf16[256,1024]{1,0:T(8,128)(2,1)S(1)}, f32[32,1024]{1,0:T(8,128)S(1)}, bf16[32,1024]{1,0:T(8,128)(...) custom-call(s32[2]{0:T(128)S(1)} %pad_add_fusion.blocks_ref, ...), custom_call_target="tpu_custom_call" | custom-call | flops 6000000000 | bytes 1 | tf_op jit(solution)/shard_map/project_and_scan/pallas_call | solution.py:653
  11.9 0.1 collective-permute-start.3
  12.0 2.9 %collective-permute-start = (bf16[32,1024]{1,0:T(8,128)(2,1)S(1)}, bf16[32,1024]{1,0:T(8,128)(2,1)S(1)}, u32[]{:S(2)}, u32[]{:S(2)}) collective-permute-start(bf16[32,1024]{1,0:T(8,128)(2,1)S(1)} %get-tuple-element.59), channel_id=1, source_target_pairs={{0,4},{4,0},{8,12},{12,8},{16,20},{20,16},{24,28},{28,24},{1,5},{5... | collective-permute-start | bytes 196616 | tf_op jit(solution)/shard_map/ppermute | solution.py:715
  14.9 0.0 collective-permute-done.1.lent_ref
  14.9 0.1 pair_sums.1
  15.1 1.6 %collective-permute-start.4 = (bf16[256,512]{1,0:T(8,128)(2,1)S(1)}, bf16[256,512]{1,0:T(8,128)(2,1)S(1)}, u32[]{:S(2)}, u32[]{:S(2)}) collective-permute-start(bf16[256,512]{1,0:T(8,128)(2,1)S(1)} %get-tuple-element.64), channel_id=1, source_target_pairs={{0,2},{1,3},{2,0},{3,1},{4,6},{5,7},{6,4},{7,5},{8,10},{9,11},{10,... | collective-permute-start | bytes 786440 | tf_op jit(solution)/shard_map/ppermute | solution.py:715
  16.7 0.5 collective-permute-start.5
  17.2 0.1 collective-permute-done.there_ref
  17.3 0.1 prefix_step.2
  17.3 2.1 %collective-permute-start.2 = (bf16[32,1024]{1,0:T(8,128)(2,1)S(1)}, bf16[32,1024]{1,0:T(8,128)(2,1)S(1)}, u32[]{:S(2)}, u32[]{:S(2)}) collective-permute-start(bf16[32,1024]{1,0:T(8,128)(2,1)S(1)} %get-tuple-element.68), channel_id=1, source_target_pairs={{0,8},{4,12},{8,0},{12,4},{16,24},{20,28},{24,16},{28,20},{1,9},{5... | collective-permute-start | bytes 196616 | tf_op jit(solution)/shard_map/ppermute | solution.py:715
  19.4 3.5 %project_last.1.refs_0_ = bf16[256,1024]{1,0:T(8,128)(2,1)S(1)} custom-call(s32[1]{0:T(128)} %bitcast.3.block_ref, bf16[256,2048]{1,0:T(8,128)(2,1)S(1)} %copy-done, bf16[4096,2048]{1,0:T(8,128)(2,1)} %w_ref.5), custom_call_target="tpu_custom_call" | custom-call | flops 4000000000 | bytes 1 | tf_op jit(solution)/shard_map/project_last/pallas_call | solution.py:682
  22.9 0.0 copy-start.2
  22.9 0.0 copy-start.4
  22.9 0.0 collective-permute-done.2.there_ref
  22.9 0.1 prefix_step.3
  23.0 2.7 %collective-permute-start.7 = (bf16[32,1024]{1,0:T(8,128)(2,1)S(1)}, bf16[32,1024]{1,0:T(8,128)(2,1)S(1)}, u32[]{:S(2)}, u32[]{:S(2)}) collective-permute-start(bf16[32,1024]{1,0:T(8,128)(2,1)S(1)} %get-tuple-element.85), channel_id=1, source_target_pairs={{0,16},{4,20},{8,24},{12,28},{16,0},{20,4},{24,8},{28,12},{1,17},{... | collective-permute-start | bytes 196616 | tf_op jit(solution)/shard_map/ppermute | solution.py:715
  25.7 0.0 collective-permute-done.4.refs_2_
  25.7 0.0 collective-permute-done.3.refs_1_
  25.7 1.1 %gradient_states.2 = (f32[256,512]{1,0:T(8,128)S(1)}, f32[4,256,128]{2,1,0:T(8,128)S(1)}, f32[16,512]{1,0:T(8,128)S(1)}) custom-call(bf16[256,1024]{1,0:T(8,128)(2,1)S(1)} %project_last.1.refs_0_, bf16[256,1024]{1,0:T(8,128)(2,1)S(1)} %collective-permute-done.3.refs_1_, bf16[256,512]{1,0:T(8,128)(2,1)S(1)} %collective-permute-done.4.refs_2_, ...), custom_call_target="tpu_custom_call" | custom-call | flops 1000000000 | bytes 1 | tf_op jit(solution)/shard_map/gradient_states/pallas_call | solution.py:163
  26.8 1.8 %filter_sums.2.refs_0_ = f32[56,512]{1,0:T(8,128)S(1)} custom-call(f32[256,512]{1,0:T(8,128)S(1)} %get-tuple-element.77.grad_ref, bf16[256,512]{1,0:T(8,128)(2,1)S(1)} %get-tuple-element.78.sigp_ref, f32[16,1024]{1,0:T(8,128)S(1)} %bitcast.15, bf16[256,512]{1,0:T(8,128)(2,1)S(1)} %get-tuple-element.79.y_ref, bf16[256,512]{1,0:T(8,128)(2,1)S(1)} %get-tuple-element.80.y1_ref), custom_call_target="tpu_custom_call" | custom-call | flops 3000000000 | bytes 1 | tf_op jit(solution)/shard_map/filter_sums/pallas_call | solution.py:236
  28.6 0.1 collective-permute-done.5.refs_2_
  28.8 1.1 %gradient_states.3 = (f32[256,512]{1,0:T(8,128)S(1)}, f32[4,256,128]{2,1,0:T(8,128)S(1)}, f32[16,512]{1,0:T(8,128)S(1)}) custom-call(bf16[256,1024]{1,0:T(8,128)(2,1)S(1)} %project_last.1.refs_0_, bf16[256,1024]{1,0:T(8,128)(2,1)S(1)} %collective-permute-done.3.refs_1_, bf16[256,512]{1,0:T(8,128)(2,1)S(1)} %collective-permute-done.5.refs_2_, ...), custom_call_target="tpu_custom_call" | custom-call | flops 1000000000 | bytes 1 | tf_op jit(solution)/shard_map/gradient_states/pallas_call | solution.py:163
  29.8 1.4 %collective-permute-start.6 = (bf16[16,1024]{1,0:T(8,128)(2,1)S(1)}, bf16[16,1024]{1,0:T(8,128)(2,1)S(1)}, u32[]{:S(2)}, u32[]{:S(2)}) collective-permute-start(bf16[16,1024]{1,0:T(8,128)(2,1)S(1)} %get-tuple-element.83), channel_id=1, source_target_pairs={{0,4},{4,0},{8,12},{12,8},{16,20},{20,16},{24,28},{28,24},{1,5},{5... | collective-permute-start | bytes 98312 | tf_op jit(solution)/shard_map/ppermute | solution.py:715
  31.3 1.8 %filter_sums.3.refs_1_ = f32[56,512]{1,0:T(8,128)S(1)} custom-call(f32[256,512]{1,0:T(8,128)S(1)} %get-tuple-element.87.grad_ref, bf16[256,512]{1,0:T(8,128)(2,1)S(1)} %get-tuple-element.88.sigp_ref, f32[16,1024]{1,0:T(8,128)S(1)} %bitcast.17, bf16[256,512]{1,0:T(8,128)(2,1)S(1)} %get-tuple-element.89.y_ref, bf16[256,512]{1,0:T(8,128)(2,1)S(1)} %get-tuple-element.90.y1_ref), custom_call_target="tpu_custom_call" | custom-call | flops 3000000000 | bytes 1 | tf_op jit(solution)/shard_map/filter_sums/pallas_call | solution.py:236
  33.1 0.0 collective-permute-done.7.ends_ref
  33.1 0.7 %collective-permute-done.6.there_ref = bf16[16,1024]{1,0:T(8,128)(2,1)S(1)} collective-permute-done((bf16[16,1024]{1,0:T(8,128)(2,1)S(1)}, bf16[16,1024]{1,0:T(8,128)(2,1)S(1)}, u32[]{:S(2)}, u32[]{:S(2)}) %collective-permute-start.6) | collective-permute-done | bytes 32800 | tf_op jit(solution)/shard_map/ppermute | solution.py:715
  33.8 0.1 merge.1
  33.9 1.6 %collective-permute-start.8 = (bf16[56,1024]{1,0:T(8,128)(2,1)S(1)}, bf16[56,1024]{1,0:T(8,128)(2,1)S(1)}, u32[]{:S(2)}, u32[]{:S(2)}) collective-permute-start(bf16[56,1024]{1,0:T(8,128)(2,1)S(1)} %get-tuple-element.92), channel_id=1, source_target_pairs={{0,8},{4,12},{8,0},{12,4},{16,24},{20,28},{24,16},{28,20},{1,9},{5... | collective-permute-start | bytes 344072 | tf_op jit(solution)/shard_map/ppermute | solution.py:715
  35.6 1.3 %local_part.3 = (f32[256,512]{1,0:T(8,128)S(1)}, f32[256,512]{1,0:T(8,128)S(1)}) custom-call(f32[256,512]{1,0:T(8,128)S(1)} %get-tuple-element.87.grad_ref, f32[4,256,128]{2,1,0:T(8,128)S(1)} %get-tuple-element.100.z_ref, f32[16,1024]{1,0:T(8,128)S(1)} %bitcast.19, f32[16,1024]{1,0:T(8,128)S(1)} %bitcast.23, f32[1,1024]{1,0:T(1,128)S(1)} %bitcast.26), custom_call_target="tpu_custom_call" | custom-call | flops 1500000000 | bytes 1 | tf_op jit(solution)/shard_map/local_part/pallas_call | solution.py:305
  36.9 1.8 %collective-permute-done.8.there_ref = bf16[56,1024]{1,0:T(8,128)(2,1)S(1)} collective-permute-done((bf16[56,1024]{1,0:T(8,128)(2,1)S(1)}, bf16[56,1024]{1,0:T(8,128)(2,1)S(1)}, u32[]{:S(2)}, u32[]{:S(2)}) %collective-permute-start.8) | collective-permute-done | bytes 114720 | tf_op jit(solution)/shard_map/ppermute | solution.py:715
  38.8 0.1 tail_step.1
  38.8 3.5 %collective-permute-start.9 = (bf16[56,1024]{1,0:T(8,128)(2,1)S(1)}, bf16[56,1024]{1,0:T(8,128)(2,1)S(1)}, u32[]{:S(2)}, u32[]{:S(2)}) collective-permute-start(bf16[56,1024]{1,0:T(8,128)(2,1)S(1)} %get-tuple-element.96), channel_id=1, source_target_pairs={{0,16},{4,20},{8,24},{12,28},{16,0},{20,4},{24,8},{28,12},{1,17},{... | collective-permute-start | bytes 344072 | tf_op jit(solution)/shard_map/ppermute | solution.py:715
  42.3 1.3 %local_part.2 = (f32[256,512]{1,0:T(8,128)S(1)}, f32[256,512]{1,0:T(8,128)S(1)}) custom-call(f32[256,512]{1,0:T(8,128)S(1)} %get-tuple-element.77.grad_ref, f32[4,256,128]{2,1,0:T(8,128)S(1)} %get-tuple-element.98.z_ref, f32[16,1024]{1,0:T(8,128)S(1)} %bitcast.21, f32[16,1024]{1,0:T(8,128)S(1)} %bitcast.24, f32[1,1024]{1,0:T(1,128)S(1)} %bitcast.27), custom_call_target="tpu_custom_call" | custom-call | flops 1500000000 | bytes 1 | tf_op jit(solution)/shard_map/local_part/pallas_call | solution.py:305
  43.7 2.6 %collective-permute-done.9.there_ref = bf16[56,1024]{1,0:T(8,128)(2,1)S(1)} collective-permute-done((bf16[56,1024]{1,0:T(8,128)(2,1)S(1)}, bf16[56,1024]{1,0:T(8,128)(2,1)S(1)}, u32[]{:S(2)}, u32[]{:S(2)}) %collective-permute-start.9) | collective-permute-done | bytes 114720 | tf_op jit(solution)/shard_map/ppermute | solution.py:715
  46.4 1.1 %collective-permute-start.10 = (bf16[40,1024]{1,0:T(8,128)(2,1)S(1)}, bf16[40,1024]{1,0:T(8,128)(2,1)S(1)}, u32[]{:S(2)}, u32[]{:S(2)}) collective-permute-start(bf16[40,1024]{1,0:T(8,128)(2,1)S(1)} %get-tuple-element.105), channel_id=1, source_target_pairs={{0,4},{4,0},{8,12},{12,8},{16,20},{20,16},{24,28},{28,24},{1,5},{5... | collective-permute-start | bytes 245768 | tf_op jit(solution)/shard_map/ppermute | solution.py:715
  47.5 2.8 %finish.1 = bf16[256,1024]{1,0:T(8,128)(2,1)} custom-call(s32[1]{0:T(128)} %bitcast.4.me_ref, bf16[56,1024]{1,0:T(8,128)(2,1)S(1)} %collective-permute-done.9.there_ref, f32[16,1024]{1,0:T(8,128)S(1)} %get-tuple-element.97.later_ref, f32[16,1024]{1,0:T(8,128)S(1)} %bitcast.22, f32[256,512]{1,0:T(8,128)S(1)} %get-tuple-element.99.refs_0_, ...), custom_call_target="tpu_custom_call" | custom-call | flops 3000000000 | bytes 1 | tf_op jit(solution)/shard_map/finish/pallas_call | solution.py:354
  50.3 0.6 %collective-permute-done.10.there_ref = bf16[40,1024]{1,0:T(8,128)(2,1)S(1)} collective-permute-done((bf16[40,1024]{1,0:T(8,128)(2,1)S(1)}, bf16[40,1024]{1,0:T(8,128)(2,1)S(1)}, u32[]{:S(2)}, u32[]{:S(2)}) %collective-permute-start.10) | collective-permute-done | bytes 81952 | tf_op jit(solution)/shard_map/ppermute | solution.py:715
  50.9 0.7 %results.1 = (f32[16,1024]{1,0:T(8,128)}, f32[16,1024]{1,0:T(8,128)}, f32[1,1024]{1,0:T(1,128)}) custom-call(bf16[40,1024]{1,0:T(8,128)(2,1)S(1)} %collective-permute-done.10.there_ref, f32[40,1024]{1,0:T(8,128)S(1)} %get-tuple-element.106.sums_ref, f32[16,1024]{1,0:T(8,128)S(1)} %bitcast.25), custom_call_target="tpu_custom_call" | custom-call | flops 1 | bytes 1 | tf_op jit(solution)/shard_map/results/pallas_call | solution.py:520
  (4 shorter events, 0.0 us)
Async XLA Ops:
  0.6 2.5 %copy-start = (bf16[256,2048]{1,0:T(8,128)(2,1)S(1)}, bf16[256,2048]{1,0:T(8,128)(2,1)}, u32[]{:S(2)}) copy-start(bf16[256,2048]{1,0:T(8,128)(2,1)} %up_ref.4) | copy-start | bytes 3145732
  0.6 4.3 %copy-start.1 = (f32[1024,16]{0,1:T(8,128)S(1)}, f32[1024,16]{0,1:T(8,128)}, u32[]{:S(2)}) copy-start(f32[1024,16]{0,1:T(8,128)} %param.10) | copy-start | bytes 196612
  0.7 4.3 %copy-start.3 = (bf16[256,1024]{1,0:T(8,128)(2,1)S(1)}, bf16[256,1024]{1,0:T(8,128)(2,1)}, u32[]{:S(2)}) copy-start(bf16[256,1024]{1,0:T(8,128)(2,1)} %sig_ref.1) | copy-start | bytes 1572868
  4.4 10.5 %collective-permute-start.1 = (bf16[256,1024]{1,0:T(8,128)(2,1)S(1)}, bf16[256,1024]{1,0:T(8,128)(2,1)S(1)}, u32[]{:S(2)}, u32[]{:S(2)}) collective-permute-start(bf16[256,1024]{1,0:T(8,128)(2,1)S(1)} %multiply.1), channel_id=1, source_target_pairs={{0,1},{1,0},{2,3},{3,2},{4,5},{5,4},{6,7},{7,6},{8,9},{9,8},{10,11... | collective-permute-start | bytes 1572872 | tf_op jit(solution)/shard_map/ppermute | solution.py:715
  11.9 13.8 %collective-permute-start.3 = (bf16[256,1024]{1,0:T(8,128)(2,1)S(1)}, bf16[256,1024]{1,0:T(8,128)(2,1)S(1)}, u32[]{:S(2)}, u32[]{:S(2)}) collective-permute-start(bf16[256,1024]{1,0:T(8,128)(2,1)S(1)} %get-tuple-element.75), channel_id=1, source_target_pairs={{0,1},{1,0},{2,3},{3,2},{4,5},{5,4},{6,7},{7,6},{8,9},{9,8},{10,11... | collective-permute-start | bytes 1572872 | tf_op jit(solution)/shard_map/ppermute | solution.py:715
  12.0 5.3 %collective-permute-start = (bf16[32,1024]{1,0:T(8,128)(2,1)S(1)}, bf16[32,1024]{1,0:T(8,128)(2,1)S(1)}, u32[]{:S(2)}, u32[]{:S(2)}) collective-permute-start(bf16[32,1024]{1,0:T(8,128)(2,1)S(1)} %get-tuple-element.59), channel_id=1, source_target_pairs={{0,4},{4,0},{8,12},{12,8},{16,20},{20,16},{24,28},{28,24},{1,5},{5... | collective-permute-start | bytes 196616 | tf_op jit(solution)/shard_map/ppermute | solution.py:715
  15.1 10.6 %collective-permute-start.4 = (bf16[256,512]{1,0:T(8,128)(2,1)S(1)}, bf16[256,512]{1,0:T(8,128)(2,1)S(1)}, u32[]{:S(2)}, u32[]{:S(2)}) collective-permute-start(bf16[256,512]{1,0:T(8,128)(2,1)S(1)} %get-tuple-element.64), channel_id=1, source_target_pairs={{0,2},{1,3},{2,0},{3,1},{4,6},{5,7},{6,4},{7,5},{8,10},{9,11},{10,... | collective-permute-start | bytes 786440 | tf_op jit(solution)/shard_map/ppermute | solution.py:715
  16.7 12.1 %collective-permute-start.5 = (bf16[256,512]{1,0:T(8,128)(2,1)S(1)}, bf16[256,512]{1,0:T(8,128)(2,1)S(1)}, u32[]{:S(2)}, u32[]{:S(2)}) collective-permute-start(bf16[256,512]{1,0:T(8,128)(2,1)S(1)} %get-tuple-element.65), channel_id=1, source_target_pairs={{0,2},{1,3},{2,0},{3,1},{4,6},{5,7},{6,4},{7,5},{8,10},{9,11},{10,... | collective-permute-start | bytes 786440 | tf_op jit(solution)/shard_map/ppermute | solution.py:715
  17.3 5.6 %collective-permute-start.2 = (bf16[32,1024]{1,0:T(8,128)(2,1)S(1)}, bf16[32,1024]{1,0:T(8,128)(2,1)S(1)}, u32[]{:S(2)}, u32[]{:S(2)}) collective-permute-start(bf16[32,1024]{1,0:T(8,128)(2,1)S(1)} %get-tuple-element.68), channel_id=1, source_target_pairs={{0,8},{4,12},{8,0},{12,4},{16,24},{20,28},{24,16},{28,20},{1,9},{5... | collective-permute-start | bytes 196616 | tf_op jit(solution)/shard_map/ppermute | solution.py:715
  22.9 12.7 %copy-start.2 = (f32[1024,16]{0,1:T(8,128)S(1)}, f32[1024,16]{0,1:T(8,128)}, u32[]{:S(2)}) copy-start(f32[1024,16]{0,1:T(8,128)} %param.9) | copy-start | bytes 196612
  22.9 12.7 %copy-start.4 = (f32[1024]{0:T(1024)S(1)}, f32[1024]{0:T(1024)}, u32[]{:S(2)}) copy-start(f32[1024]{0:T(1024)} %param.11) | copy-start | bytes 12292
  23.0 10.1 %collective-permute-start.7 = (bf16[32,1024]{1,0:T(8,128)(2,1)S(1)}, bf16[32,1024]{1,0:T(8,128)(2,1)S(1)}, u32[]{:S(2)}, u32[]{:S(2)}) collective-permute-start(bf16[32,1024]{1,0:T(8,128)(2,1)S(1)} %get-tuple-element.85), channel_id=1, source_target_pairs={{0,16},{4,20},{8,24},{12,28},{16,0},{20,4},{24,8},{28,12},{1,17},{... | collective-permute-start | bytes 196616 | tf_op jit(solution)/shard_map/ppermute | solution.py:715
  29.8 4.0 %collective-permute-start.6 = (bf16[16,1024]{1,0:T(8,128)(2,1)S(1)}, bf16[16,1024]{1,0:T(8,128)(2,1)S(1)}, u32[]{:S(2)}, u32[]{:S(2)}) collective-permute-start(bf16[16,1024]{1,0:T(8,128)(2,1)S(1)} %get-tuple-element.83), channel_id=1, source_target_pairs={{0,4},{4,0},{8,12},{12,8},{16,20},{20,16},{24,28},{28,24},{1,5},{5... | collective-permute-start | bytes 98312 | tf_op jit(solution)/shard_map/ppermute | solution.py:715
  33.9 4.9 %collective-permute-start.8 = (bf16[56,1024]{1,0:T(8,128)(2,1)S(1)}, bf16[56,1024]{1,0:T(8,128)(2,1)S(1)}, u32[]{:S(2)}, u32[]{:S(2)}) collective-permute-start(bf16[56,1024]{1,0:T(8,128)(2,1)S(1)} %get-tuple-element.92), channel_id=1, source_target_pairs={{0,8},{4,12},{8,0},{12,4},{16,24},{20,28},{24,16},{28,20},{1,9},{5... | collective-permute-start | bytes 344072 | tf_op jit(solution)/shard_map/ppermute | solution.py:715
  38.8 7.5 %collective-permute-start.9 = (bf16[56,1024]{1,0:T(8,128)(2,1)S(1)}, bf16[56,1024]{1,0:T(8,128)(2,1)S(1)}, u32[]{:S(2)}, u32[]{:S(2)}) collective-permute-start(bf16[56,1024]{1,0:T(8,128)(2,1)S(1)} %get-tuple-element.96), channel_id=1, source_target_pairs={{0,16},{4,20},{8,24},{12,28},{16,0},{20,4},{24,8},{28,12},{1,17},{... | collective-permute-start | bytes 344072 | tf_op jit(solution)/shard_map/ppermute | solution.py:715
  46.4 4.5 %collective-permute-start.10 = (bf16[40,1024]{1,0:T(8,128)(2,1)S(1)}, bf16[40,1024]{1,0:T(8,128)(2,1)S(1)}, u32[]{:S(2)}, u32[]{:S(2)}) collective-permute-start(bf16[40,1024]{1,0:T(8,128)(2,1)S(1)} %get-tuple-element.105), channel_id=1, source_target_pairs={{0,4},{4,0},{8,12},{12,8},{16,20},{20,16},{24,28},{28,24},{1,5},{5... | collective-permute-start | bytes 245768 | tf_op jit(solution)/shard_map/ppermute | solution.py:715
